TPU v7x, 32 devices: a whole 2x2x4 slice. The times are simulated.
32 devices in a mesh: section: 4 (over x, core), tp: 8 (over z, y).
Axes of the slice: x: 2, y: 2, z: 4, core: 2. Of those that a mesh axis runs over, the one named last changes fastest.
Arguments:
- grad_attn: bfloat16 [4, 8, 128, 128], P('section', 'tp'), may hold values from -6 to 6
- w_value: bfloat16 [4, 12288, 1024], P('section', 'tp'), may hold values from -0.0546875 to 0.0546875
- probs_own: bfloat16 [4, 8, 128, 128], P('section', 'tp'), may hold values from 0.0009994507 to 0.25
- probs_spare: bfloat16 [4, 8, 128, 128], P('section', 'tp'), may hold values from 0.0009994507 to 0.25
- evicted: int32 [4, 4], P('section'), may hold values from 0 to 1, as said below
- layer_input: bfloat16 [4, 128, 12288], P('section', None, 'tp'), may hold values from -6 to 6
- gain: float32 [4, 12288], P('section', 'tp'), may hold values from 0.1 to 1.9
Outputs:
- handed: bfloat16 [4, 128, 12288], P('section', None, 'tp')
Inputs may be any that keep to these rules, and one draw needn't show every extreme that they name: Section 0 has every tile evicted.
All inputs are finite; a program needn't handle non-finite values.
Results may differ from a plain program's by a relative error of at most 0.0049.
Values may be sent and summed in bfloat16 or wider, within the bound.
No kernel may reach another device: no remote copies, remote signals or barrier semaphores. Data moves between devices by JAX's collectives and lax.ppermute only.
A program may use at most 64 MiB of HBM per device.

v0:
```python
import functools

import jax
import jax.numpy as jnp
from jax import lax
from jax.experimental import pallas as pl
from jax.experimental.pallas import tpu as pltpu
from jax.sharding import PartitionSpec as P

D = 12288
LANES = 128
PIECES = (0, 3, 5, 7, 8)
EXTRA = 16
HIDES = pl.CostEstimate(flops=1 << 35, bytes_accessed=1 << 25, transcendentals=0)


def passed_along(block, axis, distance):
    devices = range(lax.axis_size(axis))
    route = [((i - distance) % len(devices), i) for i in devices]
    return lax.ppermute(block, axis, route)


def swapped(block, axis, mask):
    return lax.ppermute(block, axis, [(i ^ mask, i) for i in range(lax.axis_size(axis))])


def in_vmem(array):
    return pltpu.with_memory_space_constraint(array, pltpu.VMEM)


def in_hbm(array):
    return pltpu.with_memory_space_constraint(array, pltpu.HBM)


def vmem_specs(count):
    return [pl.BlockSpec(memory_space=pltpu.VMEM)] * count


def as_row(column):
    return jnp.broadcast_to(column, (column.shape[0], column.shape[0])).T[:1]


def standing(rows):
    tokens = rows.shape[1]
    return jnp.concatenate([rows, jnp.zeros((tokens - rows.shape[0], tokens), rows.dtype)]).T


def split(values):
    parts = []
    for _ in range(3):
        parts.append(values.astype(jnp.bfloat16).astype(jnp.float32))
        values = values - parts[-1]
    return parts


def own_ratio(squares, inner):
    return inner / jnp.maximum(squares, 1e-30)


def as_parts(row):
    rest = jnp.zeros((EXTRA - 3, row.shape[1]), jnp.float32)
    return jnp.concatenate(split(row) + [rest]).astype(jnp.bfloat16)


def pack_kernel(own_ref, grad_ref, spare_ref, evicted_ref, *refs):
    out_ref, spare_out, taken_ref, flags, sems = refs
    copies = [
        pltpu.make_async_copy(evicted_ref, flags, sems.at[0]),
        pltpu.make_async_copy(own_ref, out_ref.at[0], sems.at[1]),
        pltpu.make_async_copy(grad_ref, out_ref.at[1], sems.at[2]),
        pltpu.make_async_copy(spare_ref, spare_out, sems.at[3]),
    ]
    for copy in copies:
        copy.start()
    copies[0].wait()
    tiles = evicted_ref.shape[1]
    rows = taken_ref.shape[0] // tiles
    for tile in range(tiles):
        part = pl.ds(tile * rows, rows)
        taken = jnp.full((rows, taken_ref.shape[1]), flags[0, tile], jnp.int32)
        taken_ref[part, :] = taken.astype(jnp.float32).astype(taken_ref.dtype)
    for copy in copies[1:]:
        copy.wait()


def pack(own, grad, spare, evicted):
    return pl.pallas_call(
        pack_kernel,
        out_shape=(
            pltpu.VMEM((2, *own.shape), own.dtype),
            pltpu.VMEM(spare.shape, spare.dtype),
            pltpu.VMEM(own.shape, own.dtype),
        ),
        in_specs=[pl.BlockSpec(memory_space=pltpu.HBM)] * 4,
        out_specs=tuple(vmem_specs(3)),
        scratch_shapes=[
            pltpu.SMEM(evicted.shape, evicted.dtype),
            pltpu.SemaphoreType.DMA((4,)),
        ],
        cost_estimate=HIDES,
        compiler_params=pltpu.CompilerParams(vmem_limit_bytes=4 << 20),
    )(*map(in_hbm, (own, grad, spare, evicted)))


def reach_kernel(weight_ref, input_ref, gain_ref, first_ref, reach_ref, own_ref):
    del first_ref
    tokens, features = input_ref.shape
    values = input_ref[...].astype(jnp.float32)
    reach_ref[tokens:, :] = jnp.zeros_like(reach_ref[tokens:, :])
    squares = as_row(jnp.sum(values * values, axis=1, keepdims=True))
    reach_ref[tokens:, :tokens] = as_parts(squares)
    gained = (values * gain_ref[...]).astype(jnp.bfloat16)
    reach = jnp.dot(gained, weight_ref[...], preferred_element_type=jnp.float32)
    reach_ref[:tokens, :] = reach.astype(reach_ref.dtype)
    own_ref[:tokens, :] = reach
    own_ref[tokens:, :] = reach_ref[tokens:, :].astype(own_ref.dtype)


def reach_of(weights, inputs, gain, first):
    return pl.pallas_call(
        reach_kernel,
        out_shape=tuple(
            pltpu.VMEM((inputs.shape[0] + EXTRA, weights.shape[1]), dtype)
            for dtype in (jnp.bfloat16, jnp.float32)
        ),
        in_specs=vmem_specs(4),
        out_specs=tuple(vmem_specs(2)),
        cost_estimate=HIDES,
        compiler_params=pltpu.CompilerParams(vmem_limit_bytes=8 << 20),
    )(*map(in_vmem, (weights, inputs, gain, first)))


def mix_kernel(taken_ref, *refs):
    out_ref = refs[-1]
    taken = taken_ref[...]
    for j in range(out_ref.shape[0]):
        packed_ref, spare_ref = refs[len(refs) - 2 - j], refs[j]
        out_ref[j] = lax.dot_general(
            packed_ref[0] * (1 - taken) + spare_ref[...] * taken,
            packed_ref[1],
            (((0,), (0,)), ((), ())),
            preferred_element_type=jnp.float32,
        ).astype(out_ref.dtype)


def value_gradients(taken, heads):
    return pl.pallas_call(
        mix_kernel,
        out_shape=pltpu.VMEM((len(heads), *heads[0][1].shape), jnp.bfloat16),
        in_specs=vmem_specs(1 + 2 * len(heads)),
        out_specs=pl.BlockSpec(memory_space=pltpu.VMEM),
        cost_estimate=HIDES,
        compiler_params=pltpu.CompilerParams(vmem_limit_bytes=4 << 20),
    )(*map(in_vmem, (taken, *[spare for _, spare in heads], *[packed for packed, _ in heads[::-1]])))


def column_tile(features):
    return 256 if features % 256 == 0 else features


def fill(flat, blocks, head_of, first):
    groups = []
    for ref in blocks:
        count = ref.shape[0]
        for j in range(count):
            start = pl.multiple_of(head_of(first + j) * LANES, LANES)
            flat[:, pl.ds(start, LANES)] = ref[j]
        width = count * LANES
        groups.append((pl.multiple_of(head_of(first) // count * width, width), width))
        first += count
    return groups


def times_weights(flat, groups, weight_ref, part):
    products = [
        lax.dot_general(
            flat[:, pl.ds(start, width)],
            weight_ref[part, pl.ds(start, width)],
            (((1,), (1,)), ((), ())),
            preferred_element_type=jnp.float32,
        )
        for start, width in groups
    ]
    return sum(products[1:], products[0])


def early_kernel(head_of, *refs):
    *blocks, weight_ref, out_ref, flat = refs
    groups = fill(flat, blocks, head_of, 0)
    features = weight_ref.shape[0]
    tile = column_tile(features)
    for start in range(0, features, tile):
        part = pl.ds(start, tile)
        out_ref[:, part] = times_weights(flat, groups, weight_ref, part)


def project_early(head_of, blocks, weights):
    tokens = blocks[0].shape[1]
    return pl.pallas_call(
        functools.partial(early_kernel, head_of),
        out_shape=pltpu.VMEM((tokens, weights.shape[0]), jnp.float32),
        in_specs=vmem_specs(len(blocks) + 1),
        out_specs=pl.BlockSpec(memory_space=pltpu.VMEM),
        scratch_shapes=[pltpu.VMEM((tokens, weights.shape[1]), jnp.bfloat16)],
        cost_estimate=pl.CostEstimate(flops=1 << 16, bytes_accessed=1 << 12, transcendentals=0),
        compiler_params=pltpu.CompilerParams(vmem_limit_bytes=16 << 20),
    )(*map(in_vmem, (*blocks, weights)))


def inner_part(head_of, blocks, first, reach_ref):
    total = None
    for ref in blocks:
        for j in range(ref.shape[0]):
            start = pl.multiple_of(head_of(first) * LANES, LANES)
            part = ref[j].astype(jnp.float32) * reach_ref[:, pl.ds(start, LANES)]
            total = part if total is None else total + part
            first += 1
    return total


def join_kernel(head_of, sizes, *refs):
    blocks, reach_refs = refs[: sizes[0]], refs[sizes[0] : sizes[0] + sizes[1]]
    reach_ref, folded_ref, squares_ref = refs[sizes[0] + sizes[1] :]
    tokens = reach_ref.shape[0]
    reach_ref[...] = sum(ref[:tokens, :].astype(jnp.float32) for ref in reach_refs)
    squares = sum(ref[tokens:, :tokens].astype(jnp.float32) for ref in reach_refs)
    squares_ref[...] = jnp.sum(squares, axis=0, keepdims=True)
    if blocks:
        folded_ref[...] = inner_part(head_of, blocks, 0, reach_ref)
    else:
        folded_ref[...] = jnp.zeros_like(folded_ref)


def join(head_of, blocks, reaches):
    tokens, columns = reaches[0].shape[0] - EXTRA, reaches[0].shape[1]
    operands = (*blocks, *reaches)
    return pl.pallas_call(
        functools.partial(join_kernel, head_of, (len(blocks), len(reaches))),
        out_shape=(
            pltpu.VMEM((tokens, columns), jnp.float32),
            pltpu.VMEM((tokens, LANES), jnp.float32),
            pltpu.VMEM((1, tokens), jnp.float32),
        ),
        in_specs=vmem_specs(len(operands)),
        out_specs=tuple(vmem_specs(3)),
        cost_estimate=pl.CostEstimate(flops=1 << 16, bytes_accessed=1 << 12, transcendentals=0),
        compiler_params=pltpu.CompilerParams(vmem_limit_bytes=8 << 20),
    )(*map(in_vmem, operands))


def project_kernel(head_of, first, count, *refs):
    blocks, rest = refs[:count], refs[count:]
    reach_ref, folded_ref, squares_ref, weight_ref, input_ref, gain_ref, *rest = rest
    *early_refs, scaled_ref, sums_ref, flat = rest
    tokens, features = input_ref.shape
    groups = fill(flat, blocks, head_of, first)
    squares = squares_ref[...]
    folded = folded_ref[...] + inner_part(head_of, blocks, first, reach_ref)
    inner = as_row(jnp.sum(folded, axis=1, keepdims=True))
    sums_ref[:1, :] = squares
    sums_ref[1:, :] = inner
    rho = own_ratio(squares, inner)
    rows = [*split(squares), *split(inner), rho, jnp.zeros((1, tokens), jnp.float32)]
    columns = standing(jnp.concatenate(rows))
    scaled_ref[:, features:] = columns.astype(scaled_ref.dtype)
    rho = columns[:, 6:7]
    tile = column_tile(features)
    for start in range(0, features, tile):
        part = pl.ds(start, tile)
        grad_normed = times_weights(flat, groups, weight_ref, part)
        for ref in early_refs:
            grad_normed = grad_normed + ref[:, part]
        values = input_ref[:, part].astype(jnp.float32)
        scaled_ref[:, part] = (grad_normed * gain_ref[:, part] - values * rho).astype(
            scaled_ref.dtype
        )


def project(head_of, first, blocks, joined, weights, inputs, gain, early):
    tokens, features = inputs.shape
    operands = (*blocks, *joined, weights, inputs, gain, *early)
    return pl.pallas_call(
        functools.partial(project_kernel, head_of, first, len(blocks)),
        out_shape=(
            pltpu.VMEM((tokens, features + LANES), jnp.bfloat16),
            pltpu.VMEM((2, tokens), jnp.float32),
        ),
        in_specs=vmem_specs(len(operands)),
        out_specs=tuple(vmem_specs(2)),
        scratch_shapes=[pltpu.VMEM((tokens, weights.shape[1]), jnp.bfloat16)],
        cost_estimate=HIDES,
        compiler_params=pltpu.CompilerParams(vmem_limit_bytes=16 << 20),
    )(*map(in_vmem, operands))


def finish_kernel(scaled_ref, input_ref, *refs):
    *sums_refs, out_ref, held, sems = refs
    tokens, features = input_ref.shape
    extra = scaled_ref[:, features:].astype(jnp.float32).T
    squares = extra[0:1] + extra[1:2] + extra[2:3]
    inner = extra[3:4] + extra[4:5] + extra[5:6]
    rho = own_ratio(squares, inner)
    for ref in sums_refs:
        squares = squares + ref[:1, :]
        inner = inner + ref[1:, :]
    inv = 1.0 / jnp.sqrt(squares / D + 1e-05)
    factor = inner * (inv * inv * inv) / D - inv * rho
    rows = jnp.concatenate([inv, factor, jnp.zeros((6, tokens), jnp.float32)])
    columns = standing(rows)
    inv, factor = columns[:, 0:1], columns[:, 1:2]
    copies = []
    for j in range(len(PIECES) - 1):
        part = slice(PIECES[j] * tokens // 8, PIECES[j + 1] * tokens // 8)
        scaled = scaled_ref[part, :features].astype(jnp.float32)
        values = input_ref[part, :].astype(jnp.float32)
        held[part, :] = (scaled * inv[part] - values * factor[part]).astype(held.dtype)
        copies.append(pltpu.make_async_copy(held.at[part], out_ref.at[part], sems.at[j]))
        copies[-1].start()
    for copy in copies:
        copy.wait()


def finish(scaled, inputs, sums):
    return pl.pallas_call(
        finish_kernel,
        out_shape=pltpu.HBM(inputs.shape, jnp.bfloat16),
        in_specs=vmem_specs(2 + len(sums)),
        out_specs=pl.BlockSpec(memory_space=pltpu.HBM),
        scratch_shapes=[
            pltpu.VMEM(inputs.shape, jnp.bfloat16),
            pltpu.SemaphoreType.DMA((len(PIECES) - 1,)),
        ],
        compiler_params=pltpu.CompilerParams(vmem_limit_bytes=8 << 20),
    )(*map(in_vmem, (scaled, inputs, *sums)))


FAR, NEAR, SIDE = 4, 2, 1
LINE = (FAR | NEAR, FAR, NEAR)
EARLY = 2


def handed_over(block, sections, count, distance, mask):
    route = [
        ((s - distance) % sections * count + (i ^ mask), s * count + i)
        for s in range(sections)
        for i in range(count)
    ]
    return lax.ppermute(block, ("section", "tp"), route)


def gathered(pair, axis):
    if lax.axis_size(axis) != 8:
        return [lax.all_gather(pair[0], axis)], lambda place: place
    blocks = [pair] + [swapped(pair, axis, mask) for mask in LINE]
    masks = [far | side for far in (0, *LINE) for side in (0, SIDE)]

    def head_of(place):
        return lax.axis_index(axis) ^ masks[place]

    return blocks, head_of


def per_device(grad_attn, w_value, probs_own, probs_spare, evicted, layer_input, gain):
    sections, count = lax.axis_size("section"), lax.axis_size("tp")
    packed, spares, taken = pack(probs_own[0, 0], grad_attn[0, 0], probs_spare[0, 0], evicted)
    heads = []
    for mask in (0, SIDE) if count == 8 else (0,):
        spare = handed_over(spares, sections, count, sections // 2, mask)
        heads.append((swapped(packed, "tp", mask) if mask else packed, spare))
    weights, inputs = w_value[0], layer_input[0]
    next_input = passed_along(inputs, "section", -1)
    reach, own_reach = reach_of(weights, inputs, gain, heads[-1][0])
    if count == 8:
        reaches = [own_reach, swapped(reach, "tp", SIDE)]
        reaches[1], next_input = lax.optimization_barrier((reaches[1], next_input))
    else:
        reaches = [lax.psum(own_reach, "tp")]
    pair = value_gradients(taken, heads)
    blocks, head_of = gathered(pair, "tp")
    soon, late = (blocks[:EARLY], blocks[EARLY:]) if count == 8 else ([], blocks)
    early = [project_early(head_of, soon, weights)] if soon else []
    joined = join(head_of, soon, reaches)
    first = sum(block.shape[0] for block in soon)
    scaled, sums = project(head_of, first, late, joined, weights, inputs, gain, early)
    next_scaled = passed_along(scaled, "section", -1)
    next_sums = []
    for mask in (NEAR, FAR | NEAR, FAR) if count == 8 else ():
        next_sums.append(handed_over(sums, sections, count, -1, mask))
    return finish(next_scaled, next_input, next_sums)[None]


def solution(mesh):
    in_specs = (
        P("section", "tp", None, None),
        P("section", "tp", None),
        P("section", "tp", None, None),
        P("section", "tp", None, None),
        P("section", None),
        P("section", None, "tp"),
        P("section", "tp"),
    )
    out_specs = P("section", None, "tp")
    return jax.shard_map(
        per_device, mesh=mesh, in_specs=in_specs, out_specs=out_specs, check_vma=False
    )
```

profile of v0, /device:TPU:1, one launch (start us, length us, event | category | flops | bytes accessed | tf_op | source)
XLA Modules:
  0.0 27.7 jit_solution(12554643550788200412)
XLA Ops:
  0.0 0.0 copy-start.1
  0.0 0.0 copy-start
  0.0 0.0 copy-start.2
  0.0 1.0 %shard_map.73 = (bf16[2,128,128]{2,1,0:T(8,128)(2,1)S(1)}, bf16[128,128]{1,0:T(8,128)(2,1)S(1)}, bf16[128,128]{1,0:T(8,128)(2,1)S(1)}) custom-call(bf16[128,128]{1,0:T(8,128)(2,1)} %bitcast.12, bf16[128,128]{1,0:T(8,128)(2,1)} %bitcast.13, bf16[128,128]{1,0:T(8,128)(2,1)} %bitcast.14, s32[1,4]{1,0:T(1,128)} %evicted_ref.1), custom_call_target="tpu_custom_call" | custom-call | flops 34359738368 | bytes 33554432 | tf_op jit(solution)/shard_map/pallas_call | solution.py:87
  1.0 2.1 %collective-permute-start.2 = (bf16[2,128,128]{2,1,0:T(8,128)(2,1)S(1)}, bf16[2,128,128]{2,1,0:T(8,128)(2,1)S(1)}, u32[]{:S(2)}, u32[]{:S(2)}) collective-permute-start(bf16[2,128,128]{2,1,0:T(8,128)(2,1)S(1)} %get-tuple-element.19.refs_3_), channel_id=1, source_target_pairs={{1,0},{0,1},{3,2},{2,3},{5,4},{4,5},{7,6},{6,7},{9,8},{8,9},{11,10... | collective-permute-start | bytes 196616 | tf_op jit(solution)/shard_map/ppermute | solution.py:24
  3.1 1.2 %collective-permute-start = (bf16[128,128]{1,0:T(8,128)(2,1)S(1)}, bf16[128,128]{1,0:T(8,128)(2,1)S(1)}, u32[]{:S(2)}, u32[]{:S(2)}) collective-permute-start(bf16[128,128]{1,0:T(8,128)(2,1)S(1)} %get-tuple-element.18), channel_id=1, source_target_pairs={{16,0},{17,1},{18,2},{19,3},{20,4},{21,5},{22,6},{23,7},{24,8},{25... | collective-permute-start | bytes 98312 | tf_op jit(solution)/shard_map/ppermute | solution.py:348
  4.3 0.0 collective-permute-start.1
  4.4 0.0 copy-done.1
  4.4 1.2 %collective-permute-start.7 = (bf16[128,1536]{1,0:T(8,128)(2,1)S(1)}, bf16[128,1536]{1,0:T(8,128)(2,1)S(1)}, u32[]{:S(2)}, u32[]{:S(2)}) collective-permute-start(bf16[128,1536]{1,0:T(8,128)(2,1)S(1)} %bitcast.9), channel_id=1, source_target_pairs={{8,0},{16,8},{24,16},{0,24},{9,1},{17,9},{25,17},{1,25},{10,2},{18... | collective-permute-start | bytes 1179656 | tf_op jit(solution)/shard_map/ppermute | solution.py:20
  5.6 0.0 collective-permute-done.2.refs_2_.first_ref
  5.6 0.0 copy-done
  5.6 0.0 copy-done.2
  5.6 0.6 %shard_map.75 = (bf16[144,1024]{1,0:T(8,128)(2,1)S(1)}, f32[144,1024]{1,0:T(8,128)S(1)}) custom-call(bf16[1536,1024]{1,0:T(8,128)(2,1)S(1)} %bitcast.6, bf16[128,1536]{1,0:T(8,128)(2,1)S(1)} %bitcast.10, f32[1,1536]{1,0:T(1,128)S(1)} %copy-done.2, bf16[2,128,128]{2,1,0:T(8,128)(2,1)S(1)} %collective-permute-done.2.refs_2_.first_ref), custom_call_target="tpu_custom_call" | custom-call | flops 34359738368 | bytes 33554432 | tf_op jit(solution)/shard_map/pallas_call | solution.py:120
  6.3 1.7 %collective-permute-start.6 = (bf16[144,1024]{1,0:T(8,128)(2,1)S(1)}, bf16[144,1024]{1,0:T(8,128)(2,1)S(1)}, u32[]{:S(2)}, u32[]{:S(2)}) collective-permute-start(bf16[144,1024]{1,0:T(8,128)(2,1)S(1)} %get-tuple-element.21), channel_id=1, source_target_pairs={{1,0},{0,1},{3,2},{2,3},{5,4},{4,5},{7,6},{6,7},{9,8},{8,9},{11,10... | collective-permute-start | bytes 884744 | tf_op jit(solution)/shard_map/ppermute | solution.py:24
  8.0 0.0 collective-permute-done.refs_0_
  8.0 0.0 collective-permute-done.1.refs_1_
  8.0 0.2 shard_map.74.refs_0_
  8.2 3.4 %collective-permute-start.5 = (bf16[2,128,128]{2,1,0:T(8,128)(2,1)S(1)}, bf16[2,128,128]{2,1,0:T(8,128)(2,1)S(1)}, u32[]{:S(2)}, u32[]{:S(2)}) collective-permute-start(bf16[2,128,128]{2,1,0:T(8,128)(2,1)S(1)} %shard_map.74.refs_0_), channel_id=1, source_target_pairs={{6,0},{7,1},{4,2},{5,3},{2,4},{3,5},{0,6},{1,7},{14,8},{15,9},{12,... | collective-permute-start | bytes 196616 | tf_op jit(solution)/shard_map/ppermute | solution.py:24
  11.6 0.0 collective-permute-start.3
  11.6 0.4 %collective-permute-start.4 = (bf16[2,128,128]{2,1,0:T(8,128)(2,1)S(1)}, bf16[2,128,128]{2,1,0:T(8,128)(2,1)S(1)}, u32[]{:S(2)}, u32[]{:S(2)}) collective-permute-start(bf16[2,128,128]{2,1,0:T(8,128)(2,1)S(1)} %shard_map.74.refs_0_), channel_id=1, source_target_pairs={{2,0},{3,1},{0,2},{1,3},{6,4},{7,5},{4,6},{5,7},{10,8},{11,9},{8,1... | collective-permute-start | bytes 196616 | tf_op jit(solution)/shard_map/ppermute | solution.py:24
  12.0 1.3 %collective-permute-done.5.refs_1_ = bf16[2,128,128]{2,1,0:T(8,128)(2,1)S(1)} collective-permute-done((bf16[2,128,128]{2,1,0:T(8,128)(2,1)S(1)}, bf16[2,128,128]{2,1,0:T(8,128)(2,1)S(1)}, u32[]{:S(2)}, u32[]{:S(2)}) %collective-permute-start.5) | collective-permute-done | bytes 65568 | tf_op jit(solution)/shard_map/ppermute | solution.py:24
  13.2 0.7 %shard_map.77.refs_8_ = f32[128,1536]{1,0:T(8,128)S(1)} custom-call(bf16[2,128,128]{2,1,0:T(8,128)(2,1)S(1)} %shard_map.74.refs_0_, bf16[2,128,128]{2,1,0:T(8,128)(2,1)S(1)} %collective-permute-done.5.refs_1_, bf16[1536,1024]{1,0:T(8,128)(2,1)S(1)} %bitcast.7), custom_call_target="tpu_custom_call" | custom-call | flops 65536 | bytes 4096 | tf_op jit(solution)/shard_map/pallas_call | solution.py:199
  13.9 1.4 %collective-permute-done.6.refs_3_ = bf16[144,1024]{1,0:T(8,128)(2,1)S(1)} collective-permute-done((bf16[144,1024]{1,0:T(8,128)(2,1)S(1)}, bf16[144,1024]{1,0:T(8,128)(2,1)S(1)}, u32[]{:S(2)}, u32[]{:S(2)}) %collective-permute-start.6) | collective-permute-done | bytes 294944 | tf_op jit(solution)/shard_map/ppermute | solution.py:24
  15.3 0.0 collective-permute-done.7.input_ref
  15.3 0.1 shard_map.76
  15.4 1.3 %collective-permute-done.3.refs_0_ = bf16[2,128,128]{2,1,0:T(8,128)(2,1)S(1)} collective-permute-done((bf16[2,128,128]{2,1,0:T(8,128)(2,1)S(1)}, bf16[2,128,128]{2,1,0:T(8,128)(2,1)S(1)}, u32[]{:S(2)}, u32[]{:S(2)}) %collective-permute-start.3) | collective-permute-done | bytes 65568 | tf_op jit(solution)/shard_map/ppermute | solution.py:24
  16.8 0.0 collective-permute-done.4.refs_1_
  16.8 0.8 %shard_map.78 = (bf16[128,1664]{1,0:T(8,128)(2,1)S(1)}, f32[2,128]{1,0:T(2,128)S(1)}) custom-call(bf16[2,128,128]{2,1,0:T(8,128)(2,1)S(1)} %collective-permute-done.3.refs_0_, bf16[2,128,128]{2,1,0:T(8,128)(2,1)S(1)} %collective-permute-done.4.refs_1_, f32[128,1024]{1,0:T(8,128)S(1)} %get-tuple-element.23.refs_2_, f32[128,128]{1,0:T(8,128)S(1)} %get-tuple-element.24.refs_3_, ...), custom_call_target="tpu_custom_call" | custom-call | flops 34359738368 | bytes 33554432 | tf_op jit(solution)/shard_map/pallas_call | solution.py:282
  17.5 2.8 %collective-permute-start.8 = (bf16[128,1664]{1,0:T(8,128)(2,1)S(1)}, bf16[128,1664]{1,0:T(8,128)(2,1)S(1)}, u32[]{:S(2)}, u32[]{:S(2)}) collective-permute-start(bf16[128,1664]{1,0:T(8,128)(2,1)S(1)} %get-tuple-element.26), channel_id=1, source_target_pairs={{8,0},{16,8},{24,16},{0,24},{9,1},{17,9},{25,17},{1,25},{10,2},{18... | collective-permute-start | bytes 1277960 | tf_op jit(solution)/shard_map/ppermute | solution.py:20
  20.4 1.4 %collective-permute-start.10 = (f32[2,128]{1,0:T(2,128)S(1)}, f32[2,128]{1,0:T(2,128)S(1)}, u32[]{:S(2)}, u32[]{:S(2)}) collective-permute-start(f32[2,128]{1,0:T(2,128)S(1)} %get-tuple-element.28), channel_id=1, source_target_pairs={{14,0},{15,1},{12,2},{13,3},{10,4},{11,5},{8,6},{9,7},{22,8},{23,9... | collective-permute-start | bytes 3080 | tf_op jit(solution)/shard_map/ppermute | solution.py:348
  21.8 0.4 %collective-permute-start.11 = (f32[2,128]{1,0:T(2,128)S(1)}, f32[2,128]{1,0:T(2,128)S(1)}, u32[]{:S(2)}, u32[]{:S(2)}) collective-permute-start(f32[2,128]{1,0:T(2,128)S(1)} %get-tuple-element.28), channel_id=1, source_target_pairs={{12,0},{13,1},{14,2},{15,3},{8,4},{9,5},{10,6},{11,7},{20,8},{21,9... | collective-permute-start | bytes 3080 | tf_op jit(solution)/shard_map/ppermute | solution.py:348
  22.2 2.0 %collective-permute-start.9 = (f32[2,128]{1,0:T(2,128)S(1)}, f32[2,128]{1,0:T(2,128)S(1)}, u32[]{:S(2)}, u32[]{:S(2)}) collective-permute-start(f32[2,128]{1,0:T(2,128)S(1)} %get-tuple-element.28), channel_id=1, source_target_pairs={{10,0},{11,1},{8,2},{9,3},{14,4},{15,5},{12,6},{13,7},{18,8},{19,9... | collective-permute-start | bytes 3080 | tf_op jit(solution)/shard_map/ppermute | solution.py:348
  24.2 1.9 %collective-permute-done.10.refs_1_ = f32[2,128]{1,0:T(2,128)S(1)} collective-permute-done((f32[2,128]{1,0:T(2,128)S(1)}, f32[2,128]{1,0:T(2,128)S(1)}, u32[]{:S(2)}, u32[]{:S(2)}) %collective-permute-start.10) | collective-permute-done | bytes 1056 | tf_op jit(solution)/shard_map/ppermute | solution.py:348
  26.1 0.5 %collective-permute-done.11.refs_2_ = f32[2,128]{1,0:T(2,128)S(1)} collective-permute-done((f32[2,128]{1,0:T(2,128)S(1)}, f32[2,128]{1,0:T(2,128)S(1)}, u32[]{:S(2)}, u32[]{:S(2)}) %collective-permute-start.11) | collective-permute-done | bytes 1056 | tf_op jit(solution)/shard_map/ppermute | solution.py:348
  26.6 0.0 collective-permute-done.9.refs_0_
  26.6 0.0 collective-permute-done.8.scaled_ref
  26.6 1.1 %shard_map.79 = bf16[128,1536]{1,0:T(8,128)(2,1)} custom-call(bf16[128,1664]{1,0:T(8,128)(2,1)S(1)} %collective-permute-done.8.scaled_ref, bf16[128,1536]{1,0:T(8,128)(2,1)S(1)} %collective-permute-done.7.input_ref, f32[2,128]{1,0:T(2,128)S(1)} %collective-permute-done.9.refs_0_, f32[2,128]{1,0:T(2,128)S(1)} %collective-permute-done.10.refs_1_, ...), custom_call_target="tpu_custom_call" | custom-call | tf_op jit(solution)/shard_map/pallas_call | solution.py:324
Async XLA Ops:
  0.0 4.4 %copy-start.1 = (bf16[1,128,1536]{2,1,0:T(8,128)(2,1)S(1)}, bf16[1,128,1536]{2,1,0:T(8,128)(2,1)}, u32[]{:S(2)}) copy-start(bf16[1,128,1536]{2,1,0:T(8,128)(2,1)} %param.12) | copy-start | bytes 1179652
  0.0 5.6 %copy-start = (bf16[1,1536,1024]{2,1,0:T(8,128)(2,1)S(1)}, bf16[1,1536,1024]{2,1,0:T(8,128)(2,1)}, u32[]{:S(2)}) copy-start(bf16[1,1536,1024]{2,1,0:T(8,128)(2,1)} %param.8) | copy-start | bytes 9437188
  0.0 5.6 %copy-start.2 = (f32[1,1536]{1,0:T(1,128)S(1)}, f32[1,1536]{1,0:T(1,128)}, u32[]{:S(2)}) copy-start(f32[1,1536]{1,0:T(1,128)} %refs_7_.1) | copy-start | bytes 18436
  1.0 4.6 %collective-permute-start.2 = (bf16[2,128,128]{2,1,0:T(8,128)(2,1)S(1)}, bf16[2,128,128]{2,1,0:T(8,128)(2,1)S(1)}, u32[]{:S(2)}, u32[]{:S(2)}) collective-permute-start(bf16[2,128,128]{2,1,0:T(8,128)(2,1)S(1)} %get-tuple-element.19.refs_3_), channel_id=1, source_target_pairs={{1,0},{0,1},{3,2},{2,3},{5,4},{4,5},{7,6},{6,7},{9,8},{8,9},{11,10... | collective-permute-start | bytes 196616 | tf_op jit(solution)/shard_map/ppermute | solution.py:24
  3.1 4.9 %collective-permute-start = (bf16[128,128]{1,0:T(8,128)(2,1)S(1)}, bf16[128,128]{1,0:T(8,128)(2,1)S(1)}, u32[]{:S(2)}, u32[]{:S(2)}) collective-permute-start(bf16[128,128]{1,0:T(8,128)(2,1)S(1)} %get-tuple-element.18), channel_id=1, source_target_pairs={{16,0},{17,1},{18,2},{19,3},{20,4},{21,5},{22,6},{23,7},{24,8},{25... | collective-permute-start | bytes 98312 | tf_op jit(solution)/shard_map/ppermute | solution.py:348
  4.3 3.7 %collective-permute-start.1 = (bf16[128,128]{1,0:T(8,128)(2,1)S(1)}, bf16[128,128]{1,0:T(8,128)(2,1)S(1)}, u32[]{:S(2)}, u32[]{:S(2)}) collective-permute-start(bf16[128,128]{1,0:T(8,128)(2,1)S(1)} %get-tuple-element.18), channel_id=1, source_target_pairs={{17,0},{16,1},{19,2},{18,3},{21,4},{20,5},{23,6},{22,7},{25,8},{24... | collective-permute-start | bytes 98312 | tf_op jit(solution)/shard_map/ppermute | solution.py:348
  4.4 10.9 %collective-permute-start.7 = (bf16[128,1536]{1,0:T(8,128)(2,1)S(1)}, bf16[128,1536]{1,0:T(8,128)(2,1)S(1)}, u32[]{:S(2)}, u32[]{:S(2)}) collective-permute-start(bf16[128,1536]{1,0:T(8,128)(2,1)S(1)} %bitcast.9), channel_id=1, source_target_pairs={{8,0},{16,8},{24,16},{0,24},{9,1},{17,9},{25,17},{1,25},{10,2},{18... | collective-permute-start | bytes 1179656 | tf_op jit(solution)/shard_map/ppermute | solution.py:20
  6.3 9.1 %collective-permute-start.6 = (bf16[144,1024]{1,0:T(8,128)(2,1)S(1)}, bf16[144,1024]{1,0:T(8,128)(2,1)S(1)}, u32[]{:S(2)}, u32[]{:S(2)}) collective-permute-start(bf16[144,1024]{1,0:T(8,128)(2,1)S(1)} %get-tuple-element.21), channel_id=1, source_target_pairs={{1,0},{0,1},{3,2},{2,3},{5,4},{4,5},{7,6},{6,7},{9,8},{8,9},{11,10... | collective-permute-start | bytes 884744 | tf_op jit(solution)/shard_map/ppermute | solution.py:24
  8.2 5.0 %collective-permute-start.5 = (bf16[2,128,128]{2,1,0:T(8,128)(2,1)S(1)}, bf16[2,128,128]{2,1,0:T(8,128)(2,1)S(1)}, u32[]{:S(2)}, u32[]{:S(2)}) collective-permute-start(bf16[2,128,128]{2,1,0:T(8,128)(2,1)S(1)} %shard_map.74.refs_0_), channel_id=1, source_target_pairs={{6,0},{7,1},{4,2},{5,3},{2,4},{3,5},{0,6},{1,7},{14,8},{15,9},{12,... | collective-permute-start | bytes 196616 | tf_op jit(solution)/shard_map/ppermute | solution.py:24
  11.6 5.2 %collective-permute-start.3 = (bf16[2,128,128]{2,1,0:T(8,128)(2,1)S(1)}, bf16[2,128,128]{2,1,0:T(8,128)(2,1)S(1)}, u32[]{:S(2)}, u32[]{:S(2)}) collective-permute-start(bf16[2,128,128]{2,1,0:T(8,128)(2,1)S(1)} %shard_map.74.refs_0_), channel_id=1, source_target_pairs={{4,0},{5,1},{6,2},{7,3},{0,4},{1,5},{2,6},{3,7},{12,8},{13,9},{14,... | collective-permute-start | bytes 196616 | tf_op jit(solution)/shard_map/ppermute | solution.py:24
  11.6 5.2 %collective-permute-start.4 = (bf16[2,128,128]{2,1,0:T(8,128)(2,1)S(1)}, bf16[2,128,128]{2,1,0:T(8,128)(2,1)S(1)}, u32[]{:S(2)}, u32[]{:S(2)}) collective-permute-start(bf16[2,128,128]{2,1,0:T(8,128)(2,1)S(1)} %shard_map.74.refs_0_), channel_id=1, source_target_pairs={{2,0},{3,1},{0,2},{1,3},{6,4},{7,5},{4,6},{5,7},{10,8},{11,9},{8,1... | collective-permute-start | bytes 196616 | tf_op jit(solution)/shard_map/ppermute | solution.py:24
  17.5 9.1 %collective-permute-start.8 = (bf16[128,1664]{1,0:T(8,128)(2,1)S(1)}, bf16[128,1664]{1,0:T(8,128)(2,1)S(1)}, u32[]{:S(2)}, u32[]{:S(2)}) collective-permute-start(bf16[128,1664]{1,0:T(8,128)(2,1)S(1)} %get-tuple-element.26), channel_id=1, source_target_pairs={{8,0},{16,8},{24,16},{0,24},{9,1},{17,9},{25,17},{1,25},{10,2},{18... | collective-permute-start | bytes 1277960 | tf_op jit(solution)/shard_map/ppermute | solution.py:20
  20.4 5.7 %collective-permute-start.10 = (f32[2,128]{1,0:T(2,128)S(1)}, f32[2,128]{1,0:T(2,128)S(1)}, u32[]{:S(2)}, u32[]{:S(2)}) collective-permute-start(f32[2,128]{1,0:T(2,128)S(1)} %get-tuple-element.28), channel_id=1, source_target_pairs={{14,0},{15,1},{12,2},{13,3},{10,4},{11,5},{8,6},{9,7},{22,8},{23,9... | collective-permute-start | bytes 3080 | tf_op jit(solution)/shard_map/ppermute | solution.py:348
  21.8 4.8 %collective-permute-start.11 = (f32[2,128]{1,0:T(2,128)S(1)}, f32[2,128]{1,0:T(2,128)S(1)}, u32[]{:S(2)}, u32[]{:S(2)}) collective-permute-start(f32[2,128]{1,0:T(2,128)S(1)} %get-tuple-element.28), channel_id=1, source_target_pairs={{12,0},{13,1},{14,2},{15,3},{8,4},{9,5},{10,6},{11,7},{20,8},{21,9... | collective-permute-start | bytes 3080 | tf_op jit(solution)/shard_map/ppermute | solution.py:348
  22.2 4.4 %collective-permute-start.9 = (f32[2,128]{1,0:T(2,128)S(1)}, f32[2,128]{1,0:T(2,128)S(1)}, u32[]{:S(2)}, u32[]{:S(2)}) collective-permute-start(f32[2,128]{1,0:T(2,128)S(1)} %get-tuple-element.28), channel_id=1, source_target_pairs={{10,0},{11,1},{8,2},{9,3},{14,4},{15,5},{12,6},{13,7},{18,8},{19,9... | collective-permute-start | bytes 3080 | tf_op jit(solution)/shard_map/ppermute | solution.py:348
where the time goes:
time: 27.9 us; the launch traced here: 27.7 us
  starting transfers between devices  16.8 us (60%)
  waiting for transfers between devices  6.45 us (23%)
  Pallas kernels  4.38 us (16%)
    ppermute x5, starting transfers between devices, swapped(): lax.ppermute(block, axis, [(i ^ mask, i) for i in range(lax.axis_size(axi...  7.61 us
    ppermute x5, starting transfers between devices, handed_over(): return lax.ppermute(block, ('section', 'tp'), route)  5.09 us
    ppermute x2, starting transfers between devices, passed_along(): return lax.ppermute(block, axis, route)  4.06 us
    ppermute x5, waiting for transfers between devices, swapped(): lax.ppermute(block, axis, [(i ^ mask, i) for i in range(lax.axis_size(axi...  4.02 us
    ppermute x5, waiting for transfers between devices, handed_over(): return lax.ppermute(block, ('section', 'tp'), route)  2.43 us
    pallas_call x1, Pallas kernels, finish(): pl.pallas_call(finish_kernel, out_shape=pltpu.HBM(inputs.shape, jnp.bfloa...  1.06 us
    pallas_call x1, Pallas kernels, pack(): pl.pallas_call(pack_kernel, out_shape=(pltpu.VMEM((2, *own.shape), own.dt...  0.98 us
    pallas_call x1, Pallas kernels, project(): pl.pallas_call(functools.partial(project_kernel, head_of, first, len(bloc...  0.77 us
  transfers between devices with their start and end apart: 12, of which 5 were waited for; matrix products, arithmetic and copies ran while one was open for 0% of the time, Pallas kernels for 6%

commit v1 on v0

--- a/solution.py
+++ b/solution.py
@@ -134,7 +134,7 @@
     out_ref = refs[-1]
     taken = taken_ref[...]
     for j in range(out_ref.shape[0]):
-        packed_ref, spare_ref = refs[len(refs) - 2 - j], refs[j]
+        packed_ref, spare_ref = refs[len(refs) - 2 - j], refs[out_ref.shape[0] - 1 - j]
         out_ref[j] = lax.dot_general(
             packed_ref[0] * (1 - taken) + spare_ref[...] * taken,
             packed_ref[1],
@@ -151,7 +151,7 @@
         out_specs=pl.BlockSpec(memory_space=pltpu.VMEM),
         cost_estimate=HIDES,
         compiler_params=pltpu.CompilerParams(vmem_limit_bytes=4 << 20),
-    )(*map(in_vmem, (taken, *[spare for _, spare in heads], *[packed for packed, _ in heads[::-1]])))
+    )(*map(in_vmem, (taken, *[spare for _, spare in heads[::-1]], *[packed for packed, _ in heads[::-1]])))
 
 
 def column_tile(features):

time: 27.9 us -> 27.8 us (level)
    ppermute x2, starting transfers between devices: 4.06 us -> 3.19 us  [passed_along(): return lax.ppermute(block, axis, route)]
    ppermute x5, starting transfers between devices: 5.09 us -> 5.9 us  [handed_over(): return lax.ppermute(block, ('section', 'tp'), route)]
  transfers between devices with their start and end apart: 12 -> 12, of which waited for: 5 -> 6; matrix products, arithmetic and copies ran while one was open for 0% -> 0% of each run, Pallas kernels for 6% -> 6%
where the time goes in v1:
time: 27.8 us; the launch traced here: 27.4 us
  starting transfers between devices  16.7 us (60%)
  waiting for transfers between devices  6.25 us (22%)
  Pallas kernels  4.39 us (16%)
    ppermute x5, starting transfers between devices, swapped(): lax.ppermute(block, axis, [(i ^ mask, i) for i in range(lax.axis_size(axi...  7.61 us
    ppermute x5, starting transfers between devices, handed_over(): return lax.ppermute(block, ('section', 'tp'), route)  5.9 us
    ppermute x5, waiting for transfers between devices, swapped(): lax.ppermute(block, axis, [(i ^ mask, i) for i in range(lax.axis_size(axi...  4.01 us
    ppermute x2, starting transfers between devices, passed_along(): return lax.ppermute(block, axis, route)  3.19 us
    ppermute x5, waiting for transfers between devices, handed_over(): return lax.ppermute(block, ('section', 'tp'), route)  2.17 us
    pallas_call x1, Pallas kernels, finish(): pl.pallas_call(finish_kernel, out_shape=pltpu.HBM(inputs.shape, jnp.bfloa...  1.06 us
    pallas_call x1, Pallas kernels, pack(): pl.pallas_call(pack_kernel, out_shape=(pltpu.VMEM((2, *own.shape), own.dt...  0.98 us
    pallas_call x1, Pallas kernels, project(): pl.pallas_call(functools.partial(project_kernel, head_of, first, len(bloc...  0.77 us
  transfers between devices with their start and end apart: 12, of which 6 were waited for; matrix products, arithmetic and copies ran while one was open for 0% of the time, Pallas kernels for 6%

profile of v1, /device:TPU:1, one launch (start us, length us, event | category | flops | bytes accessed | tf_op | source)
XLA Modules:
  0.0 27.4 jit_solution(14439278660303990096)
XLA Ops:
  0.0 0.0 copy-start.1
  0.0 0.0 copy-start
  0.0 0.0 copy-start.2
  0.0 1.0 %shard_map.73 = (bf16[2,128,128]{2,1,0:T(8,128)(2,1)S(1)}, bf16[128,128]{1,0:T(8,128)(2,1)S(1)}, bf16[128,128]{1,0:T(8,128)(2,1)S(1)}) custom-call(bf16[128,128]{1,0:T(8,128)(2,1)} %bitcast.12, bf16[128,128]{1,0:T(8,128)(2,1)} %bitcast.13, bf16[128,128]{1,0:T(8,128)(2,1)} %bitcast.14, s32[1,4]{1,0:T(1,128)} %evicted_ref.1), custom_call_target="tpu_custom_call" | custom-call | flops 34359738368 | bytes 33554432 | tf_op jit(solution)/shard_map/pallas_call | solution.py:87
  1.0 2.1 %collective-permute-start.2 = (bf16[2,128,128]{2,1,0:T(8,128)(2,1)S(1)}, bf16[2,128,128]{2,1,0:T(8,128)(2,1)S(1)}, u32[]{:S(2)}, u32[]{:S(2)}) collective-permute-start(bf16[2,128,128]{2,1,0:T(8,128)(2,1)S(1)} %get-tuple-element.19.refs_3_), channel_id=1, source_target_pairs={{1,0},{0,1},{3,2},{2,3},{5,4},{4,5},{7,6},{6,7},{9,8},{8,9},{11,10... | collective-permute-start | bytes 196616 | tf_op jit(solution)/shard_map/ppermute | solution.py:24
  3.1 1.2 %collective-permute-start = (bf16[128,128]{1,0:T(8,128)(2,1)S(1)}, bf16[128,128]{1,0:T(8,128)(2,1)S(1)}, u32[]{:S(2)}, u32[]{:S(2)}) collective-permute-start(bf16[128,128]{1,0:T(8,128)(2,1)S(1)} %get-tuple-element.18), channel_id=1, source_target_pairs={{17,0},{16,1},{19,2},{18,3},{21,4},{20,5},{23,6},{22,7},{25,8},{24... | collective-permute-start | bytes 98312 | tf_op jit(solution)/shard_map/ppermute | solution.py:348
  4.3 0.1 collective-permute-start.1
  4.4 0.0 copy-done.1
  4.4 1.2 %collective-permute-start.7 = (bf16[128,1536]{1,0:T(8,128)(2,1)S(1)}, bf16[128,1536]{1,0:T(8,128)(2,1)S(1)}, u32[]{:S(2)}, u32[]{:S(2)}) collective-permute-start(bf16[128,1536]{1,0:T(8,128)(2,1)S(1)} %bitcast.9), channel_id=1, source_target_pairs={{8,0},{16,8},{24,16},{0,24},{9,1},{17,9},{25,17},{1,25},{10,2},{18... | collective-permute-start | bytes 1179656 | tf_op jit(solution)/shard_map/ppermute | solution.py:20
  5.6 0.0 collective-permute-done.2.refs_2_.first_ref
  5.6 0.0 copy-done
  5.6 0.0 copy-done.2
  5.6 0.6 %shard_map.75 = (bf16[144,1024]{1,0:T(8,128)(2,1)S(1)}, f32[144,1024]{1,0:T(8,128)S(1)}) custom-call(bf16[1536,1024]{1,0:T(8,128)(2,1)S(1)} %bitcast.6, bf16[128,1536]{1,0:T(8,128)(2,1)S(1)} %bitcast.10, f32[1,1536]{1,0:T(1,128)S(1)} %copy-done.2, bf16[2,128,128]{2,1,0:T(8,128)(2,1)S(1)} %collective-permute-done.2.refs_2_.first_ref), custom_call_target="tpu_custom_call" | custom-call | flops 34359738368 | bytes 33554432 | tf_op jit(solution)/shard_map/pallas_call | solution.py:120
  6.3 1.7 %collective-permute-start.6 = (bf16[144,1024]{1,0:T(8,128)(2,1)S(1)}, bf16[144,1024]{1,0:T(8,128)(2,1)S(1)}, u32[]{:S(2)}, u32[]{:S(2)}) collective-permute-start(bf16[144,1024]{1,0:T(8,128)(2,1)S(1)} %get-tuple-element.21), channel_id=1, source_target_pairs={{1,0},{0,1},{3,2},{2,3},{5,4},{4,5},{7,6},{6,7},{9,8},{8,9},{11,10... | collective-permute-start | bytes 884744 | tf_op jit(solution)/shard_map/ppermute | solution.py:24
  8.0 0.0 collective-permute-done.refs_0_
  8.0 0.0 collective-permute-done.1.refs_1_
  8.0 0.2 shard_map.74.refs_0_
  8.2 3.4 %collective-permute-start.5 = (bf16[2,128,128]{2,1,0:T(8,128)(2,1)S(1)}, bf16[2,128,128]{2,1,0:T(8,128)(2,1)S(1)}, u32[]{:S(2)}, u32[]{:S(2)}) collective-permute-start(bf16[2,128,128]{2,1,0:T(8,128)(2,1)S(1)} %shard_map.74.refs_0_), channel_id=1, source_target_pairs={{6,0},{7,1},{4,2},{5,3},{2,4},{3,5},{0,6},{1,7},{14,8},{15,9},{12,... | collective-permute-start | bytes 196616 | tf_op jit(solution)/shard_map/ppermute | solution.py:24
  11.6 0.0 collective-permute-start.3
  11.6 0.4 %collective-permute-start.4 = (bf16[2,128,128]{2,1,0:T(8,128)(2,1)S(1)}, bf16[2,128,128]{2,1,0:T(8,128)(2,1)S(1)}, u32[]{:S(2)}, u32[]{:S(2)}) collective-permute-start(bf16[2,128,128]{2,1,0:T(8,128)(2,1)S(1)} %shard_map.74.refs_0_), channel_id=1, source_target_pairs={{2,0},{3,1},{0,2},{1,3},{6,4},{7,5},{4,6},{5,7},{10,8},{11,9},{8,1... | collective-permute-start | bytes 196616 | tf_op jit(solution)/shard_map/ppermute | solution.py:24
  11.9 1.3 %collective-permute-done.5.refs_1_ = bf16[2,128,128]{2,1,0:T(8,128)(2,1)S(1)} collective-permute-done((bf16[2,128,128]{2,1,0:T(8,128)(2,1)S(1)}, bf16[2,128,128]{2,1,0:T(8,128)(2,1)S(1)}, u32[]{:S(2)}, u32[]{:S(2)}) %collective-permute-start.5) | collective-permute-done | bytes 65568 | tf_op jit(solution)/shard_map/ppermute | solution.py:24
  13.2 0.7 %shard_map.77.refs_8_ = f32[128,1536]{1,0:T(8,128)S(1)} custom-call(bf16[2,128,128]{2,1,0:T(8,128)(2,1)S(1)} %shard_map.74.refs_0_, bf16[2,128,128]{2,1,0:T(8,128)(2,1)S(1)} %collective-permute-done.5.refs_1_, bf16[1536,1024]{1,0:T(8,128)(2,1)S(1)} %bitcast.7), custom_call_target="tpu_custom_call" | custom-call | flops 65536 | bytes 4096 | tf_op jit(solution)/shard_map/pallas_call | solution.py:199
  13.9 0.5 %collective-permute-done.6.refs_3_ = bf16[144,1024]{1,0:T(8,128)(2,1)S(1)} collective-permute-done((bf16[144,1024]{1,0:T(8,128)(2,1)S(1)}, bf16[144,1024]{1,0:T(8,128)(2,1)S(1)}, u32[]{:S(2)}, u32[]{:S(2)}) %collective-permute-start.6) | collective-permute-done | bytes 294944 | tf_op jit(solution)/shard_map/ppermute | solution.py:24
  14.4 0.0 collective-permute-done.7.input_ref
  14.4 0.1 shard_map.76
  14.5 2.2 %collective-permute-done.3.refs_0_ = bf16[2,128,128]{2,1,0:T(8,128)(2,1)S(1)} collective-permute-done((bf16[2,128,128]{2,1,0:T(8,128)(2,1)S(1)}, bf16[2,128,128]{2,1,0:T(8,128)(2,1)S(1)}, u32[]{:S(2)}, u32[]{:S(2)}) %collective-permute-start.3) | collective-permute-done | bytes 65568 | tf_op jit(solution)/shard_map/ppermute | solution.py:24
  16.7 0.0 collective-permute-done.4.refs_1_
  16.7 0.8 %shard_map.78 = (bf16[128,1664]{1,0:T(8,128)(2,1)S(1)}, f32[2,128]{1,0:T(2,128)S(1)}) custom-call(bf16[2,128,128]{2,1,0:T(8,128)(2,1)S(1)} %collective-permute-done.3.refs_0_, bf16[2,128,128]{2,1,0:T(8,128)(2,1)S(1)} %collective-permute-done.4.refs_1_, f32[128,1024]{1,0:T(8,128)S(1)} %get-tuple-element.23.refs_2_, f32[128,128]{1,0:T(8,128)S(1)} %get-tuple-element.24.refs_3_, ...), custom_call_target="tpu_custom_call" | custom-call | flops 34359738368 | bytes 33554432 | tf_op jit(solution)/shard_map/pallas_call | solution.py:282
  17.5 2.0 %collective-permute-start.8 = (bf16[128,1664]{1,0:T(8,128)(2,1)S(1)}, bf16[128,1664]{1,0:T(8,128)(2,1)S(1)}, u32[]{:S(2)}, u32[]{:S(2)}) collective-permute-start(bf16[128,1664]{1,0:T(8,128)(2,1)S(1)} %get-tuple-element.26), channel_id=1, source_target_pairs={{8,0},{16,8},{24,16},{0,24},{9,1},{17,9},{25,17},{1,25},{10,2},{18... | collective-permute-start | bytes 1277960 | tf_op jit(solution)/shard_map/ppermute | solution.py:20
  19.5 2.0 %collective-permute-start.10 = (f32[2,128]{1,0:T(2,128)S(1)}, f32[2,128]{1,0:T(2,128)S(1)}, u32[]{:S(2)}, u32[]{:S(2)}) collective-permute-start(f32[2,128]{1,0:T(2,128)S(1)} %get-tuple-element.28), channel_id=1, source_target_pairs={{14,0},{15,1},{12,2},{13,3},{10,4},{11,5},{8,6},{9,7},{22,8},{23,9... | collective-permute-start | bytes 3080 | tf_op jit(solution)/shard_map/ppermute | solution.py:348
  21.5 0.7 %collective-permute-start.11 = (f32[2,128]{1,0:T(2,128)S(1)}, f32[2,128]{1,0:T(2,128)S(1)}, u32[]{:S(2)}, u32[]{:S(2)}) collective-permute-start(f32[2,128]{1,0:T(2,128)S(1)} %get-tuple-element.28), channel_id=1, source_target_pairs={{12,0},{13,1},{14,2},{15,3},{8,4},{9,5},{10,6},{11,7},{20,8},{21,9... | collective-permute-start | bytes 3080 | tf_op jit(solution)/shard_map/ppermute | solution.py:348
  22.1 2.0 %collective-permute-start.9 = (f32[2,128]{1,0:T(2,128)S(1)}, f32[2,128]{1,0:T(2,128)S(1)}, u32[]{:S(2)}, u32[]{:S(2)}) collective-permute-start(f32[2,128]{1,0:T(2,128)S(1)} %get-tuple-element.28), channel_id=1, source_target_pairs={{10,0},{11,1},{8,2},{9,3},{14,4},{15,5},{12,6},{13,7},{18,8},{19,9... | collective-permute-start | bytes 3080 | tf_op jit(solution)/shard_map/ppermute | solution.py:348
  24.1 1.1 %collective-permute-done.10.refs_1_ = f32[2,128]{1,0:T(2,128)S(1)} collective-permute-done((f32[2,128]{1,0:T(2,128)S(1)}, f32[2,128]{1,0:T(2,128)S(1)}, u32[]{:S(2)}, u32[]{:S(2)}) %collective-permute-start.10) | collective-permute-done | bytes 1056 | tf_op jit(solution)/shard_map/ppermute | solution.py:348
  25.2 1.1 %collective-permute-done.11.refs_2_ = f32[2,128]{1,0:T(2,128)S(1)} collective-permute-done((f32[2,128]{1,0:T(2,128)S(1)}, f32[2,128]{1,0:T(2,128)S(1)}, u32[]{:S(2)}, u32[]{:S(2)}) %collective-permute-start.11) | collective-permute-done | bytes 1056 | tf_op jit(solution)/shard_map/ppermute | solution.py:348
  26.3 0.0 collective-permute-done.9.refs_0_
  26.3 0.1 collective-permute-done.8.scaled_ref
  26.4 1.1 %shard_map.79 = bf16[128,1536]{1,0:T(8,128)(2,1)} custom-call(bf16[128,1664]{1,0:T(8,128)(2,1)S(1)} %collective-permute-done.8.scaled_ref, bf16[128,1536]{1,0:T(8,128)(2,1)S(1)} %collective-permute-done.7.input_ref, f32[2,128]{1,0:T(2,128)S(1)} %collective-permute-done.9.refs_0_, f32[2,128]{1,0:T(2,128)S(1)} %collective-permute-done.10.refs_1_, ...), custom_call_target="tpu_custom_call" | custom-call | tf_op jit(solution)/shard_map/pallas_call | solution.py:324
Async XLA Ops:
  0.0 4.4 %copy-start.1 = (bf16[1,128,1536]{2,1,0:T(8,128)(2,1)S(1)}, bf16[1,128,1536]{2,1,0:T(8,128)(2,1)}, u32[]{:S(2)}) copy-start(bf16[1,128,1536]{2,1,0:T(8,128)(2,1)} %param.12) | copy-start | bytes 1179652
  0.0 5.6 %copy-start = (bf16[1,1536,1024]{2,1,0:T(8,128)(2,1)S(1)}, bf16[1,1536,1024]{2,1,0:T(8,128)(2,1)}, u32[]{:S(2)}) copy-start(bf16[1,1536,1024]{2,1,0:T(8,128)(2,1)} %param.8) | copy-start | bytes 9437188
  0.0 5.6 %copy-start.2 = (f32[1,1536]{1,0:T(1,128)S(1)}, f32[1,1536]{1,0:T(1,128)}, u32[]{:S(2)}) copy-start(f32[1,1536]{1,0:T(1,128)} %refs_7_.1) | copy-start | bytes 18436
  1.0 4.6 %collective-permute-start.2 = (bf16[2,128,128]{2,1,0:T(8,128)(2,1)S(1)}, bf16[2,128,128]{2,1,0:T(8,128)(2,1)S(1)}, u32[]{:S(2)}, u32[]{:S(2)}) collective-permute-start(bf16[2,128,128]{2,1,0:T(8,128)(2,1)S(1)} %get-tuple-element.19.refs_3_), channel_id=1, source_target_pairs={{1,0},{0,1},{3,2},{2,3},{5,4},{4,5},{7,6},{6,7},{9,8},{8,9},{11,10... | collective-permute-start | bytes 196616 | tf_op jit(solution)/shard_map/ppermute | solution.py:24
  3.1 4.9 %collective-permute-start = (bf16[128,128]{1,0:T(8,128)(2,1)S(1)}, bf16[128,128]{1,0:T(8,128)(2,1)S(1)}, u32[]{:S(2)}, u32[]{:S(2)}) collective-permute-start(bf16[128,128]{1,0:T(8,128)(2,1)S(1)} %get-tuple-element.18), channel_id=1, source_target_pairs={{17,0},{16,1},{19,2},{18,3},{21,4},{20,5},{23,6},{22,7},{25,8},{24... | collective-permute-start | bytes 98312 | tf_op jit(solution)/shard_map/ppermute | solution.py:348
  4.3 3.7 %collective-permute-start.1 = (bf16[128,128]{1,0:T(8,128)(2,1)S(1)}, bf16[128,128]{1,0:T(8,128)(2,1)S(1)}, u32[]{:S(2)}, u32[]{:S(2)}) collective-permute-start(bf16[128,128]{1,0:T(8,128)(2,1)S(1)} %get-tuple-element.18), channel_id=1, source_target_pairs={{16,0},{17,1},{18,2},{19,3},{20,4},{21,5},{22,6},{23,7},{24,8},{25... | collective-permute-start | bytes 98312 | tf_op jit(solution)/shard_map/ppermute | solution.py:348
  4.4 10.0 %collective-permute-start.7 = (bf16[128,1536]{1,0:T(8,128)(2,1)S(1)}, bf16[128,1536]{1,0:T(8,128)(2,1)S(1)}, u32[]{:S(2)}, u32[]{:S(2)}) collective-permute-start(bf16[128,1536]{1,0:T(8,128)(2,1)S(1)} %bitcast.9), channel_id=1, source_target_pairs={{8,0},{16,8},{24,16},{0,24},{9,1},{17,9},{25,17},{1,25},{10,2},{18... | collective-permute-start | bytes 1179656 | tf_op jit(solution)/shard_map/ppermute | solution.py:20
  6.3 8.1 %collective-permute-start.6 = (bf16[144,1024]{1,0:T(8,128)(2,1)S(1)}, bf16[144,1024]{1,0:T(8,128)(2,1)S(1)}, u32[]{:S(2)}, u32[]{:S(2)}) collective-permute-start(bf16[144,1024]{1,0:T(8,128)(2,1)S(1)} %get-tuple-element.21), channel_id=1, source_target_pairs={{1,0},{0,1},{3,2},{2,3},{5,4},{4,5},{7,6},{6,7},{9,8},{8,9},{11,10... | collective-permute-start | bytes 884744 | tf_op jit(solution)/shard_map/ppermute | solution.py:24
  8.2 5.0 %collective-permute-start.5 = (bf16[2,128,128]{2,1,0:T(8,128)(2,1)S(1)}, bf16[2,128,128]{2,1,0:T(8,128)(2,1)S(1)}, u32[]{:S(2)}, u32[]{:S(2)}) collective-permute-start(bf16[2,128,128]{2,1,0:T(8,128)(2,1)S(1)} %shard_map.74.refs_0_), channel_id=1, source_target_pairs={{6,0},{7,1},{4,2},{5,3},{2,4},{3,5},{0,6},{1,7},{14,8},{15,9},{12,... | collective-permute-start | bytes 196616 | tf_op jit(solution)/shard_map/ppermute | solution.py:24
  11.6 5.2 %collective-permute-start.3 = (bf16[2,128,128]{2,1,0:T(8,128)(2,1)S(1)}, bf16[2,128,128]{2,1,0:T(8,128)(2,1)S(1)}, u32[]{:S(2)}, u32[]{:S(2)}) collective-permute-start(bf16[2,128,128]{2,1,0:T(8,128)(2,1)S(1)} %shard_map.74.refs_0_), channel_id=1, source_target_pairs={{4,0},{5,1},{6,2},{7,3},{0,4},{1,5},{2,6},{3,7},{12,8},{13,9},{14,... | collective-permute-start | bytes 196616 | tf_op jit(solution)/shard_map/ppermute | solution.py:24
  11.6 5.2 %collective-permute-start.4 = (bf16[2,128,128]{2,1,0:T(8,128)(2,1)S(1)}, bf16[2,128,128]{2,1,0:T(8,128)(2,1)S(1)}, u32[]{:S(2)}, u32[]{:S(2)}) collective-permute-start(bf16[2,128,128]{2,1,0:T(8,128)(2,1)S(1)} %shard_map.74.refs_0_), channel_id=1, source_target_pairs={{2,0},{3,1},{0,2},{1,3},{6,4},{7,5},{4,6},{5,7},{10,8},{11,9},{8,1... | collective-permute-start | bytes 196616 | tf_op jit(solution)/shard_map/ppermute | solution.py:24
  17.5 8.8 %collective-permute-start.8 = (bf16[128,1664]{1,0:T(8,128)(2,1)S(1)}, bf16[128,1664]{1,0:T(8,128)(2,1)S(1)}, u32[]{:S(2)}, u32[]{:S(2)}) collective-permute-start(bf16[128,1664]{1,0:T(8,128)(2,1)S(1)} %get-tuple-element.26), channel_id=1, source_target_pairs={{8,0},{16,8},{24,16},{0,24},{9,1},{17,9},{25,17},{1,25},{10,2},{18... | collective-permute-start | bytes 1277960 | tf_op jit(solution)/shard_map/ppermute | solution.py:20
  19.5 5.7 %collective-permute-start.10 = (f32[2,128]{1,0:T(2,128)S(1)}, f32[2,128]{1,0:T(2,128)S(1)}, u32[]{:S(2)}, u32[]{:S(2)}) collective-permute-start(f32[2,128]{1,0:T(2,128)S(1)} %get-tuple-element.28), channel_id=1, source_target_pairs={{14,0},{15,1},{12,2},{13,3},{10,4},{11,5},{8,6},{9,7},{22,8},{23,9... | collective-permute-start | bytes 3080 | tf_op jit(solution)/shard_map/ppermute | solution.py:348
  21.5 4.8 %collective-permute-start.11 = (f32[2,128]{1,0:T(2,128)S(1)}, f32[2,128]{1,0:T(2,128)S(1)}, u32[]{:S(2)}, u32[]{:S(2)}) collective-permute-start(f32[2,128]{1,0:T(2,128)S(1)} %get-tuple-element.28), channel_id=1, source_target_pairs={{12,0},{13,1},{14,2},{15,3},{8,4},{9,5},{10,6},{11,7},{20,8},{21,9... | collective-permute-start | bytes 3080 | tf_op jit(solution)/shard_map/ppermute | solution.py:348
  22.1 4.2 %collective-permute-start.9 = (f32[2,128]{1,0:T(2,128)S(1)}, f32[2,128]{1,0:T(2,128)S(1)}, u32[]{:S(2)}, u32[]{:S(2)}) collective-permute-start(f32[2,128]{1,0:T(2,128)S(1)} %get-tuple-element.28), channel_id=1, source_target_pairs={{10,0},{11,1},{8,2},{9,3},{14,4},{15,5},{12,6},{13,7},{18,8},{19,9... | collective-permute-start | bytes 3080 | tf_op jit(solution)/shard_map/ppermute | solution.py:348

commit v2 on v1

--- a/solution.py
+++ b/solution.py
@@ -130,28 +130,33 @@
     )(*map(in_vmem, (weights, inputs, gain, first)))
 
 
-def mix_kernel(taken_ref, *refs):
+def mix_kernel(upper, taken_ref, *refs):
     out_ref = refs[-1]
     taken = taken_ref[...]
-    for j in range(out_ref.shape[0]):
-        packed_ref, spare_ref = refs[len(refs) - 2 - j], refs[out_ref.shape[0] - 1 - j]
+    count = out_ref.shape[0]
+    spares = [refs[count - 1 - j][...] for j in range(count)]
+    if count == 2:
+        swap = upper()
+        spares = [jnp.where(swap, spares[1], spares[0]), jnp.where(swap, spares[0], spares[1])]
+    for j in range(count):
+        packed_ref = refs[len(refs) - 2 - j]
         out_ref[j] = lax.dot_general(
-            packed_ref[0] * (1 - taken) + spare_ref[...] * taken,
+            packed_ref[0] * (1 - taken) + spares[j] * taken,
             packed_ref[1],
             (((0,), (0,)), ((), ())),
             preferred_element_type=jnp.float32,
         ).astype(out_ref.dtype)
 
 
-def value_gradients(taken, heads):
-    return pl.pallas_call(
-        mix_kernel,
-        out_shape=pltpu.VMEM((len(heads), *heads[0][1].shape), jnp.bfloat16),
-        in_specs=vmem_specs(1 + 2 * len(heads)),
+def value_gradients(taken, spares, packs, upper):
+    return pl.pallas_call(
+        functools.partial(mix_kernel, upper),
+        out_shape=pltpu.VMEM((len(packs), *spares[0].shape), jnp.bfloat16),
+        in_specs=vmem_specs(1 + 2 * len(packs)),
         out_specs=pl.BlockSpec(memory_space=pltpu.VMEM),
         cost_estimate=HIDES,
         compiler_params=pltpu.CompilerParams(vmem_limit_bytes=4 << 20),
-    )(*map(in_vmem, (taken, *[spare for _, spare in heads[::-1]], *[packed for packed, _ in heads[::-1]])))
+    )(*map(in_vmem, (taken, *spares[::-1], *packs[::-1])))
 
 
 def column_tile(features):
@@ -335,6 +340,7 @@
 
 
 FAR, NEAR, SIDE = 4, 2, 1
+ORDER = ((0, SIDE), (SIDE, 0))
 LINE = (FAR | NEAR, FAR, NEAR)
 EARLY = 2
 
@@ -348,6 +354,16 @@
     return lax.ppermute(block, ("section", "tp"), route)
 
 
+def fetched(block, sections, count, masks):
+    half = sections // 2
+    route = []
+    for s in range(sections):
+        mask = masks[s // half] if count == 8 else 0
+        for i in range(count):
+            route.append(((s + half) % sections * count + (i ^ mask), s * count + i))
+    return lax.ppermute(block, ("section", "tp"), route)
+
+
 def gathered(pair, axis):
     if lax.axis_size(axis) != 8:
         return [lax.all_gather(pair[0], axis)], lambda place: place
@@ -363,19 +379,18 @@
 def per_device(grad_attn, w_value, probs_own, probs_spare, evicted, layer_input, gain):
     sections, count = lax.axis_size("section"), lax.axis_size("tp")
     packed, spares, taken = pack(probs_own[0, 0], grad_attn[0, 0], probs_spare[0, 0], evicted)
-    heads = []
-    for mask in (0, SIDE) if count == 8 else (0,):
-        spare = handed_over(spares, sections, count, sections // 2, mask)
-        heads.append((swapped(packed, "tp", mask) if mask else packed, spare))
+    half = sections // 2
+    packs = [packed, swapped(packed, "tp", SIDE)] if count == 8 else [packed]
+    spares = [fetched(spares, sections, count, masks) for masks in ORDER[: len(packs)]]
     weights, inputs = w_value[0], layer_input[0]
     next_input = passed_along(inputs, "section", -1)
-    reach, own_reach = reach_of(weights, inputs, gain, heads[-1][0])
+    reach, own_reach = reach_of(weights, inputs, gain, packs[-1])
     if count == 8:
         reaches = [own_reach, swapped(reach, "tp", SIDE)]
         reaches[1], next_input = lax.optimization_barrier((reaches[1], next_input))
     else:
         reaches = [lax.psum(own_reach, "tp")]
-    pair = value_gradients(taken, heads)
+    pair = value_gradients(taken, spares, packs, lambda: lax.axis_index("section") >= half)
     blocks, head_of = gathered(pair, "tp")
     soon, late = (blocks[:EARLY], blocks[EARLY:]) if count == 8 else ([], blocks)
     early = [project_early(head_of, soon, weights)] if soon else []

time: 27.8 us -> 27.4 us (0.986)
  starting transfers between devices: 16.7 us -> 16.4 us
    ppermute x0 -> x2, starting transfers between devices: none -> 2.36 us  [fetched(): return lax.ppermute(block, ('section', 'tp'), route)]
    ppermute x5 -> x3, starting transfers between devices: 5.9 us -> 4.39 us  [handed_over(): return lax.ppermute(block, ('section', 'tp'), route)]
    ppermute x5, starting transfers between devices: 7.61 us -> 6.14 us  [swapped(): lax.ppermute(block, axis, [(i ^ mask, i) for i in range(lax.axis_size(axi...]
    ppermute x2, starting transfers between devices: 3.19 us -> 3.5 us  [passed_along(): return lax.ppermute(block, axis, route)]
    ppermute x5 -> x3, waiting for transfers between devices: 2.17 us -> 2.26 us  [handed_over(): return lax.ppermute(block, ('section', 'tp'), route)]
  transfers between devices with their start and end apart: 12 -> 12, of which waited for: 6 -> 5; matrix products, arithmetic and copies ran while one was open for 0% -> 0% of each run, Pallas kernels for 6% -> 6%
where the time goes in v2:
time: 27.4 us; the launch traced here: 27.3 us
  starting transfers between devices  16.4 us (60%)
  waiting for transfers between devices  6.39 us (23%)
  Pallas kernels  4.41 us (16%)
    ppermute x5, starting transfers between devices, swapped(): lax.ppermute(block, axis, [(i ^ mask, i) for i in range(lax.axis_size(axi...  6.14 us
    ppermute x3, starting transfers between devices, handed_over(): return lax.ppermute(block, ('section', 'tp'), route)  4.39 us
    ppermute x5, waiting for transfers between devices, swapped(): lax.ppermute(block, axis, [(i ^ mask, i) for i in range(lax.axis_size(axi...  4.12 us
    ppermute x2, starting transfers between devices, passed_along(): return lax.ppermute(block, axis, route)  3.5 us
    ppermute x2, starting transfers between devices, fetched(): return lax.ppermute(block, ('section', 'tp'), route)  2.36 us
    ppermute x3, waiting for transfers between devices, handed_over(): return lax.ppermute(block, ('section', 'tp'), route)  2.26 us
    pallas_call x1, Pallas kernels, finish(): pl.pallas_call(finish_kernel, out_shape=pltpu.HBM(inputs.shape, jnp.bfloa...  1.06 us
    pallas_call x1, Pallas kernels, pack(): pl.pallas_call(pack_kernel, out_shape=(pltpu.VMEM((2, *own.shape), own.dt...  0.98 us
  transfers between devices with their start and end apart: 12, of which 5 were waited for; matrix products, arithmetic and copies ran while one was open for 0% of the time, Pallas kernels for 6%

profile of v2, /device:TPU:1, one launch (start us, length us, event | category | flops | bytes accessed | tf_op | source)
XLA Modules:
  0.0 27.3 jit_solution(3698367009484783854)
XLA Ops:
  0.0 0.0 copy-start.1
  0.0 0.0 copy-start
  0.0 0.0 copy-start.2
  0.0 1.0 %shard_map.73 = (bf16[2,128,128]{2,1,0:T(8,128)(2,1)S(1)}, bf16[128,128]{1,0:T(8,128)(2,1)S(1)}, bf16[128,128]{1,0:T(8,128)(2,1)S(1)}) custom-call(bf16[128,128]{1,0:T(8,128)(2,1)} %bitcast.12, bf16[128,128]{1,0:T(8,128)(2,1)} %bitcast.13, bf16[128,128]{1,0:T(8,128)(2,1)} %bitcast.14, s32[1,4]{1,0:T(1,128)} %evicted_ref.1), custom_call_target="tpu_custom_call" | custom-call | flops 34359738368 | bytes 33554432 | tf_op jit(solution)/shard_map/pallas_call | solution.py:87
  1.0 2.1 %collective-permute-start.2 = (bf16[2,128,128]{2,1,0:T(8,128)(2,1)S(1)}, bf16[2,128,128]{2,1,0:T(8,128)(2,1)S(1)}, u32[]{:S(2)}, u32[]{:S(2)}) collective-permute-start(bf16[2,128,128]{2,1,0:T(8,128)(2,1)S(1)} %get-tuple-element.19.refs_3_), channel_id=1, source_target_pairs={{1,0},{0,1},{3,2},{2,3},{5,4},{4,5},{7,6},{6,7},{9,8},{8,9},{11,10... | collective-permute-start | bytes 196616 | tf_op jit(solution)/shard_map/ppermute | solution.py:24
  3.1 1.2 %collective-permute-start = (bf16[128,128]{1,0:T(8,128)(2,1)S(1)}, bf16[128,128]{1,0:T(8,128)(2,1)S(1)}, u32[]{:S(2)}, u32[]{:S(2)}) collective-permute-start(bf16[128,128]{1,0:T(8,128)(2,1)S(1)} %get-tuple-element.18), channel_id=1, source_target_pairs={{17,0},{16,1},{19,2},{18,3},{21,4},{20,5},{23,6},{22,7},{25,8},{24... | collective-permute-start | bytes 98312 | tf_op jit(solution)/shard_map/ppermute | solution.py:364
  4.3 1.2 %collective-permute-start.1 = (bf16[128,128]{1,0:T(8,128)(2,1)S(1)}, bf16[128,128]{1,0:T(8,128)(2,1)S(1)}, u32[]{:S(2)}, u32[]{:S(2)}) collective-permute-start(bf16[128,128]{1,0:T(8,128)(2,1)S(1)} %get-tuple-element.18), channel_id=1, source_target_pairs={{16,0},{17,1},{18,2},{19,3},{20,4},{21,5},{22,6},{23,7},{24,8},{25... | collective-permute-start | bytes 98312 | tf_op jit(solution)/shard_map/ppermute | solution.py:364
  5.5 0.0 copy-done.1
  5.5 1.5 %collective-permute-start.7 = (bf16[128,1536]{1,0:T(8,128)(2,1)S(1)}, bf16[128,1536]{1,0:T(8,128)(2,1)S(1)}, u32[]{:S(2)}, u32[]{:S(2)}) collective-permute-start(bf16[128,1536]{1,0:T(8,128)(2,1)S(1)} %bitcast.9), channel_id=1, source_target_pairs={{8,0},{16,8},{24,16},{0,24},{9,1},{17,9},{25,17},{1,25},{10,2},{18... | collective-permute-start | bytes 1179656 | tf_op jit(solution)/shard_map/ppermute | solution.py:20
  7.0 0.0 collective-permute-done.2.refs_2_.first_ref
  7.0 0.0 copy-done
  7.0 0.0 copy-done.2
  7.0 0.6 %shard_map.75 = (bf16[144,1024]{1,0:T(8,128)(2,1)S(1)}, f32[144,1024]{1,0:T(8,128)S(1)}) custom-call(bf16[1536,1024]{1,0:T(8,128)(2,1)S(1)} %bitcast.6, bf16[128,1536]{1,0:T(8,128)(2,1)S(1)} %bitcast.10, f32[1,1536]{1,0:T(1,128)S(1)} %copy-done.2, bf16[2,128,128]{2,1,0:T(8,128)(2,1)S(1)} %collective-permute-done.2.refs_2_.first_ref), custom_call_target="tpu_custom_call" | custom-call | flops 34359738368 | bytes 33554432 | tf_op jit(solution)/shard_map/pallas_call | solution.py:120
  7.6 0.1 collective-permute-start.6
  7.7 0.0 collective-permute-done.refs_0_
  7.7 0.0 collective-permute-done.1.refs_1_
  7.7 0.2 shard_map.74.refs_0_
  8.0 3.6 %collective-permute-start.5 = (bf16[2,128,128]{2,1,0:T(8,128)(2,1)S(1)}, bf16[2,128,128]{2,1,0:T(8,128)(2,1)S(1)}, u32[]{:S(2)}, u32[]{:S(2)}) collective-permute-start(bf16[2,128,128]{2,1,0:T(8,128)(2,1)S(1)} %shard_map.74.refs_0_), channel_id=1, source_target_pairs={{6,0},{7,1},{4,2},{5,3},{2,4},{3,5},{0,6},{1,7},{14,8},{15,9},{12,... | collective-permute-start | bytes 196616 | tf_op jit(solution)/shard_map/ppermute | solution.py:24
  11.5 0.0 collective-permute-start.3
  11.5 0.4 %collective-permute-start.4 = (bf16[2,128,128]{2,1,0:T(8,128)(2,1)S(1)}, bf16[2,128,128]{2,1,0:T(8,128)(2,1)S(1)}, u32[]{:S(2)}, u32[]{:S(2)}) collective-permute-start(bf16[2,128,128]{2,1,0:T(8,128)(2,1)S(1)} %shard_map.74.refs_0_), channel_id=1, source_target_pairs={{2,0},{3,1},{0,2},{1,3},{6,4},{7,5},{4,6},{5,7},{10,8},{11,9},{8,1... | collective-permute-start | bytes 196616 | tf_op jit(solution)/shard_map/ppermute | solution.py:24
  11.9 1.3 %collective-permute-done.5.refs_1_ = bf16[2,128,128]{2,1,0:T(8,128)(2,1)S(1)} collective-permute-done((bf16[2,128,128]{2,1,0:T(8,128)(2,1)S(1)}, bf16[2,128,128]{2,1,0:T(8,128)(2,1)S(1)}, u32[]{:S(2)}, u32[]{:S(2)}) %collective-permute-start.5) | collective-permute-done | bytes 65568 | tf_op jit(solution)/shard_map/ppermute | solution.py:24
  13.2 0.7 %shard_map.77.refs_8_ = f32[128,1536]{1,0:T(8,128)S(1)} custom-call(bf16[2,128,128]{2,1,0:T(8,128)(2,1)S(1)} %shard_map.74.refs_0_, bf16[2,128,128]{2,1,0:T(8,128)(2,1)S(1)} %collective-permute-done.5.refs_1_, bf16[1536,1024]{1,0:T(8,128)(2,1)S(1)} %bitcast.7), custom_call_target="tpu_custom_call" | custom-call | flops 65536 | bytes 4096 | tf_op jit(solution)/shard_map/pallas_call | solution.py:204
  13.9 2.5 %collective-permute-done.6.refs_3_ = bf16[144,1024]{1,0:T(8,128)(2,1)S(1)} collective-permute-done((bf16[144,1024]{1,0:T(8,128)(2,1)S(1)}, bf16[144,1024]{1,0:T(8,128)(2,1)S(1)}, u32[]{:S(2)}, u32[]{:S(2)}) %collective-permute-start.6) | collective-permute-done | bytes 294944 | tf_op jit(solution)/shard_map/ppermute | solution.py:24
  16.3 0.0 collective-permute-done.7.input_ref
  16.3 0.1 shard_map.76
  16.4 0.4 %collective-permute-done.3.refs_0_ = bf16[2,128,128]{2,1,0:T(8,128)(2,1)S(1)} collective-permute-done((bf16[2,128,128]{2,1,0:T(8,128)(2,1)S(1)}, bf16[2,128,128]{2,1,0:T(8,128)(2,1)S(1)}, u32[]{:S(2)}, u32[]{:S(2)}) %collective-permute-start.3) | collective-permute-done | bytes 65568 | tf_op jit(solution)/shard_map/ppermute | solution.py:24
  16.8 0.0 collective-permute-done.4.refs_1_
  16.8 0.8 %shard_map.78 = (bf16[128,1664]{1,0:T(8,128)(2,1)S(1)}, f32[2,128]{1,0:T(2,128)S(1)}) custom-call(bf16[2,128,128]{2,1,0:T(8,128)(2,1)S(1)} %collective-permute-done.3.refs_0_, bf16[2,128,128]{2,1,0:T(8,128)(2,1)S(1)} %collective-permute-done.4.refs_1_, f32[128,1024]{1,0:T(8,128)S(1)} %get-tuple-element.23.refs_2_, f32[128,128]{1,0:T(8,128)S(1)} %get-tuple-element.24.refs_3_, ...), custom_call_target="tpu_custom_call" | custom-call | flops 34359738368 | bytes 33554432 | tf_op jit(solution)/shard_map/pallas_call | solution.py:287
  17.6 2.0 %collective-permute-start.8 = (bf16[128,1664]{1,0:T(8,128)(2,1)S(1)}, bf16[128,1664]{1,0:T(8,128)(2,1)S(1)}, u32[]{:S(2)}, u32[]{:S(2)}) collective-permute-start(bf16[128,1664]{1,0:T(8,128)(2,1)S(1)} %get-tuple-element.26), channel_id=1, source_target_pairs={{8,0},{16,8},{24,16},{0,24},{9,1},{17,9},{25,17},{1,25},{10,2},{18... | collective-permute-start | bytes 1277960 | tf_op jit(solution)/shard_map/ppermute | solution.py:20
  19.6 1.9 %collective-permute-start.10 = (f32[2,128]{1,0:T(2,128)S(1)}, f32[2,128]{1,0:T(2,128)S(1)}, u32[]{:S(2)}, u32[]{:S(2)}) collective-permute-start(f32[2,128]{1,0:T(2,128)S(1)} %get-tuple-element.28), channel_id=1, source_target_pairs={{14,0},{15,1},{12,2},{13,3},{10,4},{11,5},{8,6},{9,7},{22,8},{23,9... | collective-permute-start | bytes 3080 | tf_op jit(solution)/shard_map/ppermute | solution.py:354
  21.4 0.4 %collective-permute-start.11 = (f32[2,128]{1,0:T(2,128)S(1)}, f32[2,128]{1,0:T(2,128)S(1)}, u32[]{:S(2)}, u32[]{:S(2)}) collective-permute-start(f32[2,128]{1,0:T(2,128)S(1)} %get-tuple-element.28), channel_id=1, source_target_pairs={{12,0},{13,1},{14,2},{15,3},{8,4},{9,5},{10,6},{11,7},{20,8},{21,9... | collective-permute-start | bytes 3080 | tf_op jit(solution)/shard_map/ppermute | solution.py:354
  21.8 2.1 %collective-permute-start.9 = (f32[2,128]{1,0:T(2,128)S(1)}, f32[2,128]{1,0:T(2,128)S(1)}, u32[]{:S(2)}, u32[]{:S(2)}) collective-permute-start(f32[2,128]{1,0:T(2,128)S(1)} %get-tuple-element.28), channel_id=1, source_target_pairs={{10,0},{11,1},{8,2},{9,3},{14,4},{15,5},{12,6},{13,7},{18,8},{19,9... | collective-permute-start | bytes 3080 | tf_op jit(solution)/shard_map/ppermute | solution.py:354
  24.0 1.3 %collective-permute-done.10.refs_1_ = f32[2,128]{1,0:T(2,128)S(1)} collective-permute-done((f32[2,128]{1,0:T(2,128)S(1)}, f32[2,128]{1,0:T(2,128)S(1)}, u32[]{:S(2)}, u32[]{:S(2)}) %collective-permute-start.10) | collective-permute-done | bytes 1056 | tf_op jit(solution)/shard_map/ppermute | solution.py:354
  25.3 1.0 %collective-permute-done.11.refs_2_ = f32[2,128]{1,0:T(2,128)S(1)} collective-permute-done((f32[2,128]{1,0:T(2,128)S(1)}, f32[2,128]{1,0:T(2,128)S(1)}, u32[]{:S(2)}, u32[]{:S(2)}) %collective-permute-start.11) | collective-permute-done | bytes 1056 | tf_op jit(solution)/shard_map/ppermute | solution.py:354
  26.2 0.0 collective-permute-done.9.refs_0_
  26.2 0.0 collective-permute-done.8.scaled_ref
  26.2 1.1 %shard_map.79 = bf16[128,1536]{1,0:T(8,128)(2,1)} custom-call(bf16[128,1664]{1,0:T(8,128)(2,1)S(1)} %collective-permute-done.8.scaled_ref, bf16[128,1536]{1,0:T(8,128)(2,1)S(1)} %collective-permute-done.7.input_ref, f32[2,128]{1,0:T(2,128)S(1)} %collective-permute-done.9.refs_0_, f32[2,128]{1,0:T(2,128)S(1)} %collective-permute-done.10.refs_1_, ...), custom_call_target="tpu_custom_call" | custom-call | tf_op jit(solution)/shard_map/pallas_call | solution.py:329
Async XLA Ops:
  0.0 5.5 %copy-start.1 = (bf16[1,128,1536]{2,1,0:T(8,128)(2,1)S(1)}, bf16[1,128,1536]{2,1,0:T(8,128)(2,1)}, u32[]{:S(2)}) copy-start(bf16[1,128,1536]{2,1,0:T(8,128)(2,1)} %param.12) | copy-start | bytes 1179652
  0.0 7.0 %copy-start = (bf16[1,1536,1024]{2,1,0:T(8,128)(2,1)S(1)}, bf16[1,1536,1024]{2,1,0:T(8,128)(2,1)}, u32[]{:S(2)}) copy-start(bf16[1,1536,1024]{2,1,0:T(8,128)(2,1)} %param.8) | copy-start | bytes 9437188
  0.0 7.0 %copy-start.2 = (f32[1,1536]{1,0:T(1,128)S(1)}, f32[1,1536]{1,0:T(1,128)}, u32[]{:S(2)}) copy-start(f32[1,1536]{1,0:T(1,128)} %refs_7_.1) | copy-start | bytes 18436
  1.0 6.0 %collective-permute-start.2 = (bf16[2,128,128]{2,1,0:T(8,128)(2,1)S(1)}, bf16[2,128,128]{2,1,0:T(8,128)(2,1)S(1)}, u32[]{:S(2)}, u32[]{:S(2)}) collective-permute-start(bf16[2,128,128]{2,1,0:T(8,128)(2,1)S(1)} %get-tuple-element.19.refs_3_), channel_id=1, source_target_pairs={{1,0},{0,1},{3,2},{2,3},{5,4},{4,5},{7,6},{6,7},{9,8},{8,9},{11,10... | collective-permute-start | bytes 196616 | tf_op jit(solution)/shard_map/ppermute | solution.py:24
  3.1 4.6 %collective-permute-start = (bf16[128,128]{1,0:T(8,128)(2,1)S(1)}, bf16[128,128]{1,0:T(8,128)(2,1)S(1)}, u32[]{:S(2)}, u32[]{:S(2)}) collective-permute-start(bf16[128,128]{1,0:T(8,128)(2,1)S(1)} %get-tuple-element.18), channel_id=1, source_target_pairs={{17,0},{16,1},{19,2},{18,3},{21,4},{20,5},{23,6},{22,7},{25,8},{24... | collective-permute-start | bytes 98312 | tf_op jit(solution)/shard_map/ppermute | solution.py:364
  4.3 3.4 %collective-permute-start.1 = (bf16[128,128]{1,0:T(8,128)(2,1)S(1)}, bf16[128,128]{1,0:T(8,128)(2,1)S(1)}, u32[]{:S(2)}, u32[]{:S(2)}) collective-permute-start(bf16[128,128]{1,0:T(8,128)(2,1)S(1)} %get-tuple-element.18), channel_id=1, source_target_pairs={{16,0},{17,1},{18,2},{19,3},{20,4},{21,5},{22,6},{23,7},{24,8},{25... | collective-permute-start | bytes 98312 | tf_op jit(solution)/shard_map/ppermute | solution.py:364
  5.5 10.8 %collective-permute-start.7 = (bf16[128,1536]{1,0:T(8,128)(2,1)S(1)}, bf16[128,1536]{1,0:T(8,128)(2,1)S(1)}, u32[]{:S(2)}, u32[]{:S(2)}) collective-permute-start(bf16[128,1536]{1,0:T(8,128)(2,1)S(1)} %bitcast.9), channel_id=1, source_target_pairs={{8,0},{16,8},{24,16},{0,24},{9,1},{17,9},{25,17},{1,25},{10,2},{18... | collective-permute-start | bytes 1179656 | tf_op jit(solution)/shard_map/ppermute | solution.py:20
  7.6 8.7 %collective-permute-start.6 = (bf16[144,1024]{1,0:T(8,128)(2,1)S(1)}, bf16[144,1024]{1,0:T(8,128)(2,1)S(1)}, u32[]{:S(2)}, u32[]{:S(2)}) collective-permute-start(bf16[144,1024]{1,0:T(8,128)(2,1)S(1)} %get-tuple-element.21), channel_id=1, source_target_pairs={{1,0},{0,1},{3,2},{2,3},{5,4},{4,5},{7,6},{6,7},{9,8},{8,9},{11,10... | collective-permute-start | bytes 884744 | tf_op jit(solution)/shard_map/ppermute | solution.py:24
  8.0 5.2 %collective-permute-start.5 = (bf16[2,128,128]{2,1,0:T(8,128)(2,1)S(1)}, bf16[2,128,128]{2,1,0:T(8,128)(2,1)S(1)}, u32[]{:S(2)}, u32[]{:S(2)}) collective-permute-start(bf16[2,128,128]{2,1,0:T(8,128)(2,1)S(1)} %shard_map.74.refs_0_), channel_id=1, source_target_pairs={{6,0},{7,1},{4,2},{5,3},{2,4},{3,5},{0,6},{1,7},{14,8},{15,9},{12,... | collective-permute-start | bytes 196616 | tf_op jit(solution)/shard_map/ppermute | solution.py:24
  11.5 5.3 %collective-permute-start.3 = (bf16[2,128,128]{2,1,0:T(8,128)(2,1)S(1)}, bf16[2,128,128]{2,1,0:T(8,128)(2,1)S(1)}, u32[]{:S(2)}, u32[]{:S(2)}) collective-permute-start(bf16[2,128,128]{2,1,0:T(8,128)(2,1)S(1)} %shard_map.74.refs_0_), channel_id=1, source_target_pairs={{4,0},{5,1},{6,2},{7,3},{0,4},{1,5},{2,6},{3,7},{12,8},{13,9},{14,... | collective-permute-start | bytes 196616 | tf_op jit(solution)/shard_map/ppermute | solution.py:24
  11.5 5.3 %collective-permute-start.4 = (bf16[2,128,128]{2,1,0:T(8,128)(2,1)S(1)}, bf16[2,128,128]{2,1,0:T(8,128)(2,1)S(1)}, u32[]{:S(2)}, u32[]{:S(2)}) collective-permute-start(bf16[2,128,128]{2,1,0:T(8,128)(2,1)S(1)} %shard_map.74.refs_0_), channel_id=1, source_target_pairs={{2,0},{3,1},{0,2},{1,3},{6,4},{7,5},{4,6},{5,7},{10,8},{11,9},{8,1... | collective-permute-start | bytes 196616 | tf_op jit(solution)/shard_map/ppermute | solution.py:24
  17.6 8.7 %collective-permute-start.8 = (bf16[128,1664]{1,0:T(8,128)(2,1)S(1)}, bf16[128,1664]{1,0:T(8,128)(2,1)S(1)}, u32[]{:S(2)}, u32[]{:S(2)}) collective-permute-start(bf16[128,1664]{1,0:T(8,128)(2,1)S(1)} %get-tuple-element.26), channel_id=1, source_target_pairs={{8,0},{16,8},{24,16},{0,24},{9,1},{17,9},{25,17},{1,25},{10,2},{18... | collective-permute-start | bytes 1277960 | tf_op jit(solution)/shard_map/ppermute | solution.py:20
  19.6 5.7 %collective-permute-start.10 = (f32[2,128]{1,0:T(2,128)S(1)}, f32[2,128]{1,0:T(2,128)S(1)}, u32[]{:S(2)}, u32[]{:S(2)}) collective-permute-start(f32[2,128]{1,0:T(2,128)S(1)} %get-tuple-element.28), channel_id=1, source_target_pairs={{14,0},{15,1},{12,2},{13,3},{10,4},{11,5},{8,6},{9,7},{22,8},{23,9... | collective-permute-start | bytes 3080 | tf_op jit(solution)/shard_map/ppermute | solution.py:354
  21.4 4.8 %collective-permute-start.11 = (f32[2,128]{1,0:T(2,128)S(1)}, f32[2,128]{1,0:T(2,128)S(1)}, u32[]{:S(2)}, u32[]{:S(2)}) collective-permute-start(f32[2,128]{1,0:T(2,128)S(1)} %get-tuple-element.28), channel_id=1, source_target_pairs={{12,0},{13,1},{14,2},{15,3},{8,4},{9,5},{10,6},{11,7},{20,8},{21,9... | collective-permute-start | bytes 3080 | tf_op jit(solution)/shard_map/ppermute | solution.py:354
  21.8 4.4 %collective-permute-start.9 = (f32[2,128]{1,0:T(2,128)S(1)}, f32[2,128]{1,0:T(2,128)S(1)}, u32[]{:S(2)}, u32[]{:S(2)}) collective-permute-start(f32[2,128]{1,0:T(2,128)S(1)} %get-tuple-element.28), channel_id=1, source_target_pairs={{10,0},{11,1},{8,2},{9,3},{14,4},{15,5},{12,6},{13,7},{18,8},{19,9... | collective-permute-start | bytes 3080 | tf_op jit(solution)/shard_map/ppermute | solution.py:354

commit v3 on v2

--- a/solution.py
+++ b/solution.py
@@ -11,6 +11,7 @@
 LANES = 128
 PIECES = (0, 3, 5, 7, 8)
 EXTRA = 16
+SHORT = pl.CostEstimate(flops=1 << 16, bytes_accessed=1 << 12, transcendentals=0)
 HIDES = pl.CostEstimate(flops=1 << 35, bytes_accessed=1 << 25, transcendentals=0)
 
 
@@ -102,8 +103,7 @@
     )(*map(in_hbm, (own, grad, spare, evicted)))
 
 
-def reach_kernel(weight_ref, input_ref, gain_ref, first_ref, reach_ref, own_ref):
-    del first_ref
+def reach_kernel(weight_ref, input_ref, gain_ref, reach_ref, own_ref):
     tokens, features = input_ref.shape
     values = input_ref[...].astype(jnp.float32)
     reach_ref[tokens:, :] = jnp.zeros_like(reach_ref[tokens:, :])
@@ -116,25 +116,25 @@
     own_ref[tokens:, :] = reach_ref[tokens:, :].astype(own_ref.dtype)
 
 
-def reach_of(weights, inputs, gain, first):
+def reach_of(weights, inputs, gain):
     return pl.pallas_call(
         reach_kernel,
         out_shape=tuple(
             pltpu.VMEM((inputs.shape[0] + EXTRA, weights.shape[1]), dtype)
             for dtype in (jnp.bfloat16, jnp.float32)
         ),
-        in_specs=vmem_specs(4),
+        in_specs=vmem_specs(3),
         out_specs=tuple(vmem_specs(2)),
-        cost_estimate=HIDES,
+        cost_estimate=SHORT,
         compiler_params=pltpu.CompilerParams(vmem_limit_bytes=8 << 20),
-    )(*map(in_vmem, (weights, inputs, gain, first)))
+    )(*map(in_vmem, (weights, inputs, gain)))
 
 
 def mix_kernel(upper, taken_ref, *refs):
     out_ref = refs[-1]
     taken = taken_ref[...]
     count = out_ref.shape[0]
-    spares = [refs[count - 1 - j][...] for j in range(count)]
+    spares = [refs[j][...] for j in range(count)]
     if count == 2:
         swap = upper()
         spares = [jnp.where(swap, spares[1], spares[0]), jnp.where(swap, spares[0], spares[1])]
@@ -156,7 +156,7 @@
         out_specs=pl.BlockSpec(memory_space=pltpu.VMEM),
         cost_estimate=HIDES,
         compiler_params=pltpu.CompilerParams(vmem_limit_bytes=4 << 20),
-    )(*map(in_vmem, (taken, *spares[::-1], *packs[::-1])))
+    )(*map(in_vmem, (taken, *spares, *packs[::-1])))
 
 
 def column_tile(features):
@@ -207,7 +207,7 @@
         in_specs=vmem_specs(len(blocks) + 1),
         out_specs=pl.BlockSpec(memory_space=pltpu.VMEM),
         scratch_shapes=[pltpu.VMEM((tokens, weights.shape[1]), jnp.bfloat16)],
-        cost_estimate=pl.CostEstimate(flops=1 << 16, bytes_accessed=1 << 12, transcendentals=0),
+        cost_estimate=SHORT,
         compiler_params=pltpu.CompilerParams(vmem_limit_bytes=16 << 20),
     )(*map(in_vmem, (*blocks, weights)))
 
@@ -248,7 +248,7 @@
         ),
         in_specs=vmem_specs(len(operands)),
         out_specs=tuple(vmem_specs(3)),
-        cost_estimate=pl.CostEstimate(flops=1 << 16, bytes_accessed=1 << 12, transcendentals=0),
+        cost_estimate=SHORT,
         compiler_params=pltpu.CompilerParams(vmem_limit_bytes=8 << 20),
     )(*map(in_vmem, operands))
 
@@ -341,7 +341,7 @@
 
 FAR, NEAR, SIDE = 4, 2, 1
 ORDER = ((0, SIDE), (SIDE, 0))
-LINE = (FAR | NEAR, FAR, NEAR)
+LINE = (FAR | NEAR, NEAR, FAR)
 EARLY = 2
 
 
@@ -384,8 +384,9 @@
     spares = [fetched(spares, sections, count, masks) for masks in ORDER[: len(packs)]]
     weights, inputs = w_value[0], layer_input[0]
     next_input = passed_along(inputs, "section", -1)
-    reach, own_reach = reach_of(weights, inputs, gain, packs[-1])
+    reach, own_reach = reach_of(weights, inputs, gain)
     if count == 8:
+        reach, packs[1] = lax.optimization_barrier((reach, packs[1]))
         reaches = [own_reach, swapped(reach, "tp", SIDE)]
         reaches[1], next_input = lax.optimization_barrier((reaches[1], next_input))
     else:
@@ -399,7 +400,7 @@
     scaled, sums = project(head_of, first, late, joined, weights, inputs, gain, early)
     next_scaled = passed_along(scaled, "section", -1)
     next_sums = []
-    for mask in (NEAR, FAR | NEAR, FAR) if count == 8 else ():
+    for mask in (NEAR, FAR, FAR | NEAR) if count == 8 else ():
         next_sums.append(handed_over(sums, sections, count, -1, mask))
     return finish(next_scaled, next_input, next_sums)[None]
 

time: 27.4 us -> 27.4 us (level)
  no operation moved by 1% of the time
where the time goes in v3:
time: 27.4 us; the launch traced here: 27.3 us
  starting transfers between devices  16.4 us (60%)
  waiting for transfers between devices  6.38 us (23%)
  Pallas kernels  4.41 us (16%)
    ppermute x5, starting transfers between devices, swapped(): lax.ppermute(block, axis, [(i ^ mask, i) for i in range(lax.axis_size(axi...  6.15 us
    ppermute x3, starting transfers between devices, handed_over(): return lax.ppermute(block, ('section', 'tp'), route)  4.39 us
    ppermute x5, waiting for transfers between devices, swapped(): lax.ppermute(block, axis, [(i ^ mask, i) for i in range(lax.axis_size(axi...  4.11 us
    ppermute x2, starting transfers between devices, passed_along(): return lax.ppermute(block, axis, route)  3.5 us
    ppermute x2, starting transfers between devices, fetched(): return lax.ppermute(block, ('section', 'tp'), route)  2.36 us
    ppermute x3, waiting for transfers between devices, handed_over(): return lax.ppermute(block, ('section', 'tp'), route)  2.26 us
    pallas_call x1, Pallas kernels, finish(): pl.pallas_call(finish_kernel, out_shape=pltpu.HBM(inputs.shape, jnp.bfloa...  1.06 us
    pallas_call x1, Pallas kernels, pack(): pl.pallas_call(pack_kernel, out_shape=(pltpu.VMEM((2, *own.shape), own.dt...  0.98 us
  transfers between devices with their start and end apart: 12, of which 5 were waited for; matrix products, arithmetic and copies ran while one was open for 0% of the time, Pallas kernels for 6%

profile of v3, /device:TPU:1, one launch (start us, length us, event | category | flops | bytes accessed | tf_op | source)
XLA Modules:
  0.0 27.3 jit_solution(149942174860889267)
XLA Ops:
  0.0 0.0 copy-start.1
  0.0 0.0 copy-start
  0.0 0.0 copy-start.2
  0.0 1.0 %shard_map.73 = (bf16[2,128,128]{2,1,0:T(8,128)(2,1)S(1)}, bf16[128,128]{1,0:T(8,128)(2,1)S(1)}, bf16[128,128]{1,0:T(8,128)(2,1)S(1)}) custom-call(bf16[128,128]{1,0:T(8,128)(2,1)} %bitcast.12, bf16[128,128]{1,0:T(8,128)(2,1)} %bitcast.13, bf16[128,128]{1,0:T(8,128)(2,1)} %bitcast.14, s32[1,4]{1,0:T(1,128)} %evicted_ref.1), custom_call_target="tpu_custom_call" | custom-call | flops 34359738368 | bytes 33554432 | tf_op jit(solution)/shard_map/pallas_call | solution.py:88
  1.0 2.1 %collective-permute-start.2 = (bf16[2,128,128]{2,1,0:T(8,128)(2,1)S(1)}, bf16[2,128,128]{2,1,0:T(8,128)(2,1)S(1)}, u32[]{:S(2)}, u32[]{:S(2)}) collective-permute-start(bf16[2,128,128]{2,1,0:T(8,128)(2,1)S(1)} %get-tuple-element.22.refs_3_), channel_id=1, source_target_pairs={{1,0},{0,1},{3,2},{2,3},{5,4},{4,5},{7,6},{6,7},{9,8},{8,9},{11,10... | collective-permute-start | bytes 196616 | tf_op jit(solution)/shard_map/ppermute | solution.py:25
  3.1 1.2 %collective-permute-start.1 = (bf16[128,128]{1,0:T(8,128)(2,1)S(1)}, bf16[128,128]{1,0:T(8,128)(2,1)S(1)}, u32[]{:S(2)}, u32[]{:S(2)}) collective-permute-start(bf16[128,128]{1,0:T(8,128)(2,1)S(1)} %get-tuple-element.20), channel_id=1, source_target_pairs={{17,0},{16,1},{19,2},{18,3},{21,4},{20,5},{23,6},{22,7},{25,8},{24... | collective-permute-start | bytes 98312 | tf_op jit(solution)/shard_map/ppermute | solution.py:364
  4.3 1.2 %collective-permute-start = (bf16[128,128]{1,0:T(8,128)(2,1)S(1)}, bf16[128,128]{1,0:T(8,128)(2,1)S(1)}, u32[]{:S(2)}, u32[]{:S(2)}) collective-permute-start(bf16[128,128]{1,0:T(8,128)(2,1)S(1)} %get-tuple-element.20), channel_id=1, source_target_pairs={{16,0},{17,1},{18,2},{19,3},{20,4},{21,5},{22,6},{23,7},{24,8},{25... | collective-permute-start | bytes 98312 | tf_op jit(solution)/shard_map/ppermute | solution.py:364
  5.5 0.0 copy-done.1
  5.5 1.5 %collective-permute-start.7 = (bf16[128,1536]{1,0:T(8,128)(2,1)S(1)}, bf16[128,1536]{1,0:T(8,128)(2,1)S(1)}, u32[]{:S(2)}, u32[]{:S(2)}) collective-permute-start(bf16[128,1536]{1,0:T(8,128)(2,1)S(1)} %bitcast.9), channel_id=1, source_target_pairs={{8,0},{16,8},{24,16},{0,24},{9,1},{17,9},{25,17},{1,25},{10,2},{18... | collective-permute-start | bytes 1179656 | tf_op jit(solution)/shard_map/ppermute | solution.py:21
  7.0 0.0 copy-done
  7.0 0.0 copy-done.2
  7.0 0.6 %shard_map.74 = (bf16[144,1024]{1,0:T(8,128)(2,1)S(1)}, f32[144,1024]{1,0:T(8,128)S(1)}) custom-call(bf16[1536,1024]{1,0:T(8,128)(2,1)S(1)} %bitcast.6, bf16[128,1536]{1,0:T(8,128)(2,1)S(1)} %bitcast.10, f32[1,1536]{1,0:T(1,128)S(1)} %copy-done.2), custom_call_target="tpu_custom_call" | custom-call | flops 65536 | bytes 4096 | tf_op jit(solution)/shard_map/pallas_call | solution.py:120
  7.6 0.0 collective-permute-done.2.refs_2_
  7.6 0.1 collective-permute-start.6
  7.7 0.0 collective-permute-done.1.refs_1_
  7.7 0.0 collective-permute-done.refs_0_
  7.7 0.2 shard_map.75.refs_0_
  8.0 3.6 %collective-permute-start.5 = (bf16[2,128,128]{2,1,0:T(8,128)(2,1)S(1)}, bf16[2,128,128]{2,1,0:T(8,128)(2,1)S(1)}, u32[]{:S(2)}, u32[]{:S(2)}) collective-permute-start(bf16[2,128,128]{2,1,0:T(8,128)(2,1)S(1)} %shard_map.75.refs_0_), channel_id=1, source_target_pairs={{6,0},{7,1},{4,2},{5,3},{2,4},{3,5},{0,6},{1,7},{14,8},{15,9},{12,... | collective-permute-start | bytes 196616 | tf_op jit(solution)/shard_map/ppermute | solution.py:25
  11.5 0.0 collective-permute-start.4
  11.5 0.4 %collective-permute-start.3 = (bf16[2,128,128]{2,1,0:T(8,128)(2,1)S(1)}, bf16[2,128,128]{2,1,0:T(8,128)(2,1)S(1)}, u32[]{:S(2)}, u32[]{:S(2)}) collective-permute-start(bf16[2,128,128]{2,1,0:T(8,128)(2,1)S(1)} %shard_map.75.refs_0_), channel_id=1, source_target_pairs={{2,0},{3,1},{0,2},{1,3},{6,4},{7,5},{4,6},{5,7},{10,8},{11,9},{8,1... | collective-permute-start | bytes 196616 | tf_op jit(solution)/shard_map/ppermute | solution.py:25
  11.9 1.3 %collective-permute-done.5.refs_1_ = bf16[2,128,128]{2,1,0:T(8,128)(2,1)S(1)} collective-permute-done((bf16[2,128,128]{2,1,0:T(8,128)(2,1)S(1)}, bf16[2,128,128]{2,1,0:T(8,128)(2,1)S(1)}, u32[]{:S(2)}, u32[]{:S(2)}) %collective-permute-start.5) | collective-permute-done | bytes 65568 | tf_op jit(solution)/shard_map/ppermute | solution.py:25
  13.2 0.7 %shard_map.77.refs_8_ = f32[128,1536]{1,0:T(8,128)S(1)} custom-call(bf16[2,128,128]{2,1,0:T(8,128)(2,1)S(1)} %shard_map.75.refs_0_, bf16[2,128,128]{2,1,0:T(8,128)(2,1)S(1)} %collective-permute-done.5.refs_1_, bf16[1536,1024]{1,0:T(8,128)(2,1)S(1)} %bitcast.7), custom_call_target="tpu_custom_call" | custom-call | flops 65536 | bytes 4096 | tf_op jit(solution)/shard_map/pallas_call | solution.py:204
  13.9 2.5 %collective-permute-done.6.refs_3_ = bf16[144,1024]{1,0:T(8,128)(2,1)S(1)} collective-permute-done((bf16[144,1024]{1,0:T(8,128)(2,1)S(1)}, bf16[144,1024]{1,0:T(8,128)(2,1)S(1)}, u32[]{:S(2)}, u32[]{:S(2)}) %collective-permute-start.6) | collective-permute-done | bytes 294944 | tf_op jit(solution)/shard_map/ppermute | solution.py:25
  16.3 0.0 collective-permute-done.7.input_ref
  16.3 0.1 shard_map.76
  16.4 0.3 %collective-permute-done.4.refs_1_ = bf16[2,128,128]{2,1,0:T(8,128)(2,1)S(1)} collective-permute-done((bf16[2,128,128]{2,1,0:T(8,128)(2,1)S(1)}, bf16[2,128,128]{2,1,0:T(8,128)(2,1)S(1)}, u32[]{:S(2)}, u32[]{:S(2)}) %collective-permute-start.4) | collective-permute-done | bytes 65568 | tf_op jit(solution)/shard_map/ppermute | solution.py:25
  16.8 0.0 collective-permute-done.3.refs_0_
  16.8 0.8 %shard_map.78 = (bf16[128,1664]{1,0:T(8,128)(2,1)S(1)}, f32[2,128]{1,0:T(2,128)S(1)}) custom-call(bf16[2,128,128]{2,1,0:T(8,128)(2,1)S(1)} %collective-permute-done.3.refs_0_, bf16[2,128,128]{2,1,0:T(8,128)(2,1)S(1)} %collective-permute-done.4.refs_1_, f32[128,1024]{1,0:T(8,128)S(1)} %get-tuple-element.27.refs_2_, f32[128,128]{1,0:T(8,128)S(1)} %get-tuple-element.28.refs_3_, ...), custom_call_target="tpu_custom_call" | custom-call | flops 34359738368 | bytes 33554432 | tf_op jit(solution)/shard_map/pallas_call | solution.py:287
  17.6 2.0 %collective-permute-start.8 = (bf16[128,1664]{1,0:T(8,128)(2,1)S(1)}, bf16[128,1664]{1,0:T(8,128)(2,1)S(1)}, u32[]{:S(2)}, u32[]{:S(2)}) collective-permute-start(bf16[128,1664]{1,0:T(8,128)(2,1)S(1)} %get-tuple-element.30), channel_id=1, source_target_pairs={{8,0},{16,8},{24,16},{0,24},{9,1},{17,9},{25,17},{1,25},{10,2},{18... | collective-permute-start | bytes 1277960 | tf_op jit(solution)/shard_map/ppermute | solution.py:21
  19.6 1.9 %collective-permute-start.11 = (f32[2,128]{1,0:T(2,128)S(1)}, f32[2,128]{1,0:T(2,128)S(1)}, u32[]{:S(2)}, u32[]{:S(2)}) collective-permute-start(f32[2,128]{1,0:T(2,128)S(1)} %get-tuple-element.32), channel_id=1, source_target_pairs={{14,0},{15,1},{12,2},{13,3},{10,4},{11,5},{8,6},{9,7},{22,8},{23,9... | collective-permute-start | bytes 3080 | tf_op jit(solution)/shard_map/ppermute | solution.py:354
  21.4 0.4 %collective-permute-start.10 = (f32[2,128]{1,0:T(2,128)S(1)}, f32[2,128]{1,0:T(2,128)S(1)}, u32[]{:S(2)}, u32[]{:S(2)}) collective-permute-start(f32[2,128]{1,0:T(2,128)S(1)} %get-tuple-element.32), channel_id=1, source_target_pairs={{12,0},{13,1},{14,2},{15,3},{8,4},{9,5},{10,6},{11,7},{20,8},{21,9... | collective-permute-start | bytes 3080 | tf_op jit(solution)/shard_map/ppermute | solution.py:354
  21.8 2.1 %collective-permute-start.9 = (f32[2,128]{1,0:T(2,128)S(1)}, f32[2,128]{1,0:T(2,128)S(1)}, u32[]{:S(2)}, u32[]{:S(2)}) collective-permute-start(f32[2,128]{1,0:T(2,128)S(1)} %get-tuple-element.32), channel_id=1, source_target_pairs={{10,0},{11,1},{8,2},{9,3},{14,4},{15,5},{12,6},{13,7},{18,8},{19,9... | collective-permute-start | bytes 3080 | tf_op jit(solution)/shard_map/ppermute | solution.py:354
  24.0 1.3 %collective-permute-done.11.refs_2_ = f32[2,128]{1,0:T(2,128)S(1)} collective-permute-done((f32[2,128]{1,0:T(2,128)S(1)}, f32[2,128]{1,0:T(2,128)S(1)}, u32[]{:S(2)}, u32[]{:S(2)}) %collective-permute-start.11) | collective-permute-done | bytes 1056 | tf_op jit(solution)/shard_map/ppermute | solution.py:354
  25.3 1.0 %collective-permute-done.10.refs_1_ = f32[2,128]{1,0:T(2,128)S(1)} collective-permute-done((f32[2,128]{1,0:T(2,128)S(1)}, f32[2,128]{1,0:T(2,128)S(1)}, u32[]{:S(2)}, u32[]{:S(2)}) %collective-permute-start.10) | collective-permute-done | bytes 1056 | tf_op jit(solution)/shard_map/ppermute | solution.py:354
  26.2 0.0 collective-permute-done.9.refs_0_
  26.2 0.0 collective-permute-done.8.scaled_ref
  26.2 1.1 %shard_map.79 = bf16[128,1536]{1,0:T(8,128)(2,1)} custom-call(bf16[128,1664]{1,0:T(8,128)(2,1)S(1)} %collective-permute-done.8.scaled_ref, bf16[128,1536]{1,0:T(8,128)(2,1)S(1)} %collective-permute-done.7.input_ref, f32[2,128]{1,0:T(2,128)S(1)} %collective-permute-done.9.refs_0_, f32[2,128]{1,0:T(2,128)S(1)} %collective-permute-done.10.refs_1_, ...), custom_call_target="tpu_custom_call" | custom-call | tf_op jit(solution)/shard_map/pallas_call | solution.py:329
Async XLA Ops:
  0.0 5.5 %copy-start.1 = (bf16[1,128,1536]{2,1,0:T(8,128)(2,1)S(1)}, bf16[1,128,1536]{2,1,0:T(8,128)(2,1)}, u32[]{:S(2)}) copy-start(bf16[1,128,1536]{2,1,0:T(8,128)(2,1)} %param.12) | copy-start | bytes 1179652
  0.0 7.0 %copy-start = (bf16[1,1536,1024]{2,1,0:T(8,128)(2,1)S(1)}, bf16[1,1536,1024]{2,1,0:T(8,128)(2,1)}, u32[]{:S(2)}) copy-start(bf16[1,1536,1024]{2,1,0:T(8,128)(2,1)} %param.8) | copy-start | bytes 9437188
  0.0 7.0 %copy-start.2 = (f32[1,1536]{1,0:T(1,128)S(1)}, f32[1,1536]{1,0:T(1,128)}, u32[]{:S(2)}) copy-start(f32[1,1536]{1,0:T(1,128)} %refs_7_.1) | copy-start | bytes 18436
  1.0 6.6 %collective-permute-start.2 = (bf16[2,128,128]{2,1,0:T(8,128)(2,1)S(1)}, bf16[2,128,128]{2,1,0:T(8,128)(2,1)S(1)}, u32[]{:S(2)}, u32[]{:S(2)}) collective-permute-start(bf16[2,128,128]{2,1,0:T(8,128)(2,1)S(1)} %get-tuple-element.22.refs_3_), channel_id=1, source_target_pairs={{1,0},{0,1},{3,2},{2,3},{5,4},{4,5},{7,6},{6,7},{9,8},{8,9},{11,10... | collective-permute-start | bytes 196616 | tf_op jit(solution)/shard_map/ppermute | solution.py:25
  3.1 4.6 %collective-permute-start.1 = (bf16[128,128]{1,0:T(8,128)(2,1)S(1)}, bf16[128,128]{1,0:T(8,128)(2,1)S(1)}, u32[]{:S(2)}, u32[]{:S(2)}) collective-permute-start(bf16[128,128]{1,0:T(8,128)(2,1)S(1)} %get-tuple-element.20), channel_id=1, source_target_pairs={{17,0},{16,1},{19,2},{18,3},{21,4},{20,5},{23,6},{22,7},{25,8},{24... | collective-permute-start | bytes 98312 | tf_op jit(solution)/shard_map/ppermute | solution.py:364
  4.3 3.4 %collective-permute-start = (bf16[128,128]{1,0:T(8,128)(2,1)S(1)}, bf16[128,128]{1,0:T(8,128)(2,1)S(1)}, u32[]{:S(2)}, u32[]{:S(2)}) collective-permute-start(bf16[128,128]{1,0:T(8,128)(2,1)S(1)} %get-tuple-element.20), channel_id=1, source_target_pairs={{16,0},{17,1},{18,2},{19,3},{20,4},{21,5},{22,6},{23,7},{24,8},{25... | collective-permute-start | bytes 98312 | tf_op jit(solution)/shard_map/ppermute | solution.py:364
  5.5 10.8 %collective-permute-start.7 = (bf16[128,1536]{1,0:T(8,128)(2,1)S(1)}, bf16[128,1536]{1,0:T(8,128)(2,1)S(1)}, u32[]{:S(2)}, u32[]{:S(2)}) collective-permute-start(bf16[128,1536]{1,0:T(8,128)(2,1)S(1)} %bitcast.9), channel_id=1, source_target_pairs={{8,0},{16,8},{24,16},{0,24},{9,1},{17,9},{25,17},{1,25},{10,2},{18... | collective-permute-start | bytes 1179656 | tf_op jit(solution)/shard_map/ppermute | solution.py:21
  7.6 8.7 %collective-permute-start.6 = (bf16[144,1024]{1,0:T(8,128)(2,1)S(1)}, bf16[144,1024]{1,0:T(8,128)(2,1)S(1)}, u32[]{:S(2)}, u32[]{:S(2)}) collective-permute-start(bf16[144,1024]{1,0:T(8,128)(2,1)S(1)} %get-tuple-element.25), channel_id=1, source_target_pairs={{1,0},{0,1},{3,2},{2,3},{5,4},{4,5},{7,6},{6,7},{9,8},{8,9},{11,10... | collective-permute-start | bytes 884744 | tf_op jit(solution)/shard_map/ppermute | solution.py:25
  8.0 5.2 %collective-permute-start.5 = (bf16[2,128,128]{2,1,0:T(8,128)(2,1)S(1)}, bf16[2,128,128]{2,1,0:T(8,128)(2,1)S(1)}, u32[]{:S(2)}, u32[]{:S(2)}) collective-permute-start(bf16[2,128,128]{2,1,0:T(8,128)(2,1)S(1)} %shard_map.75.refs_0_), channel_id=1, source_target_pairs={{6,0},{7,1},{4,2},{5,3},{2,4},{3,5},{0,6},{1,7},{14,8},{15,9},{12,... | collective-permute-start | bytes 196616 | tf_op jit(solution)/shard_map/ppermute | solution.py:25
  11.5 5.3 %collective-permute-start.4 = (bf16[2,128,128]{2,1,0:T(8,128)(2,1)S(1)}, bf16[2,128,128]{2,1,0:T(8,128)(2,1)S(1)}, u32[]{:S(2)}, u32[]{:S(2)}) collective-permute-start(bf16[2,128,128]{2,1,0:T(8,128)(2,1)S(1)} %shard_map.75.refs_0_), channel_id=1, source_target_pairs={{4,0},{5,1},{6,2},{7,3},{0,4},{1,5},{2,6},{3,7},{12,8},{13,9},{14,... | collective-permute-start | bytes 196616 | tf_op jit(solution)/shard_map/ppermute | solution.py:25
  11.5 5.3 %collective-permute-start.3 = (bf16[2,128,128]{2,1,0:T(8,128)(2,1)S(1)}, bf16[2,128,128]{2,1,0:T(8,128)(2,1)S(1)}, u32[]{:S(2)}, u32[]{:S(2)}) collective-permute-start(bf16[2,128,128]{2,1,0:T(8,128)(2,1)S(1)} %shard_map.75.refs_0_), channel_id=1, source_target_pairs={{2,0},{3,1},{0,2},{1,3},{6,4},{7,5},{4,6},{5,7},{10,8},{11,9},{8,1... | collective-permute-start | bytes 196616 | tf_op jit(solution)/shard_map/ppermute | solution.py:25
  17.6 8.6 %collective-permute-start.8 = (bf16[128,1664]{1,0:T(8,128)(2,1)S(1)}, bf16[128,1664]{1,0:T(8,128)(2,1)S(1)}, u32[]{:S(2)}, u32[]{:S(2)}) collective-permute-start(bf16[128,1664]{1,0:T(8,128)(2,1)S(1)} %get-tuple-element.30), channel_id=1, source_target_pairs={{8,0},{16,8},{24,16},{0,24},{9,1},{17,9},{25,17},{1,25},{10,2},{18... | collective-permute-start | bytes 1277960 | tf_op jit(solution)/shard_map/ppermute | solution.py:21
  19.6 5.7 %collective-permute-start.11 = (f32[2,128]{1,0:T(2,128)S(1)}, f32[2,128]{1,0:T(2,128)S(1)}, u32[]{:S(2)}, u32[]{:S(2)}) collective-permute-start(f32[2,128]{1,0:T(2,128)S(1)} %get-tuple-element.32), channel_id=1, source_target_pairs={{14,0},{15,1},{12,2},{13,3},{10,4},{11,5},{8,6},{9,7},{22,8},{23,9... | collective-permute-start | bytes 3080 | tf_op jit(solution)/shard_map/ppermute | solution.py:354
  21.4 4.8 %collective-permute-start.10 = (f32[2,128]{1,0:T(2,128)S(1)}, f32[2,128]{1,0:T(2,128)S(1)}, u32[]{:S(2)}, u32[]{:S(2)}) collective-permute-start(f32[2,128]{1,0:T(2,128)S(1)} %get-tuple-element.32), channel_id=1, source_target_pairs={{12,0},{13,1},{14,2},{15,3},{8,4},{9,5},{10,6},{11,7},{20,8},{21,9... | collective-permute-start | bytes 3080 | tf_op jit(solution)/shard_map/ppermute | solution.py:354
  21.8 4.4 %collective-permute-start.9 = (f32[2,128]{1,0:T(2,128)S(1)}, f32[2,128]{1,0:T(2,128)S(1)}, u32[]{:S(2)}, u32[]{:S(2)}) collective-permute-start(f32[2,128]{1,0:T(2,128)S(1)} %get-tuple-element.32), channel_id=1, source_target_pairs={{10,0},{11,1},{8,2},{9,3},{14,4},{15,5},{12,6},{13,7},{18,8},{19,9... | collective-permute-start | bytes 3080 | tf_op jit(solution)/shard_map/ppermute | solution.py:354

commit v4 on v2

--- a/solution.py
+++ b/solution.py
@@ -341,7 +341,7 @@
 
 FAR, NEAR, SIDE = 4, 2, 1
 ORDER = ((0, SIDE), (SIDE, 0))
-LINE = (FAR | NEAR, FAR, NEAR)
+LINE = ((FAR | NEAR, FAR), (FAR, FAR | NEAR), (NEAR, NEAR))
 EARLY = 2
 
 
@@ -364,14 +364,23 @@
     return lax.ppermute(block, ("section", "tp"), route)
 
 
-def gathered(pair, axis):
-    if lax.axis_size(axis) != 8:
+def gathered(pair, axis, sections, count):
+    if count != 8:
         return [lax.all_gather(pair[0], axis)], lambda place: place
-    blocks = [pair] + [swapped(pair, axis, mask) for mask in LINE]
-    masks = [far | side for far in (0, *LINE) for side in (0, SIDE)]
+    half = sections // 2
+    blocks = [pair]
+    for masks in LINE:
+        route = [
+            (s * count + (i ^ masks[s // half]), s * count + i)
+            for s in range(sections)
+            for i in range(count)
+        ]
+        blocks.append(lax.ppermute(pair, ("section", axis), route))
 
     def head_of(place):
-        return lax.axis_index(axis) ^ masks[place]
+        lower, upper = ((0, 0), *LINE)[place // 2]
+        mask = lower + (lax.axis_index("section") // half) * (upper - lower)
+        return lax.axis_index(axis) ^ mask ^ (place % 2 * SIDE)
 
     return blocks, head_of
 
@@ -391,7 +400,7 @@
     else:
         reaches = [lax.psum(own_reach, "tp")]
     pair = value_gradients(taken, spares, packs, lambda: lax.axis_index("section") >= half)
-    blocks, head_of = gathered(pair, "tp")
+    blocks, head_of = gathered(pair, "tp", sections, count)
     soon, late = (blocks[:EARLY], blocks[EARLY:]) if count == 8 else ([], blocks)
     early = [project_early(head_of, soon, weights)] if soon else []
     joined = join(head_of, soon, reaches)

time: 27.4 us -> 27.5 us (level)
    ppermute x0 -> x3, starting transfers between devices: none -> 3.94 us  [gathered(): blocks.append(lax.ppermute(pair, ('section', axis), route))]
    ppermute x5 -> x2, starting transfers between devices: 6.14 us -> 2.21 us  [swapped(): lax.ppermute(block, axis, [(i ^ mask, i) for i in range(lax.axis_size(axi...]
    ppermute x5 -> x2, waiting for transfers between devices: 4.12 us -> 2.47 us  [swapped(): lax.ppermute(block, axis, [(i ^ mask, i) for i in range(lax.axis_size(axi...]
    ppermute x0 -> x3, waiting for transfers between devices: none -> 1.65 us  [gathered(): blocks.append(lax.ppermute(pair, ('section', axis), route))]
  transfers between devices with their start and end apart: 12 -> 12, of which waited for: 5 -> 6; matrix products, arithmetic and copies ran while one was open for 0% -> 0% of each run, Pallas kernels for 6% -> 6%
where the time goes in v4:
time: 27.5 us; the launch traced here: 27.4 us
  starting transfers between devices  16.5 us (60%)
  waiting for transfers between devices  6.35 us (23%)
  Pallas kernels  4.4 us (16%)
    ppermute x3, starting transfers between devices, handed_over(): return lax.ppermute(block, ('section', 'tp'), route)  4.53 us
    ppermute x3, starting transfers between devices, gathered(): blocks.append(lax.ppermute(pair, ('section', axis), route))  3.94 us
    ppermute x2, starting transfers between devices, passed_along(): return lax.ppermute(block, axis, route)  3.5 us
    ppermute x2, waiting for transfers between devices, swapped(): lax.ppermute(block, axis, [(i ^ mask, i) for i in range(lax.axis_size(axi...  2.47 us
    ppermute x2, starting transfers between devices, fetched(): return lax.ppermute(block, ('section', 'tp'), route)  2.36 us
    ppermute x2, starting transfers between devices, swapped(): lax.ppermute(block, axis, [(i ^ mask, i) for i in range(lax.axis_size(axi...  2.21 us
    ppermute x3, waiting for transfers between devices, handed_over(): return lax.ppermute(block, ('section', 'tp'), route)  2.13 us
    ppermute x3, waiting for transfers between devices, gathered(): blocks.append(lax.ppermute(pair, ('section', axis), route))  1.65 us
  transfers between devices with their start and end apart: 12, of which 6 were waited for; matrix products, arithmetic and copies ran while one was open for 0% of the time, Pallas kernels for 6%

profile of v4, /device:TPU:1, one launch (start us, length us, event | category | flops | bytes accessed | tf_op | source)
XLA Modules:
  0.0 27.4 jit_solution(17158013389797184828)
XLA Ops:
  0.0 0.0 copy-start.1
  0.0 0.0 copy-start
  0.0 0.0 copy-start.2
  0.0 1.0 %shard_map.73 = (bf16[2,128,128]{2,1,0:T(8,128)(2,1)S(1)}, bf16[128,128]{1,0:T(8,128)(2,1)S(1)}, bf16[128,128]{1,0:T(8,128)(2,1)S(1)}) custom-call(bf16[128,128]{1,0:T(8,128)(2,1)} %bitcast.12, bf16[128,128]{1,0:T(8,128)(2,1)} %bitcast.13, bf16[128,128]{1,0:T(8,128)(2,1)} %bitcast.14, s32[1,4]{1,0:T(1,128)} %evicted_ref.1), custom_call_target="tpu_custom_call" | custom-call | flops 34359738368 | bytes 33554432 | tf_op jit(solution)/shard_map/pallas_call | solution.py:87
  1.0 2.1 %collective-permute-start.2 = (bf16[2,128,128]{2,1,0:T(8,128)(2,1)S(1)}, bf16[2,128,128]{2,1,0:T(8,128)(2,1)S(1)}, u32[]{:S(2)}, u32[]{:S(2)}) collective-permute-start(bf16[2,128,128]{2,1,0:T(8,128)(2,1)S(1)} %get-tuple-element.19.refs_3_), channel_id=1, source_target_pairs={{1,0},{0,1},{3,2},{2,3},{5,4},{4,5},{7,6},{6,7},{9,8},{8,9},{11,10... | collective-permute-start | bytes 196616 | tf_op jit(solution)/shard_map/ppermute | solution.py:24
  3.1 1.2 %collective-permute-start = (bf16[128,128]{1,0:T(8,128)(2,1)S(1)}, bf16[128,128]{1,0:T(8,128)(2,1)S(1)}, u32[]{:S(2)}, u32[]{:S(2)}) collective-permute-start(bf16[128,128]{1,0:T(8,128)(2,1)S(1)} %get-tuple-element.18), channel_id=1, source_target_pairs={{17,0},{16,1},{19,2},{18,3},{21,4},{20,5},{23,6},{22,7},{25,8},{24... | collective-permute-start | bytes 98312 | tf_op jit(solution)/shard_map/ppermute | solution.py:364
  4.3 1.2 %collective-permute-start.1 = (bf16[128,128]{1,0:T(8,128)(2,1)S(1)}, bf16[128,128]{1,0:T(8,128)(2,1)S(1)}, u32[]{:S(2)}, u32[]{:S(2)}) collective-permute-start(bf16[128,128]{1,0:T(8,128)(2,1)S(1)} %get-tuple-element.18), channel_id=1, source_target_pairs={{16,0},{17,1},{18,2},{19,3},{20,4},{21,5},{22,6},{23,7},{24,8},{25... | collective-permute-start | bytes 98312 | tf_op jit(solution)/shard_map/ppermute | solution.py:364
  5.5 0.0 copy-done.1
  5.5 1.5 %collective-permute-start.7 = (bf16[128,1536]{1,0:T(8,128)(2,1)S(1)}, bf16[128,1536]{1,0:T(8,128)(2,1)S(1)}, u32[]{:S(2)}, u32[]{:S(2)}) collective-permute-start(bf16[128,1536]{1,0:T(8,128)(2,1)S(1)} %bitcast.9), channel_id=1, source_target_pairs={{8,0},{16,8},{24,16},{0,24},{9,1},{17,9},{25,17},{1,25},{10,2},{18... | collective-permute-start | bytes 1179656 | tf_op jit(solution)/shard_map/ppermute | solution.py:20
  7.0 0.0 collective-permute-done.2.refs_2_.first_ref
  7.0 0.0 copy-done
  7.0 0.0 copy-done.2
  7.0 0.6 %shard_map.75 = (bf16[144,1024]{1,0:T(8,128)(2,1)S(1)}, f32[144,1024]{1,0:T(8,128)S(1)}) custom-call(bf16[1536,1024]{1,0:T(8,128)(2,1)S(1)} %bitcast.6, bf16[128,1536]{1,0:T(8,128)(2,1)S(1)} %bitcast.10, f32[1,1536]{1,0:T(1,128)S(1)} %copy-done.2, bf16[2,128,128]{2,1,0:T(8,128)(2,1)S(1)} %collective-permute-done.2.refs_2_.first_ref), custom_call_target="tpu_custom_call" | custom-call | flops 34359738368 | bytes 33554432 | tf_op jit(solution)/shard_map/pallas_call | solution.py:120
  7.6 0.1 collective-permute-start.6
  7.7 0.0 collective-permute-done.refs_0_
  7.7 0.0 collective-permute-done.1.refs_1_
  7.7 0.2 shard_map.74.refs_0_
  8.0 3.6 %collective-permute-start.5 = (bf16[2,128,128]{2,1,0:T(8,128)(2,1)S(1)}, bf16[2,128,128]{2,1,0:T(8,128)(2,1)S(1)}, u32[]{:S(2)}, u32[]{:S(2)}) collective-permute-start(bf16[2,128,128]{2,1,0:T(8,128)(2,1)S(1)} %shard_map.74.refs_0_), channel_id=1, source_target_pairs={{6,0},{7,1},{4,2},{5,3},{2,4},{3,5},{0,6},{1,7},{14,8},{15,9},{12,... | collective-permute-start | bytes 196616 | tf_op jit(solution)/shard_map/ppermute | solution.py:378
  11.5 0.0 collective-permute-start.3
  11.5 0.4 %collective-permute-start.4 = (bf16[2,128,128]{2,1,0:T(8,128)(2,1)S(1)}, bf16[2,128,128]{2,1,0:T(8,128)(2,1)S(1)}, u32[]{:S(2)}, u32[]{:S(2)}) collective-permute-start(bf16[2,128,128]{2,1,0:T(8,128)(2,1)S(1)} %shard_map.74.refs_0_), channel_id=1, source_target_pairs={{2,0},{3,1},{0,2},{1,3},{6,4},{7,5},{4,6},{5,7},{10,8},{11,9},{8,1... | collective-permute-start | bytes 196616 | tf_op jit(solution)/shard_map/ppermute | solution.py:378
  11.9 1.3 %collective-permute-done.5.refs_1_ = bf16[2,128,128]{2,1,0:T(8,128)(2,1)S(1)} collective-permute-done((bf16[2,128,128]{2,1,0:T(8,128)(2,1)S(1)}, bf16[2,128,128]{2,1,0:T(8,128)(2,1)S(1)}, u32[]{:S(2)}, u32[]{:S(2)}) %collective-permute-start.5) | collective-permute-done | bytes 65568 | tf_op jit(solution)/shard_map/ppermute | solution.py:378
  13.2 0.7 %shard_map.77.refs_8_ = f32[128,1536]{1,0:T(8,128)S(1)} custom-call(bf16[2,128,128]{2,1,0:T(8,128)(2,1)S(1)} %shard_map.74.refs_0_, bf16[2,128,128]{2,1,0:T(8,128)(2,1)S(1)} %collective-permute-done.5.refs_1_, bf16[1536,1024]{1,0:T(8,128)(2,1)S(1)} %bitcast.7), custom_call_target="tpu_custom_call" | custom-call | flops 65536 | bytes 4096 | tf_op jit(solution)/shard_map/pallas_call | solution.py:204
  13.9 2.5 %collective-permute-done.6.refs_3_ = bf16[144,1024]{1,0:T(8,128)(2,1)S(1)} collective-permute-done((bf16[144,1024]{1,0:T(8,128)(2,1)S(1)}, bf16[144,1024]{1,0:T(8,128)(2,1)S(1)}, u32[]{:S(2)}, u32[]{:S(2)}) %collective-permute-start.6) | collective-permute-done | bytes 294944 | tf_op jit(solution)/shard_map/ppermute | solution.py:24
  16.3 0.0 collective-permute-done.7.input_ref
  16.3 0.1 shard_map.76
  16.4 0.4 %collective-permute-done.3.refs_0_ = bf16[2,128,128]{2,1,0:T(8,128)(2,1)S(1)} collective-permute-done((bf16[2,128,128]{2,1,0:T(8,128)(2,1)S(1)}, bf16[2,128,128]{2,1,0:T(8,128)(2,1)S(1)}, u32[]{:S(2)}, u32[]{:S(2)}) %collective-permute-start.3) | collective-permute-done | bytes 65568 | tf_op jit(solution)/shard_map/ppermute | solution.py:378
  16.8 0.0 collective-permute-done.4.refs_1_
  16.8 0.8 %shard_map.78 = (bf16[128,1664]{1,0:T(8,128)(2,1)S(1)}, f32[2,128]{1,0:T(2,128)S(1)}) custom-call(bf16[2,128,128]{2,1,0:T(8,128)(2,1)S(1)} %collective-permute-done.3.refs_0_, bf16[2,128,128]{2,1,0:T(8,128)(2,1)S(1)} %collective-permute-done.4.refs_1_, f32[128,1024]{1,0:T(8,128)S(1)} %get-tuple-element.23.refs_2_, f32[128,128]{1,0:T(8,128)S(1)} %get-tuple-element.24.refs_3_, ...), custom_call_target="tpu_custom_call" | custom-call | flops 34359738368 | bytes 33554432 | tf_op jit(solution)/shard_map/pallas_call | solution.py:287
  17.6 2.0 %collective-permute-start.8 = (bf16[128,1664]{1,0:T(8,128)(2,1)S(1)}, bf16[128,1664]{1,0:T(8,128)(2,1)S(1)}, u32[]{:S(2)}, u32[]{:S(2)}) collective-permute-start(bf16[128,1664]{1,0:T(8,128)(2,1)S(1)} %get-tuple-element.26), channel_id=1, source_target_pairs={{8,0},{16,8},{24,16},{0,24},{9,1},{17,9},{25,17},{1,25},{10,2},{18... | collective-permute-start | bytes 1277960 | tf_op jit(solution)/shard_map/ppermute | solution.py:20
  19.6 1.9 %collective-permute-start.10 = (f32[2,128]{1,0:T(2,128)S(1)}, f32[2,128]{1,0:T(2,128)S(1)}, u32[]{:S(2)}, u32[]{:S(2)}) collective-permute-start(f32[2,128]{1,0:T(2,128)S(1)} %get-tuple-element.28), channel_id=1, source_target_pairs={{14,0},{15,1},{12,2},{13,3},{10,4},{11,5},{8,6},{9,7},{22,8},{23,9... | collective-permute-start | bytes 3080 | tf_op jit(solution)/shard_map/ppermute | solution.py:354
  21.4 0.1 collective-permute-start.11
  21.5 2.6 %collective-permute-start.9 = (f32[2,128]{1,0:T(2,128)S(1)}, f32[2,128]{1,0:T(2,128)S(1)}, u32[]{:S(2)}, u32[]{:S(2)}) collective-permute-start(f32[2,128]{1,0:T(2,128)S(1)} %get-tuple-element.28), channel_id=1, source_target_pairs={{10,0},{11,1},{8,2},{9,3},{14,4},{15,5},{12,6},{13,7},{18,8},{19,9... | collective-permute-start | bytes 3080 | tf_op jit(solution)/shard_map/ppermute | solution.py:354
  24.1 1.2 %collective-permute-done.10.refs_1_ = f32[2,128]{1,0:T(2,128)S(1)} collective-permute-done((f32[2,128]{1,0:T(2,128)S(1)}, f32[2,128]{1,0:T(2,128)S(1)}, u32[]{:S(2)}, u32[]{:S(2)}) %collective-permute-start.10) | collective-permute-done | bytes 1056 | tf_op jit(solution)/shard_map/ppermute | solution.py:354
  25.3 1.0 %collective-permute-done.11.refs_2_ = f32[2,128]{1,0:T(2,128)S(1)} collective-permute-done((f32[2,128]{1,0:T(2,128)S(1)}, f32[2,128]{1,0:T(2,128)S(1)}, u32[]{:S(2)}, u32[]{:S(2)}) %collective-permute-start.11) | collective-permute-done | bytes 1056 | tf_op jit(solution)/shard_map/ppermute | solution.py:354
  26.2 0.0 collective-permute-done.9.refs_0_
  26.2 0.1 collective-permute-done.8.scaled_ref
  26.3 1.1 %shard_map.79 = bf16[128,1536]{1,0:T(8,128)(2,1)} custom-call(bf16[128,1664]{1,0:T(8,128)(2,1)S(1)} %collective-permute-done.8.scaled_ref, bf16[128,1536]{1,0:T(8,128)(2,1)S(1)} %collective-permute-done.7.input_ref, f32[2,128]{1,0:T(2,128)S(1)} %collective-permute-done.9.refs_0_, f32[2,128]{1,0:T(2,128)S(1)} %collective-permute-done.10.refs_1_, ...), custom_call_target="tpu_custom_call" | custom-call | tf_op jit(solution)/shard_map/pallas_call | solution.py:329
Async XLA Ops:
  0.0 5.5 %copy-start.1 = (bf16[1,128,1536]{2,1,0:T(8,128)(2,1)S(1)}, bf16[1,128,1536]{2,1,0:T(8,128)(2,1)}, u32[]{:S(2)}) copy-start(bf16[1,128,1536]{2,1,0:T(8,128)(2,1)} %param.12) | copy-start | bytes 1179652
  0.0 7.0 %copy-start = (bf16[1,1536,1024]{2,1,0:T(8,128)(2,1)S(1)}, bf16[1,1536,1024]{2,1,0:T(8,128)(2,1)}, u32[]{:S(2)}) copy-start(bf16[1,1536,1024]{2,1,0:T(8,128)(2,1)} %param.8) | copy-start | bytes 9437188
  0.0 7.0 %copy-start.2 = (f32[1,1536]{1,0:T(1,128)S(1)}, f32[1,1536]{1,0:T(1,128)}, u32[]{:S(2)}) copy-start(f32[1,1536]{1,0:T(1,128)} %refs_7_.1) | copy-start | bytes 18436
  1.0 6.0 %collective-permute-start.2 = (bf16[2,128,128]{2,1,0:T(8,128)(2,1)S(1)}, bf16[2,128,128]{2,1,0:T(8,128)(2,1)S(1)}, u32[]{:S(2)}, u32[]{:S(2)}) collective-permute-start(bf16[2,128,128]{2,1,0:T(8,128)(2,1)S(1)} %get-tuple-element.19.refs_3_), channel_id=1, source_target_pairs={{1,0},{0,1},{3,2},{2,3},{5,4},{4,5},{7,6},{6,7},{9,8},{8,9},{11,10... | collective-permute-start | bytes 196616 | tf_op jit(solution)/shard_map/ppermute | solution.py:24
  3.1 4.6 %collective-permute-start = (bf16[128,128]{1,0:T(8,128)(2,1)S(1)}, bf16[128,128]{1,0:T(8,128)(2,1)S(1)}, u32[]{:S(2)}, u32[]{:S(2)}) collective-permute-start(bf16[128,128]{1,0:T(8,128)(2,1)S(1)} %get-tuple-element.18), channel_id=1, source_target_pairs={{17,0},{16,1},{19,2},{18,3},{21,4},{20,5},{23,6},{22,7},{25,8},{24... | collective-permute-start | bytes 98312 | tf_op jit(solution)/shard_map/ppermute | solution.py:364
  4.3 3.4 %collective-permute-start.1 = (bf16[128,128]{1,0:T(8,128)(2,1)S(1)}, bf16[128,128]{1,0:T(8,128)(2,1)S(1)}, u32[]{:S(2)}, u32[]{:S(2)}) collective-permute-start(bf16[128,128]{1,0:T(8,128)(2,1)S(1)} %get-tuple-element.18), channel_id=1, source_target_pairs={{16,0},{17,1},{18,2},{19,3},{20,4},{21,5},{22,6},{23,7},{24,8},{25... | collective-permute-start | bytes 98312 | tf_op jit(solution)/shard_map/ppermute | solution.py:364
  5.5 10.8 %collective-permute-start.7 = (bf16[128,1536]{1,0:T(8,128)(2,1)S(1)}, bf16[128,1536]{1,0:T(8,128)(2,1)S(1)}, u32[]{:S(2)}, u32[]{:S(2)}) collective-permute-start(bf16[128,1536]{1,0:T(8,128)(2,1)S(1)} %bitcast.9), channel_id=1, source_target_pairs={{8,0},{16,8},{24,16},{0,24},{9,1},{17,9},{25,17},{1,25},{10,2},{18... | collective-permute-start | bytes 1179656 | tf_op jit(solution)/shard_map/ppermute | solution.py:20
  7.6 8.7 %collective-permute-start.6 = (bf16[144,1024]{1,0:T(8,128)(2,1)S(1)}, bf16[144,1024]{1,0:T(8,128)(2,1)S(1)}, u32[]{:S(2)}, u32[]{:S(2)}) collective-permute-start(bf16[144,1024]{1,0:T(8,128)(2,1)S(1)} %get-tuple-element.21), channel_id=1, source_target_pairs={{1,0},{0,1},{3,2},{2,3},{5,4},{4,5},{7,6},{6,7},{9,8},{8,9},{11,10... | collective-permute-start | bytes 884744 | tf_op jit(solution)/shard_map/ppermute | solution.py:24
  8.0 5.2 %collective-permute-start.5 = (bf16[2,128,128]{2,1,0:T(8,128)(2,1)S(1)}, bf16[2,128,128]{2,1,0:T(8,128)(2,1)S(1)}, u32[]{:S(2)}, u32[]{:S(2)}) collective-permute-start(bf16[2,128,128]{2,1,0:T(8,128)(2,1)S(1)} %shard_map.74.refs_0_), channel_id=1, source_target_pairs={{6,0},{7,1},{4,2},{5,3},{2,4},{3,5},{0,6},{1,7},{14,8},{15,9},{12,... | collective-permute-start | bytes 196616 | tf_op jit(solution)/shard_map/ppermute | solution.py:378
  11.5 5.3 %collective-permute-start.3 = (bf16[2,128,128]{2,1,0:T(8,128)(2,1)S(1)}, bf16[2,128,128]{2,1,0:T(8,128)(2,1)S(1)}, u32[]{:S(2)}, u32[]{:S(2)}) collective-permute-start(bf16[2,128,128]{2,1,0:T(8,128)(2,1)S(1)} %shard_map.74.refs_0_), channel_id=1, source_target_pairs={{4,0},{5,1},{6,2},{7,3},{0,4},{1,5},{2,6},{3,7},{12,8},{13,9},{14,... | collective-permute-start | bytes 196616 | tf_op jit(solution)/shard_map/ppermute | solution.py:378
  11.5 5.3 %collective-permute-start.4 = (bf16[2,128,128]{2,1,0:T(8,128)(2,1)S(1)}, bf16[2,128,128]{2,1,0:T(8,128)(2,1)S(1)}, u32[]{:S(2)}, u32[]{:S(2)}) collective-permute-start(bf16[2,128,128]{2,1,0:T(8,128)(2,1)S(1)} %shard_map.74.refs_0_), channel_id=1, source_target_pairs={{2,0},{3,1},{0,2},{1,3},{6,4},{7,5},{4,6},{5,7},{10,8},{11,9},{8,1... | collective-permute-start | bytes 196616 | tf_op jit(solution)/shard_map/ppermute | solution.py:378
  17.6 8.8 %collective-permute-start.8 = (bf16[128,1664]{1,0:T(8,128)(2,1)S(1)}, bf16[128,1664]{1,0:T(8,128)(2,1)S(1)}, u32[]{:S(2)}, u32[]{:S(2)}) collective-permute-start(bf16[128,1664]{1,0:T(8,128)(2,1)S(1)} %get-tuple-element.26), channel_id=1, source_target_pairs={{8,0},{16,8},{24,16},{0,24},{9,1},{17,9},{25,17},{1,25},{10,2},{18... | collective-permute-start | bytes 1277960 | tf_op jit(solution)/shard_map/ppermute | solution.py:20
  19.6 5.7 %collective-permute-start.10 = (f32[2,128]{1,0:T(2,128)S(1)}, f32[2,128]{1,0:T(2,128)S(1)}, u32[]{:S(2)}, u32[]{:S(2)}) collective-permute-start(f32[2,128]{1,0:T(2,128)S(1)} %get-tuple-element.28), channel_id=1, source_target_pairs={{14,0},{15,1},{12,2},{13,3},{10,4},{11,5},{8,6},{9,7},{22,8},{23,9... | collective-permute-start | bytes 3080 | tf_op jit(solution)/shard_map/ppermute | solution.py:354
  21.4 4.8 %collective-permute-start.11 = (f32[2,128]{1,0:T(2,128)S(1)}, f32[2,128]{1,0:T(2,128)S(1)}, u32[]{:S(2)}, u32[]{:S(2)}) collective-permute-start(f32[2,128]{1,0:T(2,128)S(1)} %get-tuple-element.28), channel_id=1, source_target_pairs={{12,0},{13,1},{14,2},{15,3},{8,4},{9,5},{10,6},{11,7},{20,8},{21,9... | collective-permute-start | bytes 3080 | tf_op jit(solution)/shard_map/ppermute | solution.py:354
  21.5 4.7 %collective-permute-start.9 = (f32[2,128]{1,0:T(2,128)S(1)}, f32[2,128]{1,0:T(2,128)S(1)}, u32[]{:S(2)}, u32[]{:S(2)}) collective-permute-start(f32[2,128]{1,0:T(2,128)S(1)} %get-tuple-element.28), channel_id=1, source_target_pairs={{10,0},{11,1},{8,2},{9,3},{14,4},{15,5},{12,6},{13,7},{18,8},{19,9... | collective-permute-start | bytes 3080 | tf_op jit(solution)/shard_map/ppermute | solution.py:354

commit v5 on v4

--- a/solution.py
+++ b/solution.py
@@ -341,7 +341,7 @@
 
 FAR, NEAR, SIDE = 4, 2, 1
 ORDER = ((0, SIDE), (SIDE, 0))
-LINE = ((FAR | NEAR, FAR), (FAR, FAR | NEAR), (NEAR, NEAR))
+LINE = ((FAR, FAR | NEAR), (FAR | NEAR, FAR), (NEAR, NEAR))
 EARLY = 2
 
 

time: 27.5 us -> 28 us (1.018)
  waiting for transfers between devices: 6.35 us -> 6.63 us
    ppermute x3, waiting for transfers between devices: 1.65 us -> 0.36 us  [gathered(): blocks.append(lax.ppermute(pair, ('section', axis), route))]
    ppermute x2, waiting for transfers between devices: 2.47 us -> 3.48 us  [swapped(): lax.ppermute(block, axis, [(i ^ mask, i) for i in range(lax.axis_size(axi...]
    ppermute x3, waiting for transfers between devices: 2.13 us -> 2.78 us  [handed_over(): return lax.ppermute(block, ('section', 'tp'), route)]
  transfers between devices with their start and end apart: 12 -> 12, of which waited for: 6 -> 4; matrix products, arithmetic and copies ran while one was open for 0% -> 0% of each run, Pallas kernels for 6% -> 6%
where the time goes in v5:
time: 28 us; the launch traced here: 27.8 us
  starting transfers between devices  16.7 us (60%)
  waiting for transfers between devices  6.63 us (24%)
  Pallas kernels  4.42 us (16%)
    ppermute x3, starting transfers between devices, handed_over(): return lax.ppermute(block, ('section', 'tp'), route)  4.46 us
    ppermute x3, starting transfers between devices, gathered(): blocks.append(lax.ppermute(pair, ('section', axis), route))  3.86 us
    ppermute x2, starting transfers between devices, passed_along(): return lax.ppermute(block, axis, route)  3.76 us
    ppermute x2, waiting for transfers between devices, swapped(): lax.ppermute(block, axis, [(i ^ mask, i) for i in range(lax.axis_size(axi...  3.48 us
    ppermute x3, waiting for transfers between devices, handed_over(): return lax.ppermute(block, ('section', 'tp'), route)  2.78 us
    ppermute x2, starting transfers between devices, fetched(): return lax.ppermute(block, ('section', 'tp'), route)  2.36 us
    ppermute x2, starting transfers between devices, swapped(): lax.ppermute(block, axis, [(i ^ mask, i) for i in range(lax.axis_size(axi...  2.21 us
    pallas_call x1, Pallas kernels, finish(): pl.pallas_call(finish_kernel, out_shape=pltpu.HBM(inputs.shape, jnp.bfloa...  1.06 us
  transfers between devices with their start and end apart: 12, of which 4 were waited for; matrix products, arithmetic and copies ran while one was open for 0% of the time, Pallas kernels for 6%

profile of v5, /device:TPU:1, one launch (start us, length us, event | category | flops | bytes accessed | tf_op | source)
XLA Modules:
  0.0 27.8 jit_solution(14256543978949989387)
XLA Ops:
  0.0 0.0 copy-start.1
  0.0 0.0 copy-start
  0.0 0.0 copy-start.2
  0.0 1.0 %shard_map.73 = (bf16[2,128,128]{2,1,0:T(8,128)(2,1)S(1)}, bf16[128,128]{1,0:T(8,128)(2,1)S(1)}, bf16[128,128]{1,0:T(8,128)(2,1)S(1)}) custom-call(bf16[128,128]{1,0:T(8,128)(2,1)} %bitcast.12, bf16[128,128]{1,0:T(8,128)(2,1)} %bitcast.13, bf16[128,128]{1,0:T(8,128)(2,1)} %bitcast.14, s32[1,4]{1,0:T(1,128)} %evicted_ref.1), custom_call_target="tpu_custom_call" | custom-call | flops 34359738368 | bytes 33554432 | tf_op jit(solution)/shard_map/pallas_call | solution.py:87
  1.0 2.1 %collective-permute-start.2 = (bf16[2,128,128]{2,1,0:T(8,128)(2,1)S(1)}, bf16[2,128,128]{2,1,0:T(8,128)(2,1)S(1)}, u32[]{:S(2)}, u32[]{:S(2)}) collective-permute-start(bf16[2,128,128]{2,1,0:T(8,128)(2,1)S(1)} %get-tuple-element.19.refs_3_), channel_id=1, source_target_pairs={{1,0},{0,1},{3,2},{2,3},{5,4},{4,5},{7,6},{6,7},{9,8},{8,9},{11,10... | collective-permute-start | bytes 196616 | tf_op jit(solution)/shard_map/ppermute | solution.py:24
  3.1 1.2 %collective-permute-start = (bf16[128,128]{1,0:T(8,128)(2,1)S(1)}, bf16[128,128]{1,0:T(8,128)(2,1)S(1)}, u32[]{:S(2)}, u32[]{:S(2)}) collective-permute-start(bf16[128,128]{1,0:T(8,128)(2,1)S(1)} %get-tuple-element.18), channel_id=1, source_target_pairs={{17,0},{16,1},{19,2},{18,3},{21,4},{20,5},{23,6},{22,7},{25,8},{24... | collective-permute-start | bytes 98312 | tf_op jit(solution)/shard_map/ppermute | solution.py:364
  4.3 1.2 %collective-permute-start.1 = (bf16[128,128]{1,0:T(8,128)(2,1)S(1)}, bf16[128,128]{1,0:T(8,128)(2,1)S(1)}, u32[]{:S(2)}, u32[]{:S(2)}) collective-permute-start(bf16[128,128]{1,0:T(8,128)(2,1)S(1)} %get-tuple-element.18), channel_id=1, source_target_pairs={{16,0},{17,1},{18,2},{19,3},{20,4},{21,5},{22,6},{23,7},{24,8},{25... | collective-permute-start | bytes 98312 | tf_op jit(solution)/shard_map/ppermute | solution.py:364
  5.5 0.0 copy-done.1
  5.5 1.5 %collective-permute-start.7 = (bf16[128,1536]{1,0:T(8,128)(2,1)S(1)}, bf16[128,1536]{1,0:T(8,128)(2,1)S(1)}, u32[]{:S(2)}, u32[]{:S(2)}) collective-permute-start(bf16[128,1536]{1,0:T(8,128)(2,1)S(1)} %bitcast.9), channel_id=1, source_target_pairs={{8,0},{16,8},{24,16},{0,24},{9,1},{17,9},{25,17},{1,25},{10,2},{18... | collective-permute-start | bytes 1179656 | tf_op jit(solution)/shard_map/ppermute | solution.py:20
  7.0 0.0 collective-permute-done.2.refs_2_.first_ref
  7.0 0.0 copy-done
  7.0 0.0 copy-done.2
  7.0 0.6 %shard_map.75 = (bf16[144,1024]{1,0:T(8,128)(2,1)S(1)}, f32[144,1024]{1,0:T(8,128)S(1)}) custom-call(bf16[1536,1024]{1,0:T(8,128)(2,1)S(1)} %bitcast.6, bf16[128,1536]{1,0:T(8,128)(2,1)S(1)} %bitcast.10, f32[1,1536]{1,0:T(1,128)S(1)} %copy-done.2, bf16[2,128,128]{2,1,0:T(8,128)(2,1)S(1)} %collective-permute-done.2.refs_2_.first_ref), custom_call_target="tpu_custom_call" | custom-call | flops 34359738368 | bytes 33554432 | tf_op jit(solution)/shard_map/pallas_call | solution.py:120
  7.6 0.1 collective-permute-start.6
  7.7 0.0 collective-permute-done.refs_0_
  7.7 0.0 collective-permute-done.1.refs_1_
  7.7 0.2 shard_map.74.refs_0_
  8.0 2.6 %collective-permute-start.5 = (bf16[2,128,128]{2,1,0:T(8,128)(2,1)S(1)}, bf16[2,128,128]{2,1,0:T(8,128)(2,1)S(1)}, u32[]{:S(2)}, u32[]{:S(2)}) collective-permute-start(bf16[2,128,128]{2,1,0:T(8,128)(2,1)S(1)} %shard_map.74.refs_0_), channel_id=1, source_target_pairs={{4,0},{5,1},{6,2},{7,3},{0,4},{1,5},{2,6},{3,7},{12,8},{13,9},{14,... | collective-permute-start | bytes 196616 | tf_op jit(solution)/shard_map/ppermute | solution.py:378
  10.5 1.1 %collective-permute-start.3 = (bf16[2,128,128]{2,1,0:T(8,128)(2,1)S(1)}, bf16[2,128,128]{2,1,0:T(8,128)(2,1)S(1)}, u32[]{:S(2)}, u32[]{:S(2)}) collective-permute-start(bf16[2,128,128]{2,1,0:T(8,128)(2,1)S(1)} %shard_map.74.refs_0_), channel_id=1, source_target_pairs={{6,0},{7,1},{4,2},{5,3},{2,4},{3,5},{0,6},{1,7},{14,8},{15,9},{12,... | collective-permute-start | bytes 196616 | tf_op jit(solution)/shard_map/ppermute | solution.py:378
  11.6 0.2 collective-permute-start.4
  11.8 0.4 %collective-permute-done.5.refs_1_ = bf16[2,128,128]{2,1,0:T(8,128)(2,1)S(1)} collective-permute-done((bf16[2,128,128]{2,1,0:T(8,128)(2,1)S(1)}, bf16[2,128,128]{2,1,0:T(8,128)(2,1)S(1)}, u32[]{:S(2)}, u32[]{:S(2)}) %collective-permute-start.5) | collective-permute-done | bytes 65568 | tf_op jit(solution)/shard_map/ppermute | solution.py:378
  12.2 0.7 %shard_map.77.refs_8_ = f32[128,1536]{1,0:T(8,128)S(1)} custom-call(bf16[2,128,128]{2,1,0:T(8,128)(2,1)S(1)} %shard_map.74.refs_0_, bf16[2,128,128]{2,1,0:T(8,128)(2,1)S(1)} %collective-permute-done.5.refs_1_, bf16[1536,1024]{1,0:T(8,128)(2,1)S(1)} %bitcast.7), custom_call_target="tpu_custom_call" | custom-call | flops 65536 | bytes 4096 | tf_op jit(solution)/shard_map/pallas_call | solution.py:204
  12.9 3.5 %collective-permute-done.6.refs_3_ = bf16[144,1024]{1,0:T(8,128)(2,1)S(1)} collective-permute-done((bf16[144,1024]{1,0:T(8,128)(2,1)S(1)}, bf16[144,1024]{1,0:T(8,128)(2,1)S(1)}, u32[]{:S(2)}, u32[]{:S(2)}) %collective-permute-start.6) | collective-permute-done | bytes 294944 | tf_op jit(solution)/shard_map/ppermute | solution.py:24
  16.3 0.0 collective-permute-done.7.input_ref
  16.3 0.1 shard_map.76
  16.4 0.0 collective-permute-done.3.refs_0_
  16.4 0.0 collective-permute-done.4.refs_1_
  16.5 0.8 %shard_map.78 = (bf16[128,1664]{1,0:T(8,128)(2,1)S(1)}, f32[2,128]{1,0:T(2,128)S(1)}) custom-call(bf16[2,128,128]{2,1,0:T(8,128)(2,1)S(1)} %collective-permute-done.3.refs_0_, bf16[2,128,128]{2,1,0:T(8,128)(2,1)S(1)} %collective-permute-done.4.refs_1_, f32[128,1024]{1,0:T(8,128)S(1)} %get-tuple-element.23.refs_2_, f32[128,128]{1,0:T(8,128)S(1)} %get-tuple-element.24.refs_3_, ...), custom_call_target="tpu_custom_call" | custom-call | flops 34359738368 | bytes 33554432 | tf_op jit(solution)/shard_map/pallas_call | solution.py:287
  17.3 2.2 %collective-permute-start.8 = (bf16[128,1664]{1,0:T(8,128)(2,1)S(1)}, bf16[128,1664]{1,0:T(8,128)(2,1)S(1)}, u32[]{:S(2)}, u32[]{:S(2)}) collective-permute-start(bf16[128,1664]{1,0:T(8,128)(2,1)S(1)} %get-tuple-element.26), channel_id=1, source_target_pairs={{8,0},{16,8},{24,16},{0,24},{9,1},{17,9},{25,17},{1,25},{10,2},{18... | collective-permute-start | bytes 1277960 | tf_op jit(solution)/shard_map/ppermute | solution.py:20
  19.5 2.5 %collective-permute-start.10 = (f32[2,128]{1,0:T(2,128)S(1)}, f32[2,128]{1,0:T(2,128)S(1)}, u32[]{:S(2)}, u32[]{:S(2)}) collective-permute-start(f32[2,128]{1,0:T(2,128)S(1)} %get-tuple-element.28), channel_id=1, source_target_pairs={{14,0},{15,1},{12,2},{13,3},{10,4},{11,5},{8,6},{9,7},{22,8},{23,9... | collective-permute-start | bytes 3080 | tf_op jit(solution)/shard_map/ppermute | solution.py:354
  22.0 0.0 collective-permute-start.11
  22.0 2.0 %collective-permute-start.9 = (f32[2,128]{1,0:T(2,128)S(1)}, f32[2,128]{1,0:T(2,128)S(1)}, u32[]{:S(2)}, u32[]{:S(2)}) collective-permute-start(f32[2,128]{1,0:T(2,128)S(1)} %get-tuple-element.28), channel_id=1, source_target_pairs={{10,0},{11,1},{8,2},{9,3},{14,4},{15,5},{12,6},{13,7},{18,8},{19,9... | collective-permute-start | bytes 3080 | tf_op jit(solution)/shard_map/ppermute | solution.py:354
  24.0 1.2 %collective-permute-done.10.refs_1_ = f32[2,128]{1,0:T(2,128)S(1)} collective-permute-done((f32[2,128]{1,0:T(2,128)S(1)}, f32[2,128]{1,0:T(2,128)S(1)}, u32[]{:S(2)}, u32[]{:S(2)}) %collective-permute-start.10) | collective-permute-done | bytes 1056 | tf_op jit(solution)/shard_map/ppermute | solution.py:354
  25.2 1.6 %collective-permute-done.11.refs_2_ = f32[2,128]{1,0:T(2,128)S(1)} collective-permute-done((f32[2,128]{1,0:T(2,128)S(1)}, f32[2,128]{1,0:T(2,128)S(1)}, u32[]{:S(2)}, u32[]{:S(2)}) %collective-permute-start.11) | collective-permute-done | bytes 1056 | tf_op jit(solution)/shard_map/ppermute | solution.py:354
  26.8 0.0 collective-permute-done.9.refs_0_
  26.8 0.0 collective-permute-done.8.scaled_ref
  26.8 1.1 %shard_map.79 = bf16[128,1536]{1,0:T(8,128)(2,1)} custom-call(bf16[128,1664]{1,0:T(8,128)(2,1)S(1)} %collective-permute-done.8.scaled_ref, bf16[128,1536]{1,0:T(8,128)(2,1)S(1)} %collective-permute-done.7.input_ref, f32[2,128]{1,0:T(2,128)S(1)} %collective-permute-done.9.refs_0_, f32[2,128]{1,0:T(2,128)S(1)} %collective-permute-done.10.refs_1_, ...), custom_call_target="tpu_custom_call" | custom-call | tf_op jit(solution)/shard_map/pallas_call | solution.py:329
Async XLA Ops:
  0.0 5.5 %copy-start.1 = (bf16[1,128,1536]{2,1,0:T(8,128)(2,1)S(1)}, bf16[1,128,1536]{2,1,0:T(8,128)(2,1)}, u32[]{:S(2)}) copy-start(bf16[1,128,1536]{2,1,0:T(8,128)(2,1)} %param.12) | copy-start | bytes 1179652
  0.0 7.0 %copy-start = (bf16[1,1536,1024]{2,1,0:T(8,128)(2,1)S(1)}, bf16[1,1536,1024]{2,1,0:T(8,128)(2,1)}, u32[]{:S(2)}) copy-start(bf16[1,1536,1024]{2,1,0:T(8,128)(2,1)} %param.8) | copy-start | bytes 9437188
  0.0 7.0 %copy-start.2 = (f32[1,1536]{1,0:T(1,128)S(1)}, f32[1,1536]{1,0:T(1,128)}, u32[]{:S(2)}) copy-start(f32[1,1536]{1,0:T(1,128)} %refs_7_.1) | copy-start | bytes 18436
  1.0 6.0 %collective-permute-start.2 = (bf16[2,128,128]{2,1,0:T(8,128)(2,1)S(1)}, bf16[2,128,128]{2,1,0:T(8,128)(2,1)S(1)}, u32[]{:S(2)}, u32[]{:S(2)}) collective-permute-start(bf16[2,128,128]{2,1,0:T(8,128)(2,1)S(1)} %get-tuple-element.19.refs_3_), channel_id=1, source_target_pairs={{1,0},{0,1},{3,2},{2,3},{5,4},{4,5},{7,6},{6,7},{9,8},{8,9},{11,10... | collective-permute-start | bytes 196616 | tf_op jit(solution)/shard_map/ppermute | solution.py:24
  3.1 4.6 %collective-permute-start = (bf16[128,128]{1,0:T(8,128)(2,1)S(1)}, bf16[128,128]{1,0:T(8,128)(2,1)S(1)}, u32[]{:S(2)}, u32[]{:S(2)}) collective-permute-start(bf16[128,128]{1,0:T(8,128)(2,1)S(1)} %get-tuple-element.18), channel_id=1, source_target_pairs={{17,0},{16,1},{19,2},{18,3},{21,4},{20,5},{23,6},{22,7},{25,8},{24... | collective-permute-start | bytes 98312 | tf_op jit(solution)/shard_map/ppermute | solution.py:364
  4.3 3.4 %collective-permute-start.1 = (bf16[128,128]{1,0:T(8,128)(2,1)S(1)}, bf16[128,128]{1,0:T(8,128)(2,1)S(1)}, u32[]{:S(2)}, u32[]{:S(2)}) collective-permute-start(bf16[128,128]{1,0:T(8,128)(2,1)S(1)} %get-tuple-element.18), channel_id=1, source_target_pairs={{16,0},{17,1},{18,2},{19,3},{20,4},{21,5},{22,6},{23,7},{24,8},{25... | collective-permute-start | bytes 98312 | tf_op jit(solution)/shard_map/ppermute | solution.py:364
  5.5 10.8 %collective-permute-start.7 = (bf16[128,1536]{1,0:T(8,128)(2,1)S(1)}, bf16[128,1536]{1,0:T(8,128)(2,1)S(1)}, u32[]{:S(2)}, u32[]{:S(2)}) collective-permute-start(bf16[128,1536]{1,0:T(8,128)(2,1)S(1)} %bitcast.9), channel_id=1, source_target_pairs={{8,0},{16,8},{24,16},{0,24},{9,1},{17,9},{25,17},{1,25},{10,2},{18... | collective-permute-start | bytes 1179656 | tf_op jit(solution)/shard_map/ppermute | solution.py:20
  7.6 8.7 %collective-permute-start.6 = (bf16[144,1024]{1,0:T(8,128)(2,1)S(1)}, bf16[144,1024]{1,0:T(8,128)(2,1)S(1)}, u32[]{:S(2)}, u32[]{:S(2)}) collective-permute-start(bf16[144,1024]{1,0:T(8,128)(2,1)S(1)} %get-tuple-element.21), channel_id=1, source_target_pairs={{1,0},{0,1},{3,2},{2,3},{5,4},{4,5},{7,6},{6,7},{9,8},{8,9},{11,10... | collective-permute-start | bytes 884744 | tf_op jit(solution)/shard_map/ppermute | solution.py:24
  8.0 4.2 %collective-permute-start.5 = (bf16[2,128,128]{2,1,0:T(8,128)(2,1)S(1)}, bf16[2,128,128]{2,1,0:T(8,128)(2,1)S(1)}, u32[]{:S(2)}, u32[]{:S(2)}) collective-permute-start(bf16[2,128,128]{2,1,0:T(8,128)(2,1)S(1)} %shard_map.74.refs_0_), channel_id=1, source_target_pairs={{4,0},{5,1},{6,2},{7,3},{0,4},{1,5},{2,6},{3,7},{12,8},{13,9},{14,... | collective-permute-start | bytes 196616 | tf_op jit(solution)/shard_map/ppermute | solution.py:378
  10.5 5.9 %collective-permute-start.3 = (bf16[2,128,128]{2,1,0:T(8,128)(2,1)S(1)}, bf16[2,128,128]{2,1,0:T(8,128)(2,1)S(1)}, u32[]{:S(2)}, u32[]{:S(2)}) collective-permute-start(bf16[2,128,128]{2,1,0:T(8,128)(2,1)S(1)} %shard_map.74.refs_0_), channel_id=1, source_target_pairs={{6,0},{7,1},{4,2},{5,3},{2,4},{3,5},{0,6},{1,7},{14,8},{15,9},{12,... | collective-permute-start | bytes 196616 | tf_op jit(solution)/shard_map/ppermute | solution.py:378
  11.6 4.8 %collective-permute-start.4 = (bf16[2,128,128]{2,1,0:T(8,128)(2,1)S(1)}, bf16[2,128,128]{2,1,0:T(8,128)(2,1)S(1)}, u32[]{:S(2)}, u32[]{:S(2)}) collective-permute-start(bf16[2,128,128]{2,1,0:T(8,128)(2,1)S(1)} %shard_map.74.refs_0_), channel_id=1, source_target_pairs={{2,0},{3,1},{0,2},{1,3},{6,4},{7,5},{4,6},{5,7},{10,8},{11,9},{8,1... | collective-permute-start | bytes 196616 | tf_op jit(solution)/shard_map/ppermute | solution.py:378
  17.3 9.5 %collective-permute-start.8 = (bf16[128,1664]{1,0:T(8,128)(2,1)S(1)}, bf16[128,1664]{1,0:T(8,128)(2,1)S(1)}, u32[]{:S(2)}, u32[]{:S(2)}) collective-permute-start(bf16[128,1664]{1,0:T(8,128)(2,1)S(1)} %get-tuple-element.26), channel_id=1, source_target_pairs={{8,0},{16,8},{24,16},{0,24},{9,1},{17,9},{25,17},{1,25},{10,2},{18... | collective-permute-start | bytes 1277960 | tf_op jit(solution)/shard_map/ppermute | solution.py:20
  19.5 5.7 %collective-permute-start.10 = (f32[2,128]{1,0:T(2,128)S(1)}, f32[2,128]{1,0:T(2,128)S(1)}, u32[]{:S(2)}, u32[]{:S(2)}) collective-permute-start(f32[2,128]{1,0:T(2,128)S(1)} %get-tuple-element.28), channel_id=1, source_target_pairs={{14,0},{15,1},{12,2},{13,3},{10,4},{11,5},{8,6},{9,7},{22,8},{23,9... | collective-permute-start | bytes 3080 | tf_op jit(solution)/shard_map/ppermute | solution.py:354
  22.0 4.8 %collective-permute-start.11 = (f32[2,128]{1,0:T(2,128)S(1)}, f32[2,128]{1,0:T(2,128)S(1)}, u32[]{:S(2)}, u32[]{:S(2)}) collective-permute-start(f32[2,128]{1,0:T(2,128)S(1)} %get-tuple-element.28), channel_id=1, source_target_pairs={{12,0},{13,1},{14,2},{15,3},{8,4},{9,5},{10,6},{11,7},{20,8},{21,9... | collective-permute-start | bytes 3080 | tf_op jit(solution)/shard_map/ppermute | solution.py:354
  22.0 4.8 %collective-permute-start.9 = (f32[2,128]{1,0:T(2,128)S(1)}, f32[2,128]{1,0:T(2,128)S(1)}, u32[]{:S(2)}, u32[]{:S(2)}) collective-permute-start(f32[2,128]{1,0:T(2,128)S(1)} %get-tuple-element.28), channel_id=1, source_target_pairs={{10,0},{11,1},{8,2},{9,3},{14,4},{15,5},{12,6},{13,7},{18,8},{19,9... | collective-permute-start | bytes 3080 | tf_op jit(solution)/shard_map/ppermute | solution.py:354

commit v6 on v2

--- a/solution.py
+++ b/solution.py
@@ -9,7 +9,7 @@
 
 D = 12288
 LANES = 128
-PIECES = (0, 3, 5, 7, 8)
+PIECES = (0, 1, 2, 3, 4, 5, 6, 7, 8)
 EXTRA = 16
 HIDES = pl.CostEstimate(flops=1 << 35, bytes_accessed=1 << 25, transcendentals=0)
 

time: 27.4 us -> 27.4 us (level)
  no operation moved by 1% of the time
where the time goes in v6:
time: 27.4 us; the launch traced here: 27.3 us
  starting transfers between devices  16.4 us (60%)
  waiting for transfers between devices  6.39 us (23%)
  Pallas kernels  4.41 us (16%)
    ppermute x5, starting transfers between devices, swapped(): lax.ppermute(block, axis, [(i ^ mask, i) for i in range(lax.axis_size(axi...  6.14 us
    ppermute x3, starting transfers between devices, handed_over(): return lax.ppermute(block, ('section', 'tp'), route)  4.39 us
    ppermute x5, waiting for transfers between devices, swapped(): lax.ppermute(block, axis, [(i ^ mask, i) for i in range(lax.axis_size(axi...  4.12 us
    ppermute x2, starting transfers between devices, passed_along(): return lax.ppermute(block, axis, route)  3.5 us
    ppermute x2, starting transfers between devices, fetched(): return lax.ppermute(block, ('section', 'tp'), route)  2.36 us
    ppermute x3, waiting for transfers between devices, handed_over(): return lax.ppermute(block, ('section', 'tp'), route)  2.26 us
    pallas_call x1, Pallas kernels, finish(): pl.pallas_call(finish_kernel, out_shape=pltpu.HBM(inputs.shape, jnp.bfloa...  1.07 us
    pallas_call x1, Pallas kernels, pack(): pl.pallas_call(pack_kernel, out_shape=(pltpu.VMEM((2, *own.shape), own.dt...  0.98 us
  transfers between devices with their start and end apart: 12, of which 5 were waited for; matrix products, arithmetic and copies ran while one was open for 0% of the time, Pallas kernels for 6%

profile of v6, /device:TPU:1, one launch (start us, length us, event | category | flops | bytes accessed | tf_op | source)
XLA Modules:
  0.0 27.3 jit_solution(2935493855361331461)
XLA Ops:
  0.0 0.0 copy-start.1
  0.0 0.0 copy-start
  0.0 0.0 copy-start.2
  0.0 1.0 %shard_map.73 = (bf16[2,128,128]{2,1,0:T(8,128)(2,1)S(1)}, bf16[128,128]{1,0:T(8,128)(2,1)S(1)}, bf16[128,128]{1,0:T(8,128)(2,1)S(1)}) custom-call(bf16[128,128]{1,0:T(8,128)(2,1)} %bitcast.12, bf16[128,128]{1,0:T(8,128)(2,1)} %bitcast.13, bf16[128,128]{1,0:T(8,128)(2,1)} %bitcast.14, s32[1,4]{1,0:T(1,128)} %evicted_ref.1), custom_call_target="tpu_custom_call" | custom-call | flops 34359738368 | bytes 33554432 | tf_op jit(solution)/shard_map/pallas_call | solution.py:87
  1.0 2.1 %collective-permute-start.2 = (bf16[2,128,128]{2,1,0:T(8,128)(2,1)S(1)}, bf16[2,128,128]{2,1,0:T(8,128)(2,1)S(1)}, u32[]{:S(2)}, u32[]{:S(2)}) collective-permute-start(bf16[2,128,128]{2,1,0:T(8,128)(2,1)S(1)} %get-tuple-element.19.refs_3_), channel_id=1, source_target_pairs={{1,0},{0,1},{3,2},{2,3},{5,4},{4,5},{7,6},{6,7},{9,8},{8,9},{11,10... | collective-permute-start | bytes 196616 | tf_op jit(solution)/shard_map/ppermute | solution.py:24
  3.1 1.2 %collective-permute-start = (bf16[128,128]{1,0:T(8,128)(2,1)S(1)}, bf16[128,128]{1,0:T(8,128)(2,1)S(1)}, u32[]{:S(2)}, u32[]{:S(2)}) collective-permute-start(bf16[128,128]{1,0:T(8,128)(2,1)S(1)} %get-tuple-element.18), channel_id=1, source_target_pairs={{17,0},{16,1},{19,2},{18,3},{21,4},{20,5},{23,6},{22,7},{25,8},{24... | collective-permute-start | bytes 98312 | tf_op jit(solution)/shard_map/ppermute | solution.py:364
  4.3 1.2 %collective-permute-start.1 = (bf16[128,128]{1,0:T(8,128)(2,1)S(1)}, bf16[128,128]{1,0:T(8,128)(2,1)S(1)}, u32[]{:S(2)}, u32[]{:S(2)}) collective-permute-start(bf16[128,128]{1,0:T(8,128)(2,1)S(1)} %get-tuple-element.18), channel_id=1, source_target_pairs={{16,0},{17,1},{18,2},{19,3},{20,4},{21,5},{22,6},{23,7},{24,8},{25... | collective-permute-start | bytes 98312 | tf_op jit(solution)/shard_map/ppermute | solution.py:364
  5.5 0.0 copy-done.1
  5.5 1.5 %collective-permute-start.7 = (bf16[128,1536]{1,0:T(8,128)(2,1)S(1)}, bf16[128,1536]{1,0:T(8,128)(2,1)S(1)}, u32[]{:S(2)}, u32[]{:S(2)}) collective-permute-start(bf16[128,1536]{1,0:T(8,128)(2,1)S(1)} %bitcast.9), channel_id=1, source_target_pairs={{8,0},{16,8},{24,16},{0,24},{9,1},{17,9},{25,17},{1,25},{10,2},{18... | collective-permute-start | bytes 1179656 | tf_op jit(solution)/shard_map/ppermute | solution.py:20
  7.0 0.0 collective-permute-done.2.refs_2_.first_ref
  7.0 0.0 copy-done
  7.0 0.0 copy-done.2
  7.0 0.6 %shard_map.75 = (bf16[144,1024]{1,0:T(8,128)(2,1)S(1)}, f32[144,1024]{1,0:T(8,128)S(1)}) custom-call(bf16[1536,1024]{1,0:T(8,128)(2,1)S(1)} %bitcast.6, bf16[128,1536]{1,0:T(8,128)(2,1)S(1)} %bitcast.10, f32[1,1536]{1,0:T(1,128)S(1)} %copy-done.2, bf16[2,128,128]{2,1,0:T(8,128)(2,1)S(1)} %collective-permute-done.2.refs_2_.first_ref), custom_call_target="tpu_custom_call" | custom-call | flops 34359738368 | bytes 33554432 | tf_op jit(solution)/shard_map/pallas_call | solution.py:120
  7.6 0.1 collective-permute-start.6
  7.7 0.0 collective-permute-done.refs_0_
  7.7 0.0 collective-permute-done.1.refs_1_
  7.7 0.2 shard_map.74.refs_0_
  8.0 3.6 %collective-permute-start.5 = (bf16[2,128,128]{2,1,0:T(8,128)(2,1)S(1)}, bf16[2,128,128]{2,1,0:T(8,128)(2,1)S(1)}, u32[]{:S(2)}, u32[]{:S(2)}) collective-permute-start(bf16[2,128,128]{2,1,0:T(8,128)(2,1)S(1)} %shard_map.74.refs_0_), channel_id=1, source_target_pairs={{6,0},{7,1},{4,2},{5,3},{2,4},{3,5},{0,6},{1,7},{14,8},{15,9},{12,... | collective-permute-start | bytes 196616 | tf_op jit(solution)/shard_map/ppermute | solution.py:24
  11.5 0.0 collective-permute-start.3
  11.5 0.4 %collective-permute-start.4 = (bf16[2,128,128]{2,1,0:T(8,128)(2,1)S(1)}, bf16[2,128,128]{2,1,0:T(8,128)(2,1)S(1)}, u32[]{:S(2)}, u32[]{:S(2)}) collective-permute-start(bf16[2,128,128]{2,1,0:T(8,128)(2,1)S(1)} %shard_map.74.refs_0_), channel_id=1, source_target_pairs={{2,0},{3,1},{0,2},{1,3},{6,4},{7,5},{4,6},{5,7},{10,8},{11,9},{8,1... | collective-permute-start | bytes 196616 | tf_op jit(solution)/shard_map/ppermute | solution.py:24
  11.9 1.3 %collective-permute-done.5.refs_1_ = bf16[2,128,128]{2,1,0:T(8,128)(2,1)S(1)} collective-permute-done((bf16[2,128,128]{2,1,0:T(8,128)(2,1)S(1)}, bf16[2,128,128]{2,1,0:T(8,128)(2,1)S(1)}, u32[]{:S(2)}, u32[]{:S(2)}) %collective-permute-start.5) | collective-permute-done | bytes 65568 | tf_op jit(solution)/shard_map/ppermute | solution.py:24
  13.2 0.7 %shard_map.77.refs_8_ = f32[128,1536]{1,0:T(8,128)S(1)} custom-call(bf16[2,128,128]{2,1,0:T(8,128)(2,1)S(1)} %shard_map.74.refs_0_, bf16[2,128,128]{2,1,0:T(8,128)(2,1)S(1)} %collective-permute-done.5.refs_1_, bf16[1536,1024]{1,0:T(8,128)(2,1)S(1)} %bitcast.7), custom_call_target="tpu_custom_call" | custom-call | flops 65536 | bytes 4096 | tf_op jit(solution)/shard_map/pallas_call | solution.py:204
  13.9 2.5 %collective-permute-done.6.refs_3_ = bf16[144,1024]{1,0:T(8,128)(2,1)S(1)} collective-permute-done((bf16[144,1024]{1,0:T(8,128)(2,1)S(1)}, bf16[144,1024]{1,0:T(8,128)(2,1)S(1)}, u32[]{:S(2)}, u32[]{:S(2)}) %collective-permute-start.6) | collective-permute-done | bytes 294944 | tf_op jit(solution)/shard_map/ppermute | solution.py:24
  16.3 0.0 collective-permute-done.7.input_ref
  16.3 0.1 shard_map.76
  16.4 0.4 %collective-permute-done.3.refs_0_ = bf16[2,128,128]{2,1,0:T(8,128)(2,1)S(1)} collective-permute-done((bf16[2,128,128]{2,1,0:T(8,128)(2,1)S(1)}, bf16[2,128,128]{2,1,0:T(8,128)(2,1)S(1)}, u32[]{:S(2)}, u32[]{:S(2)}) %collective-permute-start.3) | collective-permute-done | bytes 65568 | tf_op jit(solution)/shard_map/ppermute | solution.py:24
  16.8 0.0 collective-permute-done.4.refs_1_
  16.8 0.8 %shard_map.78 = (bf16[128,1664]{1,0:T(8,128)(2,1)S(1)}, f32[2,128]{1,0:T(2,128)S(1)}) custom-call(bf16[2,128,128]{2,1,0:T(8,128)(2,1)S(1)} %collective-permute-done.3.refs_0_, bf16[2,128,128]{2,1,0:T(8,128)(2,1)S(1)} %collective-permute-done.4.refs_1_, f32[128,1024]{1,0:T(8,128)S(1)} %get-tuple-element.23.refs_2_, f32[128,128]{1,0:T(8,128)S(1)} %get-tuple-element.24.refs_3_, ...), custom_call_target="tpu_custom_call" | custom-call | flops 34359738368 | bytes 33554432 | tf_op jit(solution)/shard_map/pallas_call | solution.py:287
  17.6 2.0 %collective-permute-start.8 = (bf16[128,1664]{1,0:T(8,128)(2,1)S(1)}, bf16[128,1664]{1,0:T(8,128)(2,1)S(1)}, u32[]{:S(2)}, u32[]{:S(2)}) collective-permute-start(bf16[128,1664]{1,0:T(8,128)(2,1)S(1)} %get-tuple-element.26), channel_id=1, source_target_pairs={{8,0},{16,8},{24,16},{0,24},{9,1},{17,9},{25,17},{1,25},{10,2},{18... | collective-permute-start | bytes 1277960 | tf_op jit(solution)/shard_map/ppermute | solution.py:20
  19.6 1.9 %collective-permute-start.10 = (f32[2,128]{1,0:T(2,128)S(1)}, f32[2,128]{1,0:T(2,128)S(1)}, u32[]{:S(2)}, u32[]{:S(2)}) collective-permute-start(f32[2,128]{1,0:T(2,128)S(1)} %get-tuple-element.28), channel_id=1, source_target_pairs={{14,0},{15,1},{12,2},{13,3},{10,4},{11,5},{8,6},{9,7},{22,8},{23,9... | collective-permute-start | bytes 3080 | tf_op jit(solution)/shard_map/ppermute | solution.py:354
  21.4 0.4 %collective-permute-start.11 = (f32[2,128]{1,0:T(2,128)S(1)}, f32[2,128]{1,0:T(2,128)S(1)}, u32[]{:S(2)}, u32[]{:S(2)}) collective-permute-start(f32[2,128]{1,0:T(2,128)S(1)} %get-tuple-element.28), channel_id=1, source_target_pairs={{12,0},{13,1},{14,2},{15,3},{8,4},{9,5},{10,6},{11,7},{20,8},{21,9... | collective-permute-start | bytes 3080 | tf_op jit(solution)/shard_map/ppermute | solution.py:354
  21.8 2.1 %collective-permute-start.9 = (f32[2,128]{1,0:T(2,128)S(1)}, f32[2,128]{1,0:T(2,128)S(1)}, u32[]{:S(2)}, u32[]{:S(2)}) collective-permute-start(f32[2,128]{1,0:T(2,128)S(1)} %get-tuple-element.28), channel_id=1, source_target_pairs={{10,0},{11,1},{8,2},{9,3},{14,4},{15,5},{12,6},{13,7},{18,8},{19,9... | collective-permute-start | bytes 3080 | tf_op jit(solution)/shard_map/ppermute | solution.py:354
  24.0 1.3 %collective-permute-done.10.refs_1_ = f32[2,128]{1,0:T(2,128)S(1)} collective-permute-done((f32[2,128]{1,0:T(2,128)S(1)}, f32[2,128]{1,0:T(2,128)S(1)}, u32[]{:S(2)}, u32[]{:S(2)}) %collective-permute-start.10) | collective-permute-done | bytes 1056 | tf_op jit(solution)/shard_map/ppermute | solution.py:354
  25.3 1.0 %collective-permute-done.11.refs_2_ = f32[2,128]{1,0:T(2,128)S(1)} collective-permute-done((f32[2,128]{1,0:T(2,128)S(1)}, f32[2,128]{1,0:T(2,128)S(1)}, u32[]{:S(2)}, u32[]{:S(2)}) %collective-permute-start.11) | collective-permute-done | bytes 1056 | tf_op jit(solution)/shard_map/ppermute | solution.py:354
  26.2 0.0 collective-permute-done.9.refs_0_
  26.2 0.0 collective-permute-done.8.scaled_ref
  26.2 1.1 %shard_map.79 = bf16[128,1536]{1,0:T(8,128)(2,1)} custom-call(bf16[128,1664]{1,0:T(8,128)(2,1)S(1)} %collective-permute-done.8.scaled_ref, bf16[128,1536]{1,0:T(8,128)(2,1)S(1)} %collective-permute-done.7.input_ref, f32[2,128]{1,0:T(2,128)S(1)} %collective-permute-done.9.refs_0_, f32[2,128]{1,0:T(2,128)S(1)} %collective-permute-done.10.refs_1_, ...), custom_call_target="tpu_custom_call" | custom-call | tf_op jit(solution)/shard_map/pallas_call | solution.py:329
Async XLA Ops:
  0.0 5.5 %copy-start.1 = (bf16[1,128,1536]{2,1,0:T(8,128)(2,1)S(1)}, bf16[1,128,1536]{2,1,0:T(8,128)(2,1)}, u32[]{:S(2)}) copy-start(bf16[1,128,1536]{2,1,0:T(8,128)(2,1)} %param.12) | copy-start | bytes 1179652
  0.0 7.0 %copy-start = (bf16[1,1536,1024]{2,1,0:T(8,128)(2,1)S(1)}, bf16[1,1536,1024]{2,1,0:T(8,128)(2,1)}, u32[]{:S(2)}) copy-start(bf16[1,1536,1024]{2,1,0:T(8,128)(2,1)} %param.8) | copy-start | bytes 9437188
  0.0 7.0 %copy-start.2 = (f32[1,1536]{1,0:T(1,128)S(1)}, f32[1,1536]{1,0:T(1,128)}, u32[]{:S(2)}) copy-start(f32[1,1536]{1,0:T(1,128)} %refs_7_.1) | copy-start | bytes 18436
  1.0 6.0 %collective-permute-start.2 = (bf16[2,128,128]{2,1,0:T(8,128)(2,1)S(1)}, bf16[2,128,128]{2,1,0:T(8,128)(2,1)S(1)}, u32[]{:S(2)}, u32[]{:S(2)}) collective-permute-start(bf16[2,128,128]{2,1,0:T(8,128)(2,1)S(1)} %get-tuple-element.19.refs_3_), channel_id=1, source_target_pairs={{1,0},{0,1},{3,2},{2,3},{5,4},{4,5},{7,6},{6,7},{9,8},{8,9},{11,10... | collective-permute-start | bytes 196616 | tf_op jit(solution)/shard_map/ppermute | solution.py:24
  3.1 4.6 %collective-permute-start = (bf16[128,128]{1,0:T(8,128)(2,1)S(1)}, bf16[128,128]{1,0:T(8,128)(2,1)S(1)}, u32[]{:S(2)}, u32[]{:S(2)}) collective-permute-start(bf16[128,128]{1,0:T(8,128)(2,1)S(1)} %get-tuple-element.18), channel_id=1, source_target_pairs={{17,0},{16,1},{19,2},{18,3},{21,4},{20,5},{23,6},{22,7},{25,8},{24... | collective-permute-start | bytes 98312 | tf_op jit(solution)/shard_map/ppermute | solution.py:364
  4.3 3.4 %collective-permute-start.1 = (bf16[128,128]{1,0:T(8,128)(2,1)S(1)}, bf16[128,128]{1,0:T(8,128)(2,1)S(1)}, u32[]{:S(2)}, u32[]{:S(2)}) collective-permute-start(bf16[128,128]{1,0:T(8,128)(2,1)S(1)} %get-tuple-element.18), channel_id=1, source_target_pairs={{16,0},{17,1},{18,2},{19,3},{20,4},{21,5},{22,6},{23,7},{24,8},{25... | collective-permute-start | bytes 98312 | tf_op jit(solution)/shard_map/ppermute | solution.py:364
  5.5 10.8 %collective-permute-start.7 = (bf16[128,1536]{1,0:T(8,128)(2,1)S(1)}, bf16[128,1536]{1,0:T(8,128)(2,1)S(1)}, u32[]{:S(2)}, u32[]{:S(2)}) collective-permute-start(bf16[128,1536]{1,0:T(8,128)(2,1)S(1)} %bitcast.9), channel_id=1, source_target_pairs={{8,0},{16,8},{24,16},{0,24},{9,1},{17,9},{25,17},{1,25},{10,2},{18... | collective-permute-start | bytes 1179656 | tf_op jit(solution)/shard_map/ppermute | solution.py:20
  7.6 8.7 %collective-permute-start.6 = (bf16[144,1024]{1,0:T(8,128)(2,1)S(1)}, bf16[144,1024]{1,0:T(8,128)(2,1)S(1)}, u32[]{:S(2)}, u32[]{:S(2)}) collective-permute-start(bf16[144,1024]{1,0:T(8,128)(2,1)S(1)} %get-tuple-element.21), channel_id=1, source_target_pairs={{1,0},{0,1},{3,2},{2,3},{5,4},{4,5},{7,6},{6,7},{9,8},{8,9},{11,10... | collective-permute-start | bytes 884744 | tf_op jit(solution)/shard_map/ppermute | solution.py:24
  8.0 5.2 %collective-permute-start.5 = (bf16[2,128,128]{2,1,0:T(8,128)(2,1)S(1)}, bf16[2,128,128]{2,1,0:T(8,128)(2,1)S(1)}, u32[]{:S(2)}, u32[]{:S(2)}) collective-permute-start(bf16[2,128,128]{2,1,0:T(8,128)(2,1)S(1)} %shard_map.74.refs_0_), channel_id=1, source_target_pairs={{6,0},{7,1},{4,2},{5,3},{2,4},{3,5},{0,6},{1,7},{14,8},{15,9},{12,... | collective-permute-start | bytes 196616 | tf_op jit(solution)/shard_map/ppermute | solution.py:24
  11.5 5.3 %collective-permute-start.3 = (bf16[2,128,128]{2,1,0:T(8,128)(2,1)S(1)}, bf16[2,128,128]{2,1,0:T(8,128)(2,1)S(1)}, u32[]{:S(2)}, u32[]{:S(2)}) collective-permute-start(bf16[2,128,128]{2,1,0:T(8,128)(2,1)S(1)} %shard_map.74.refs_0_), channel_id=1, source_target_pairs={{4,0},{5,1},{6,2},{7,3},{0,4},{1,5},{2,6},{3,7},{12,8},{13,9},{14,... | collective-permute-start | bytes 196616 | tf_op jit(solution)/shard_map/ppermute | solution.py:24
  11.5 5.3 %collective-permute-start.4 = (bf16[2,128,128]{2,1,0:T(8,128)(2,1)S(1)}, bf16[2,128,128]{2,1,0:T(8,128)(2,1)S(1)}, u32[]{:S(2)}, u32[]{:S(2)}) collective-permute-start(bf16[2,128,128]{2,1,0:T(8,128)(2,1)S(1)} %shard_map.74.refs_0_), channel_id=1, source_target_pairs={{2,0},{3,1},{0,2},{1,3},{6,4},{7,5},{4,6},{5,7},{10,8},{11,9},{8,1... | collective-permute-start | bytes 196616 | tf_op jit(solution)/shard_map/ppermute | solution.py:24
  17.6 8.7 %collective-permute-start.8 = (bf16[128,1664]{1,0:T(8,128)(2,1)S(1)}, bf16[128,1664]{1,0:T(8,128)(2,1)S(1)}, u32[]{:S(2)}, u32[]{:S(2)}) collective-permute-start(bf16[128,1664]{1,0:T(8,128)(2,1)S(1)} %get-tuple-element.26), channel_id=1, source_target_pairs={{8,0},{16,8},{24,16},{0,24},{9,1},{17,9},{25,17},{1,25},{10,2},{18... | collective-permute-start | bytes 1277960 | tf_op jit(solution)/shard_map/ppermute | solution.py:20
  19.6 5.7 %collective-permute-start.10 = (f32[2,128]{1,0:T(2,128)S(1)}, f32[2,128]{1,0:T(2,128)S(1)}, u32[]{:S(2)}, u32[]{:S(2)}) collective-permute-start(f32[2,128]{1,0:T(2,128)S(1)} %get-tuple-element.28), channel_id=1, source_target_pairs={{14,0},{15,1},{12,2},{13,3},{10,4},{11,5},{8,6},{9,7},{22,8},{23,9... | collective-permute-start | bytes 3080 | tf_op jit(solution)/shard_map/ppermute | solution.py:354
  21.4 4.8 %collective-permute-start.11 = (f32[2,128]{1,0:T(2,128)S(1)}, f32[2,128]{1,0:T(2,128)S(1)}, u32[]{:S(2)}, u32[]{:S(2)}) collective-permute-start(f32[2,128]{1,0:T(2,128)S(1)} %get-tuple-element.28), channel_id=1, source_target_pairs={{12,0},{13,1},{14,2},{15,3},{8,4},{9,5},{10,6},{11,7},{20,8},{21,9... | collective-permute-start | bytes 3080 | tf_op jit(solution)/shard_map/ppermute | solution.py:354
  21.8 4.4 %collective-permute-start.9 = (f32[2,128]{1,0:T(2,128)S(1)}, f32[2,128]{1,0:T(2,128)S(1)}, u32[]{:S(2)}, u32[]{:S(2)}) collective-permute-start(f32[2,128]{1,0:T(2,128)S(1)} %get-tuple-element.28), channel_id=1, source_target_pairs={{10,0},{11,1},{8,2},{9,3},{14,4},{15,5},{12,6},{13,7},{18,8},{19,9... | collective-permute-start | bytes 3080 | tf_op jit(solution)/shard_map/ppermute | solution.py:354

commit v7 on v3

--- a/solution.py
+++ b/solution.py
@@ -9,7 +9,7 @@
 
 D = 12288
 LANES = 128
-PIECES = (0, 3, 5, 7, 8)
+PIECES = (0, 1, 2, 3, 4, 5, 6, 7, 8)
 EXTRA = 16
 SHORT = pl.CostEstimate(flops=1 << 16, bytes_accessed=1 << 12, transcendentals=0)
 HIDES = pl.CostEstimate(flops=1 << 35, bytes_accessed=1 << 25, transcendentals=0)

time: 27.4 us -> 27.4 us (level)
  no operation moved by 1% of the time
where the time goes in v7:
time: 27.4 us; the launch traced here: 27.3 us
  starting transfers between devices  16.4 us (60%)
  waiting for transfers between devices  6.38 us (23%)
  Pallas kernels  4.42 us (16%)
    ppermute x5, starting transfers between devices, swapped(): lax.ppermute(block, axis, [(i ^ mask, i) for i in range(lax.axis_size(axi...  6.15 us
    ppermute x3, starting transfers between devices, handed_over(): return lax.ppermute(block, ('section', 'tp'), route)  4.39 us
    ppermute x5, waiting for transfers between devices, swapped(): lax.ppermute(block, axis, [(i ^ mask, i) for i in range(lax.axis_size(axi...  4.11 us
    ppermute x2, starting transfers between devices, passed_along(): return lax.ppermute(block, axis, route)  3.5 us
    ppermute x2, starting transfers between devices, fetched(): return lax.ppermute(block, ('section', 'tp'), route)  2.36 us
    ppermute x3, waiting for transfers between devices, handed_over(): return lax.ppermute(block, ('section', 'tp'), route)  2.26 us
    pallas_call x1, Pallas kernels, finish(): pl.pallas_call(finish_kernel, out_shape=pltpu.HBM(inputs.shape, jnp.bfloa...  1.07 us
    pallas_call x1, Pallas kernels, pack(): pl.pallas_call(pack_kernel, out_shape=(pltpu.VMEM((2, *own.shape), own.dt...  0.98 us
  transfers between devices with their start and end apart: 12, of which 5 were waited for; matrix products, arithmetic and copies ran while one was open for 0% of the time, Pallas kernels for 6%

profile of v7, /device:TPU:1, one launch (start us, length us, event | category | flops | bytes accessed | tf_op | source)
XLA Modules:
  0.0 27.3 jit_solution(10511982292603501463)
XLA Ops:
  0.0 0.0 copy-start.1
  0.0 0.0 copy-start
  0.0 0.0 copy-start.2
  0.0 1.0 %shard_map.73 = (bf16[2,128,128]{2,1,0:T(8,128)(2,1)S(1)}, bf16[128,128]{1,0:T(8,128)(2,1)S(1)}, bf16[128,128]{1,0:T(8,128)(2,1)S(1)}) custom-call(bf16[128,128]{1,0:T(8,128)(2,1)} %bitcast.12, bf16[128,128]{1,0:T(8,128)(2,1)} %bitcast.13, bf16[128,128]{1,0:T(8,128)(2,1)} %bitcast.14, s32[1,4]{1,0:T(1,128)} %evicted_ref.1), custom_call_target="tpu_custom_call" | custom-call | flops 34359738368 | bytes 33554432 | tf_op jit(solution)/shard_map/pallas_call | solution.py:88
  1.0 2.1 %collective-permute-start.2 = (bf16[2,128,128]{2,1,0:T(8,128)(2,1)S(1)}, bf16[2,128,128]{2,1,0:T(8,128)(2,1)S(1)}, u32[]{:S(2)}, u32[]{:S(2)}) collective-permute-start(bf16[2,128,128]{2,1,0:T(8,128)(2,1)S(1)} %get-tuple-element.22.refs_3_), channel_id=1, source_target_pairs={{1,0},{0,1},{3,2},{2,3},{5,4},{4,5},{7,6},{6,7},{9,8},{8,9},{11,10... | collective-permute-start | bytes 196616 | tf_op jit(solution)/shard_map/ppermute | solution.py:25
  3.1 1.2 %collective-permute-start.1 = (bf16[128,128]{1,0:T(8,128)(2,1)S(1)}, bf16[128,128]{1,0:T(8,128)(2,1)S(1)}, u32[]{:S(2)}, u32[]{:S(2)}) collective-permute-start(bf16[128,128]{1,0:T(8,128)(2,1)S(1)} %get-tuple-element.20), channel_id=1, source_target_pairs={{17,0},{16,1},{19,2},{18,3},{21,4},{20,5},{23,6},{22,7},{25,8},{24... | collective-permute-start | bytes 98312 | tf_op jit(solution)/shard_map/ppermute | solution.py:364
  4.3 1.2 %collective-permute-start = (bf16[128,128]{1,0:T(8,128)(2,1)S(1)}, bf16[128,128]{1,0:T(8,128)(2,1)S(1)}, u32[]{:S(2)}, u32[]{:S(2)}) collective-permute-start(bf16[128,128]{1,0:T(8,128)(2,1)S(1)} %get-tuple-element.20), channel_id=1, source_target_pairs={{16,0},{17,1},{18,2},{19,3},{20,4},{21,5},{22,6},{23,7},{24,8},{25... | collective-permute-start | bytes 98312 | tf_op jit(solution)/shard_map/ppermute | solution.py:364
  5.5 0.0 copy-done.1
  5.5 1.5 %collective-permute-start.7 = (bf16[128,1536]{1,0:T(8,128)(2,1)S(1)}, bf16[128,1536]{1,0:T(8,128)(2,1)S(1)}, u32[]{:S(2)}, u32[]{:S(2)}) collective-permute-start(bf16[128,1536]{1,0:T(8,128)(2,1)S(1)} %bitcast.9), channel_id=1, source_target_pairs={{8,0},{16,8},{24,16},{0,24},{9,1},{17,9},{25,17},{1,25},{10,2},{18... | collective-permute-start | bytes 1179656 | tf_op jit(solution)/shard_map/ppermute | solution.py:21
  7.0 0.0 copy-done
  7.0 0.0 copy-done.2
  7.0 0.6 %shard_map.74 = (bf16[144,1024]{1,0:T(8,128)(2,1)S(1)}, f32[144,1024]{1,0:T(8,128)S(1)}) custom-call(bf16[1536,1024]{1,0:T(8,128)(2,1)S(1)} %bitcast.6, bf16[128,1536]{1,0:T(8,128)(2,1)S(1)} %bitcast.10, f32[1,1536]{1,0:T(1,128)S(1)} %copy-done.2), custom_call_target="tpu_custom_call" | custom-call | flops 65536 | bytes 4096 | tf_op jit(solution)/shard_map/pallas_call | solution.py:120
  7.6 0.0 collective-permute-done.2.refs_2_
  7.6 0.1 collective-permute-start.6
  7.7 0.0 collective-permute-done.1.refs_1_
  7.7 0.0 collective-permute-done.refs_0_
  7.7 0.2 shard_map.75.refs_0_
  8.0 3.6 %collective-permute-start.5 = (bf16[2,128,128]{2,1,0:T(8,128)(2,1)S(1)}, bf16[2,128,128]{2,1,0:T(8,128)(2,1)S(1)}, u32[]{:S(2)}, u32[]{:S(2)}) collective-permute-start(bf16[2,128,128]{2,1,0:T(8,128)(2,1)S(1)} %shard_map.75.refs_0_), channel_id=1, source_target_pairs={{6,0},{7,1},{4,2},{5,3},{2,4},{3,5},{0,6},{1,7},{14,8},{15,9},{12,... | collective-permute-start | bytes 196616 | tf_op jit(solution)/shard_map/ppermute | solution.py:25
  11.5 0.0 collective-permute-start.4
  11.5 0.4 %collective-permute-start.3 = (bf16[2,128,128]{2,1,0:T(8,128)(2,1)S(1)}, bf16[2,128,128]{2,1,0:T(8,128)(2,1)S(1)}, u32[]{:S(2)}, u32[]{:S(2)}) collective-permute-start(bf16[2,128,128]{2,1,0:T(8,128)(2,1)S(1)} %shard_map.75.refs_0_), channel_id=1, source_target_pairs={{2,0},{3,1},{0,2},{1,3},{6,4},{7,5},{4,6},{5,7},{10,8},{11,9},{8,1... | collective-permute-start | bytes 196616 | tf_op jit(solution)/shard_map/ppermute | solution.py:25
  11.9 1.3 %collective-permute-done.5.refs_1_ = bf16[2,128,128]{2,1,0:T(8,128)(2,1)S(1)} collective-permute-done((bf16[2,128,128]{2,1,0:T(8,128)(2,1)S(1)}, bf16[2,128,128]{2,1,0:T(8,128)(2,1)S(1)}, u32[]{:S(2)}, u32[]{:S(2)}) %collective-permute-start.5) | collective-permute-done | bytes 65568 | tf_op jit(solution)/shard_map/ppermute | solution.py:25
  13.2 0.7 %shard_map.77.refs_8_ = f32[128,1536]{1,0:T(8,128)S(1)} custom-call(bf16[2,128,128]{2,1,0:T(8,128)(2,1)S(1)} %shard_map.75.refs_0_, bf16[2,128,128]{2,1,0:T(8,128)(2,1)S(1)} %collective-permute-done.5.refs_1_, bf16[1536,1024]{1,0:T(8,128)(2,1)S(1)} %bitcast.7), custom_call_target="tpu_custom_call" | custom-call | flops 65536 | bytes 4096 | tf_op jit(solution)/shard_map/pallas_call | solution.py:204
  13.9 2.5 %collective-permute-done.6.refs_3_ = bf16[144,1024]{1,0:T(8,128)(2,1)S(1)} collective-permute-done((bf16[144,1024]{1,0:T(8,128)(2,1)S(1)}, bf16[144,1024]{1,0:T(8,128)(2,1)S(1)}, u32[]{:S(2)}, u32[]{:S(2)}) %collective-permute-start.6) | collective-permute-done | bytes 294944 | tf_op jit(solution)/shard_map/ppermute | solution.py:25
  16.3 0.0 collective-permute-done.7.input_ref
  16.3 0.1 shard_map.76
  16.4 0.3 %collective-permute-done.4.refs_1_ = bf16[2,128,128]{2,1,0:T(8,128)(2,1)S(1)} collective-permute-done((bf16[2,128,128]{2,1,0:T(8,128)(2,1)S(1)}, bf16[2,128,128]{2,1,0:T(8,128)(2,1)S(1)}, u32[]{:S(2)}, u32[]{:S(2)}) %collective-permute-start.4) | collective-permute-done | bytes 65568 | tf_op jit(solution)/shard_map/ppermute | solution.py:25
  16.8 0.0 collective-permute-done.3.refs_0_
  16.8 0.8 %shard_map.78 = (bf16[128,1664]{1,0:T(8,128)(2,1)S(1)}, f32[2,128]{1,0:T(2,128)S(1)}) custom-call(bf16[2,128,128]{2,1,0:T(8,128)(2,1)S(1)} %collective-permute-done.3.refs_0_, bf16[2,128,128]{2,1,0:T(8,128)(2,1)S(1)} %collective-permute-done.4.refs_1_, f32[128,1024]{1,0:T(8,128)S(1)} %get-tuple-element.27.refs_2_, f32[128,128]{1,0:T(8,128)S(1)} %get-tuple-element.28.refs_3_, ...), custom_call_target="tpu_custom_call" | custom-call | flops 34359738368 | bytes 33554432 | tf_op jit(solution)/shard_map/pallas_call | solution.py:287
  17.6 2.0 %collective-permute-start.8 = (bf16[128,1664]{1,0:T(8,128)(2,1)S(1)}, bf16[128,1664]{1,0:T(8,128)(2,1)S(1)}, u32[]{:S(2)}, u32[]{:S(2)}) collective-permute-start(bf16[128,1664]{1,0:T(8,128)(2,1)S(1)} %get-tuple-element.30), channel_id=1, source_target_pairs={{8,0},{16,8},{24,16},{0,24},{9,1},{17,9},{25,17},{1,25},{10,2},{18... | collective-permute-start | bytes 1277960 | tf_op jit(solution)/shard_map/ppermute | solution.py:21
  19.6 1.9 %collective-permute-start.11 = (f32[2,128]{1,0:T(2,128)S(1)}, f32[2,128]{1,0:T(2,128)S(1)}, u32[]{:S(2)}, u32[]{:S(2)}) collective-permute-start(f32[2,128]{1,0:T(2,128)S(1)} %get-tuple-element.32), channel_id=1, source_target_pairs={{14,0},{15,1},{12,2},{13,3},{10,4},{11,5},{8,6},{9,7},{22,8},{23,9... | collective-permute-start | bytes 3080 | tf_op jit(solution)/shard_map/ppermute | solution.py:354
  21.4 0.4 %collective-permute-start.10 = (f32[2,128]{1,0:T(2,128)S(1)}, f32[2,128]{1,0:T(2,128)S(1)}, u32[]{:S(2)}, u32[]{:S(2)}) collective-permute-start(f32[2,128]{1,0:T(2,128)S(1)} %get-tuple-element.32), channel_id=1, source_target_pairs={{12,0},{13,1},{14,2},{15,3},{8,4},{9,5},{10,6},{11,7},{20,8},{21,9... | collective-permute-start | bytes 3080 | tf_op jit(solution)/shard_map/ppermute | solution.py:354
  21.8 2.1 %collective-permute-start.9 = (f32[2,128]{1,0:T(2,128)S(1)}, f32[2,128]{1,0:T(2,128)S(1)}, u32[]{:S(2)}, u32[]{:S(2)}) collective-permute-start(f32[2,128]{1,0:T(2,128)S(1)} %get-tuple-element.32), channel_id=1, source_target_pairs={{10,0},{11,1},{8,2},{9,3},{14,4},{15,5},{12,6},{13,7},{18,8},{19,9... | collective-permute-start | bytes 3080 | tf_op jit(solution)/shard_map/ppermute | solution.py:354
  24.0 1.3 %collective-permute-done.11.refs_2_ = f32[2,128]{1,0:T(2,128)S(1)} collective-permute-done((f32[2,128]{1,0:T(2,128)S(1)}, f32[2,128]{1,0:T(2,128)S(1)}, u32[]{:S(2)}, u32[]{:S(2)}) %collective-permute-start.11) | collective-permute-done | bytes 1056 | tf_op jit(solution)/shard_map/ppermute | solution.py:354
  25.3 1.0 %collective-permute-done.10.refs_1_ = f32[2,128]{1,0:T(2,128)S(1)} collective-permute-done((f32[2,128]{1,0:T(2,128)S(1)}, f32[2,128]{1,0:T(2,128)S(1)}, u32[]{:S(2)}, u32[]{:S(2)}) %collective-permute-start.10) | collective-permute-done | bytes 1056 | tf_op jit(solution)/shard_map/ppermute | solution.py:354
  26.2 0.0 collective-permute-done.9.refs_0_
  26.2 0.0 collective-permute-done.8.scaled_ref
  26.2 1.1 %shard_map.79 = bf16[128,1536]{1,0:T(8,128)(2,1)} custom-call(bf16[128,1664]{1,0:T(8,128)(2,1)S(1)} %collective-permute-done.8.scaled_ref, bf16[128,1536]{1,0:T(8,128)(2,1)S(1)} %collective-permute-done.7.input_ref, f32[2,128]{1,0:T(2,128)S(1)} %collective-permute-done.9.refs_0_, f32[2,128]{1,0:T(2,128)S(1)} %collective-permute-done.10.refs_1_, ...), custom_call_target="tpu_custom_call" | custom-call | tf_op jit(solution)/shard_map/pallas_call | solution.py:329
Async XLA Ops:
  0.0 5.5 %copy-start.1 = (bf16[1,128,1536]{2,1,0:T(8,128)(2,1)S(1)}, bf16[1,128,1536]{2,1,0:T(8,128)(2,1)}, u32[]{:S(2)}) copy-start(bf16[1,128,1536]{2,1,0:T(8,128)(2,1)} %param.12) | copy-start | bytes 1179652
  0.0 7.0 %copy-start = (bf16[1,1536,1024]{2,1,0:T(8,128)(2,1)S(1)}, bf16[1,1536,1024]{2,1,0:T(8,128)(2,1)}, u32[]{:S(2)}) copy-start(bf16[1,1536,1024]{2,1,0:T(8,128)(2,1)} %param.8) | copy-start | bytes 9437188
  0.0 7.0 %copy-start.2 = (f32[1,1536]{1,0:T(1,128)S(1)}, f32[1,1536]{1,0:T(1,128)}, u32[]{:S(2)}) copy-start(f32[1,1536]{1,0:T(1,128)} %refs_7_.1) | copy-start | bytes 18436
  1.0 6.6 %collective-permute-start.2 = (bf16[2,128,128]{2,1,0:T(8,128)(2,1)S(1)}, bf16[2,128,128]{2,1,0:T(8,128)(2,1)S(1)}, u32[]{:S(2)}, u32[]{:S(2)}) collective-permute-start(bf16[2,128,128]{2,1,0:T(8,128)(2,1)S(1)} %get-tuple-element.22.refs_3_), channel_id=1, source_target_pairs={{1,0},{0,1},{3,2},{2,3},{5,4},{4,5},{7,6},{6,7},{9,8},{8,9},{11,10... | collective-permute-start | bytes 196616 | tf_op jit(solution)/shard_map/ppermute | solution.py:25
  3.1 4.6 %collective-permute-start.1 = (bf16[128,128]{1,0:T(8,128)(2,1)S(1)}, bf16[128,128]{1,0:T(8,128)(2,1)S(1)}, u32[]{:S(2)}, u32[]{:S(2)}) collective-permute-start(bf16[128,128]{1,0:T(8,128)(2,1)S(1)} %get-tuple-element.20), channel_id=1, source_target_pairs={{17,0},{16,1},{19,2},{18,3},{21,4},{20,5},{23,6},{22,7},{25,8},{24... | collective-permute-start | bytes 98312 | tf_op jit(solution)/shard_map/ppermute | solution.py:364
  4.3 3.4 %collective-permute-start = (bf16[128,128]{1,0:T(8,128)(2,1)S(1)}, bf16[128,128]{1,0:T(8,128)(2,1)S(1)}, u32[]{:S(2)}, u32[]{:S(2)}) collective-permute-start(bf16[128,128]{1,0:T(8,128)(2,1)S(1)} %get-tuple-element.20), channel_id=1, source_target_pairs={{16,0},{17,1},{18,2},{19,3},{20,4},{21,5},{22,6},{23,7},{24,8},{25... | collective-permute-start | bytes 98312 | tf_op jit(solution)/shard_map/ppermute | solution.py:364
  5.5 10.8 %collective-permute-start.7 = (bf16[128,1536]{1,0:T(8,128)(2,1)S(1)}, bf16[128,1536]{1,0:T(8,128)(2,1)S(1)}, u32[]{:S(2)}, u32[]{:S(2)}) collective-permute-start(bf16[128,1536]{1,0:T(8,128)(2,1)S(1)} %bitcast.9), channel_id=1, source_target_pairs={{8,0},{16,8},{24,16},{0,24},{9,1},{17,9},{25,17},{1,25},{10,2},{18... | collective-permute-start | bytes 1179656 | tf_op jit(solution)/shard_map/ppermute | solution.py:21
  7.6 8.7 %collective-permute-start.6 = (bf16[144,1024]{1,0:T(8,128)(2,1)S(1)}, bf16[144,1024]{1,0:T(8,128)(2,1)S(1)}, u32[]{:S(2)}, u32[]{:S(2)}) collective-permute-start(bf16[144,1024]{1,0:T(8,128)(2,1)S(1)} %get-tuple-element.25), channel_id=1, source_target_pairs={{1,0},{0,1},{3,2},{2,3},{5,4},{4,5},{7,6},{6,7},{9,8},{8,9},{11,10... | collective-permute-start | bytes 884744 | tf_op jit(solution)/shard_map/ppermute | solution.py:25
  8.0 5.2 %collective-permute-start.5 = (bf16[2,128,128]{2,1,0:T(8,128)(2,1)S(1)}, bf16[2,128,128]{2,1,0:T(8,128)(2,1)S(1)}, u32[]{:S(2)}, u32[]{:S(2)}) collective-permute-start(bf16[2,128,128]{2,1,0:T(8,128)(2,1)S(1)} %shard_map.75.refs_0_), channel_id=1, source_target_pairs={{6,0},{7,1},{4,2},{5,3},{2,4},{3,5},{0,6},{1,7},{14,8},{15,9},{12,... | collective-permute-start | bytes 196616 | tf_op jit(solution)/shard_map/ppermute | solution.py:25
  11.5 5.3 %collective-permute-start.4 = (bf16[2,128,128]{2,1,0:T(8,128)(2,1)S(1)}, bf16[2,128,128]{2,1,0:T(8,128)(2,1)S(1)}, u32[]{:S(2)}, u32[]{:S(2)}) collective-permute-start(bf16[2,128,128]{2,1,0:T(8,128)(2,1)S(1)} %shard_map.75.refs_0_), channel_id=1, source_target_pairs={{4,0},{5,1},{6,2},{7,3},{0,4},{1,5},{2,6},{3,7},{12,8},{13,9},{14,... | collective-permute-start | bytes 196616 | tf_op jit(solution)/shard_map/ppermute | solution.py:25
  11.5 5.3 %collective-permute-start.3 = (bf16[2,128,128]{2,1,0:T(8,128)(2,1)S(1)}, bf16[2,128,128]{2,1,0:T(8,128)(2,1)S(1)}, u32[]{:S(2)}, u32[]{:S(2)}) collective-permute-start(bf16[2,128,128]{2,1,0:T(8,128)(2,1)S(1)} %shard_map.75.refs_0_), channel_id=1, source_target_pairs={{2,0},{3,1},{0,2},{1,3},{6,4},{7,5},{4,6},{5,7},{10,8},{11,9},{8,1... | collective-permute-start | bytes 196616 | tf_op jit(solution)/shard_map/ppermute | solution.py:25
  17.6 8.6 %collective-permute-start.8 = (bf16[128,1664]{1,0:T(8,128)(2,1)S(1)}, bf16[128,1664]{1,0:T(8,128)(2,1)S(1)}, u32[]{:S(2)}, u32[]{:S(2)}) collective-permute-start(bf16[128,1664]{1,0:T(8,128)(2,1)S(1)} %get-tuple-element.30), channel_id=1, source_target_pairs={{8,0},{16,8},{24,16},{0,24},{9,1},{17,9},{25,17},{1,25},{10,2},{18... | collective-permute-start | bytes 1277960 | tf_op jit(solution)/shard_map/ppermute | solution.py:21
  19.6 5.7 %collective-permute-start.11 = (f32[2,128]{1,0:T(2,128)S(1)}, f32[2,128]{1,0:T(2,128)S(1)}, u32[]{:S(2)}, u32[]{:S(2)}) collective-permute-start(f32[2,128]{1,0:T(2,128)S(1)} %get-tuple-element.32), channel_id=1, source_target_pairs={{14,0},{15,1},{12,2},{13,3},{10,4},{11,5},{8,6},{9,7},{22,8},{23,9... | collective-permute-start | bytes 3080 | tf_op jit(solution)/shard_map/ppermute | solution.py:354
  21.4 4.8 %collective-permute-start.10 = (f32[2,128]{1,0:T(2,128)S(1)}, f32[2,128]{1,0:T(2,128)S(1)}, u32[]{:S(2)}, u32[]{:S(2)}) collective-permute-start(f32[2,128]{1,0:T(2,128)S(1)} %get-tuple-element.32), channel_id=1, source_target_pairs={{12,0},{13,1},{14,2},{15,3},{8,4},{9,5},{10,6},{11,7},{20,8},{21,9... | collective-permute-start | bytes 3080 | tf_op jit(solution)/shard_map/ppermute | solution.py:354
  21.8 4.4 %collective-permute-start.9 = (f32[2,128]{1,0:T(2,128)S(1)}, f32[2,128]{1,0:T(2,128)S(1)}, u32[]{:S(2)}, u32[]{:S(2)}) collective-permute-start(f32[2,128]{1,0:T(2,128)S(1)} %get-tuple-element.32), channel_id=1, source_target_pairs={{10,0},{11,1},{8,2},{9,3},{14,4},{15,5},{12,6},{13,7},{18,8},{19,9... | collective-permute-start | bytes 3080 | tf_op jit(solution)/shard_map/ppermute | solution.py:354
